TPU v7x, 32 devices: a whole 2x2x4 slice. The times are simulated.
32 devices in a mesh: tm: 8 (over y, x, core), space: 4 (over z).
Axes of the slice: x: 2, y: 2, z: 4, core: 2. Of those that a mesh axis runs over, the one named last changes fastest.
Arguments:
- sep_block: float32 [8, 1536, 1536], P('tm', 'space'), may hold values from -1 to 10, as said below
- own_couple: bfloat16 [8, 1536, 1536], P('tm', 'space'), may hold values from -0.1875 to 0.1875
- prev_couple: bfloat16 [8, 1536, 1536], P('tm', 'space'), may hold values from -0.1875 to 0.1875
- inner_diag: float32 [8, 1536], P('tm'), may hold values from 0.5 to 4
Outputs:
- reduced_blocks: float32 [8, 1536, 1536], P('tm', 'space')
- left_links: bfloat16 [8, 1536, 1536], P('tm', 'space')
Inputs may be any that keep to these rules, and one draw needn't show every extreme that they name: sep_block is symmetric in its last two dimensions; its diagonal entries lie between 3.5 and 10.
All inputs are finite; a program needn't handle non-finite values.
Results may differ from a plain program's by a relative error of at most 0.0083.
Values may be sent and summed in bfloat16 or wider, within the bound.
No kernel may reach another device: no remote copies, remote signals or barrier semaphores. Data moves between devices by JAX's collectives and lax.ppermute only.
A program may use at most 64 MiB of HBM per device.

v0:
```python
import jax
import jax.numpy as jnp
from jax import lax
from jax.sharding import PartitionSpec as P


def passed_along(block, axis, distance):
    devices = range(lax.axis_size(axis))
    route = [(i - distance, i) for i in devices if i - distance in devices]
    return lax.ppermute(block, axis, route)


def scaled_by(matrix, factors):
    return (matrix.astype(jnp.float32) * factors.astype(jnp.float32)[None, :]).astype(jnp.bfloat16)


def outer_form(left_side, right_side):
    return jnp.einsum("ik,jk->ij", left_side, right_side, preferred_element_type=jnp.float32)


def reduce_level(schur, link, distance, partition, row_start):
    row_count = schur.shape[0]
    diag_block = lax.dynamic_slice_in_dim(schur, row_start, row_count, 1)
    scale_local = (1.0 / jnp.maximum(jnp.diagonal(diag_block), 1.0)).astype(jnp.bfloat16)
    scale_full = lax.all_gather(scale_local, "space", axis=0, tiled=True)
    own_full = lax.all_gather(link, "space", axis=0, tiled=True)
    next_full, next_scale = passed_along((own_full, scale_full), "tm", -distance)
    flipped = lax.dynamic_slice_in_dim(next_full, row_start, row_count, 1).T
    flipped_scaled = scaled_by(flipped, scale_full)
    right_form = jnp.dot(flipped_scaled, next_full, preferred_element_type=jnp.float32)
    own_scaled = scaled_by(link, scale_full)
    fill_link = (-jnp.dot(own_scaled, next_full, preferred_element_type=jnp.float32)).astype(
        jnp.bfloat16
    )
    right_recv, fill_recv = (
        passed_along(right_form.astype(jnp.bfloat16), "tm", distance).astype(right_form.dtype),
        passed_along(fill_link.astype(jnp.float32).astype(jnp.bfloat16), "tm", distance).astype(
            jnp.float32
        ),
    )
    next_local = lax.dynamic_slice_in_dim(next_full, row_start, row_count, 0)
    next_scaled = scaled_by(next_local, next_scale)
    left_form = outer_form(next_scaled, next_full)
    new_schur = schur - left_form - right_recv
    receiver = partition % (2 * distance) == 2 * distance - 1
    return (
        jnp.where(receiver, new_schur, schur),
        jnp.where(receiver, fill_recv.astype(jnp.bfloat16), link),
    )


def on_device(sep_block, own_couple, prev_couple, inner_diag):
    separator = sep_block[0]
    own_rows = own_couple[0]
    prev_rows = prev_couple[0]
    reciprocal = 1.0 / inner_diag[0]
    row_count = separator.shape[0]
    row_start = lax.axis_index("space") * row_count
    partition = lax.axis_index("tm")
    own_scaled = scaled_by(own_rows, reciprocal)
    prev_scaled = scaled_by(prev_rows, reciprocal)
    couple_pair = jnp.stack([own_rows, prev_rows])
    piece_rows = lax.all_gather(couple_pair, "space", axis=1, tiled=True)
    local_forms = jnp.stack(
        [
            outer_form(own_scaled, piece_rows[0]),
            outer_form(prev_scaled, piece_rows[1]),
            outer_form(prev_scaled, piece_rows[0]),
        ]
    )
    incoming = passed_along(local_forms[1], "tm", -1)
    schur = separator - local_forms[0] - incoming
    link = (-local_forms[2]).astype(jnp.bfloat16)
    link = jnp.where(partition == 0, jnp.zeros_like(link), link)
    for distance in (1, 2):
        schur, link = reduce_level(schur, link, distance, partition, row_start)
    return (schur[None], link[None])


def solution(mesh):
    placed = (P("tm", "space", None), P("tm", "space", None), P("tm", "space", None), P("tm", None))
    return jax.shard_map(
        on_device,
        mesh=mesh,
        in_specs=placed,
        out_specs=(P("tm", "space", None), P("tm", "space", None)),
        check_vma=False,
    )
```

profile of v0, /device:TPU:3, one launch (start us, length us, event | category | flops | bytes accessed | tf_op | source)
XLA Modules:
  0.0 691.4 jit_solution(3961774172100284619)
XLA Ops:
  7.2 0.0 all-gather.6.cloned.1.call-start
  7.2 3.2 pad_maximum_fusion
  10.5 0.0 copy-start.8
  10.5 0.0 copy-start.2
  10.5 0.0 all-gather.6.cloned.1.call-update
  10.5 0.0 all-gather.8.cloned.1.call-start
  10.5 0.6 copy-done.8
  11.2 167.7 %all-gather.6.cloned.1.call-done = bf16[2,1536,1536]{2,1,0:T(8,128)(2,1)} async-done(((bf16[2,384,1536]{2,1,0:T(8,128)(2,1)}), bf16[2,1536,1536]{2,1,0:T(8,128)(2,1)}) %all-gather.6.cloned.1.call-update) | async-done | bytes 9437200 | tf_op jit(solution)/shard_map/all_gather | solution.py:63
  178.9 0.0 copy-done.2
  178.9 5.4 fusion.14
  184.2 0.0 all-gather.8.cloned.1.call-update
  184.3 0.0 copy-start.3
  184.3 0.0 all-gather.10.cloned.1.call-start
  184.3 87.6 %all-gather.8.cloned.1.call-done = bf16[1536,1536]{1,0:T(8,128)(2,1)} async-done(((bf16[384,1536]{1,0:T(8,128)(2,1)}), bf16[1536,1536]{1,0:T(8,128)(2,1)}) %all-gather.8.cloned.1.call-update) | async-done | bytes 4718608 | tf_op jit(solution)/shard_map/all_gather | solution.py:26
  271.9 2.5 collective-permute-start.1
  274.4 5.8 fusion
  280.2 1.9 collective-permute-start
  282.2 71.6 %collective-permute-done = f32[384,1536]{1,0:T(8,128)} collective-permute-done((f32[384,1536]{1,0:T(8,128)}, f32[384,1536]{1,0:T(8,128)}, u32[]{:S(2)}, u32[]{:S(2)}) %collective-permute-start) | collective-permute-done | bytes 2359328 | tf_op jit(solution)/shard_map/ppermute | solution.py:10
  353.8 0.0 copy-done.3
  353.8 5.7 fusion.10
  359.6 0.0 copy-start.4
  359.6 1.4 copy-done.4
  361.0 0.0 copy-start.1
  361.0 0.1 constant_dynamic-slice_fusion.1
  361.0 3.4 gather_fusion
  364.5 9.3 %all-gather = bf16[4,1,384]{2,1,0:T(2,128)(2,1)S(1)} all-gather(bf16[1,1,384]{2,1,0:T(2,128)(2,1)S(1)} %reshape.41), channel_id=1, replica_groups=mesh['tm'=8,'space'=4] {'space'}, dimensions={0}, use_global_device_ids=true | all-gather | bytes 3840 | tf_op jit(solution)/shard_map/all_gather | solution.py:25
  373.9 0.0 collective-permute-done.1
  373.9 0.0 copy-done.1
  373.9 4.3 fusion.11
  378.2 4.3 collective-permute-start.4
  382.6 13.1 %collective-permute-done.4 = bf16[384,1536]{1,0:T(8,128)(2,1)S(1)} collective-permute-done((bf16[384,1536]{1,0:T(8,128)(2,1)S(1)}, bf16[384,1536]{1,0:T(8,128)(2,1)S(1)}, u32[]{:S(2)}, u32[]{:S(2)}) %collective-permute-start.4) | collective-permute-done | bytes 1179680 | tf_op jit(solution)/shard_map/ppermute | solution.py:10
  395.7 1.1 broadcast_select_fusion
  396.8 0.0 all-gather.10.cloned.1.call-update
  396.8 0.0 copy-start.5
  396.9 88.8 %all-gather.10.cloned.1.call-done = bf16[1536,1536]{1,0:T(8,128)(2,1)} async-done(((bf16[384,1536]{1,0:T(8,128)(2,1)}), bf16[1536,1536]{1,0:T(8,128)(2,1)}) %all-gather.10.cloned.1.call-update) | async-done | bytes 4718608 | tf_op jit(solution)/shard_map/all_gather | solution.py:26
  485.6 2.2 collective-permute-start.5
  487.8 4.8 convolution_convert_fusion.1
  492.7 4.8 collective-permute-start.3
  497.5 2.1 collective-permute-start.2
  499.6 94.1 %collective-permute-done.2 = bf16[1536]{0:T(1024)(128)(2,1)S(1)} collective-permute-done((bf16[1536]{0:T(1024)(128)(2,1)S(1)}, bf16[1536]{0:T(1024)(128)(2,1)S(1)}, u32[]{:S(2)}, u32[]{:S(2)}) %collective-permute-start.2) | collective-permute-done | bytes 3104 | tf_op jit(solution)/shard_map/ppermute | solution.py:10
  593.7 8.7 %collective-permute-done.3 = bf16[384,1536]{1,0:T(8,128)(2,1)S(1)} collective-permute-done((bf16[384,1536]{1,0:T(8,128)(2,1)S(1)}, bf16[384,1536]{1,0:T(8,128)(2,1)S(1)}, u32[]{:S(2)}, u32[]{:S(2)}) %collective-permute-start.3) | collective-permute-done | bytes 1179680 | tf_op jit(solution)/shard_map/ppermute | solution.py:10
  602.3 0.0 copy-done.5
  602.3 4.8 fusion.6
  607.1 0.0 copy-start.6
  607.1 1.4 copy-done.6
  608.5 0.0 copy-start
  608.5 0.1 constant_dynamic-slice_fusion
  608.6 3.4 gather_fusion.1
  612.1 9.3 %all-gather.1 = bf16[4,1,384]{2,1,0:T(2,128)(2,1)S(1)} all-gather(bf16[1,1,384]{2,1,0:T(2,128)(2,1)S(1)} %reshape.43), channel_id=1, replica_groups=mesh['tm'=8,'space'=4] {'space'}, dimensions={0}, use_global_device_ids=true | all-gather | bytes 3840 | tf_op jit(solution)/shard_map/all_gather | solution.py:25
  621.4 0.0 collective-permute-done.5
  621.4 0.0 copy-done
  621.4 5.4 fusion.12
  626.8 4.0 collective-permute-start.8
  630.8 5.9 convolution_convert_fusion
  636.6 1.9 collective-permute-start.7
  638.5 3.4 collective-permute-start.6
  642.0 0.0 copy-start.7
  642.0 35.6 %collective-permute-done.6 = bf16[1536]{0:T(1024)(128)(2,1)S(1)} collective-permute-done((bf16[1536]{0:T(1024)(128)(2,1)S(1)}, bf16[1536]{0:T(1024)(128)(2,1)S(1)}, u32[]{:S(2)}, u32[]{:S(2)}) %collective-permute-start.6) | collective-permute-done | bytes 3104 | tf_op jit(solution)/shard_map/ppermute | solution.py:10
  677.6 0.0 collective-permute-done.8
  677.6 1.1 select_bitcast_fusion
  678.7 0.0 collective-permute-done.7
  678.7 0.0 copy-done.7
  678.7 6.1 fusion.9
  (14 shorter events, 0.2 us)
Async XLA Ops:
  7.2 171.7 %all-gather.6.cloned.1.call-start = ((), (), s32[]{:S(2)}) async-start(), calls=%async_computation | async-start | bytes 11796480 | tf_op jit(solution)/shard_map/all_gather | solution.py:63
  10.5 0.7 copy-start.8
  10.5 168.4 %copy-start.2 = (bf16[1,384,1536]{2,1,0:T(8,128)(2,1)S(1)}, bf16[1,384,1536]{2,1,0:T(8,128)(2,1)}, u32[]{:S(2)}) copy-start(bf16[1,384,1536]{2,1,0:T(8,128)(2,1)} %param.6) | copy-start | bytes 3538948
  10.5 261.4 %all-gather.8.cloned.1.call-start = ((), (), s32[]{:S(2)}) async-start(), calls=%async_computation.1 | async-start | bytes 5898240 | tf_op jit(solution)/shard_map/all_gather | solution.py:26
  184.3 169.6 %copy-start.3 = (bf16[1,384,1536]{2,1,0:T(8,128)(2,1)S(1)}, bf16[1,384,1536]{2,1,0:T(8,128)(2,1)}, u32[]{:S(2)}) copy-start(bf16[1,384,1536]{2,1,0:T(8,128)(2,1)} %param.5) | copy-start | bytes 3538948
  184.3 301.4 %all-gather.10.cloned.1.call-start = ((), (), s32[]{:S(2)}) async-start(), calls=%async_computation.2 | async-start | bytes 5898240 | tf_op jit(solution)/shard_map/all_gather | solution.py:26
  271.9 102.0 %collective-permute-start.1 = (bf16[1536,1536]{1,0:T(8,128)(2,1)}, bf16[1536,1536]{1,0:T(8,128)(2,1)}, u32[]{:S(2)}, u32[]{:S(2)}) collective-permute-start(bf16[1536,1536]{1,0:T(8,128)(2,1)} %all-gather.8.cloned.1.call-done), channel_id=1, source_target_pairs={{4,0},{8,4},{12,8},{16,12},{20,16},{24,20},{28,24},{5,1},{9,5},{13... | collective-permute-start | bytes 14155784 | tf_op jit(solution)/shard_map/ppermute | solution.py:10
  280.2 73.6 %collective-permute-start = (f32[384,1536]{1,0:T(8,128)}, f32[384,1536]{1,0:T(8,128)}, u32[]{:S(2)}, u32[]{:S(2)}) collective-permute-start(f32[384,1536]{1,0:T(8,128)} %fusion), channel_id=1, source_target_pairs={{4,0},{8,4},{12,8},{16,12},{20,16},{24,20},{28,24},{5,1},{9,5},{13... | collective-permute-start | bytes 7077896 | tf_op jit(solution)/shard_map/ppermute | solution.py:10
  359.6 1.4 copy-start.4
  361.0 12.9 %copy-start.1 = (bf16[384,1536]{1,0:T(8,128)(2,1)S(1)}, bf16[384,1536]{1,0:T(8,128)(2,1)}, u32[]{:S(2)}) copy-start(bf16[384,1536]{1,0:T(8,128)(2,1)} %fusion.14) | copy-start | bytes 3538948
  378.2 17.5 %collective-permute-start.4 = (bf16[384,1536]{1,0:T(8,128)(2,1)S(1)}, bf16[384,1536]{1,0:T(8,128)(2,1)S(1)}, u32[]{:S(2)}, u32[]{:S(2)}) collective-permute-start(bf16[384,1536]{1,0:T(8,128)(2,1)S(1)} %fusion.11), channel_id=1, source_target_pairs={{0,4},{4,8},{8,12},{12,16},{16,20},{20,24},{24,28},{1,5},{5,9},{9,... | collective-permute-start | bytes 3538952 | tf_op jit(solution)/shard_map/ppermute | solution.py:10
  396.8 205.5 %copy-start.5 = (f32[384,1536]{1,0:T(8,128)S(1)}, f32[384,1536]{1,0:T(8,128)}, u32[]{:S(2)}) copy-start(f32[384,1536]{1,0:T(8,128)} %copy-done.4) | copy-start | bytes 7077892
  485.6 135.8 %collective-permute-start.5 = (bf16[1536,1536]{1,0:T(8,128)(2,1)}, bf16[1536,1536]{1,0:T(8,128)(2,1)}, u32[]{:S(2)}, u32[]{:S(2)}) collective-permute-start(bf16[1536,1536]{1,0:T(8,128)(2,1)} %all-gather.10.cloned.1.call-done), channel_id=1, source_target_pairs={{8,0},{12,4},{16,8},{20,12},{24,16},{28,20},{9,1},{13,5},{17,9},{2... | collective-permute-start | bytes 14155784 | tf_op jit(solution)/shard_map/ppermute | solution.py:10
  492.7 109.6 %collective-permute-start.3 = (bf16[384,1536]{1,0:T(8,128)(2,1)S(1)}, bf16[384,1536]{1,0:T(8,128)(2,1)S(1)}, u32[]{:S(2)}, u32[]{:S(2)}) collective-permute-start(bf16[384,1536]{1,0:T(8,128)(2,1)S(1)} %convolution_convert_fusion.1), channel_id=1, source_target_pairs={{0,4},{4,8},{8,12},{12,16},{16,20},{20,24},{24,28},{1,5},{5,9},{9,... | collective-permute-start | bytes 3538952 | tf_op jit(solution)/shard_map/ppermute | solution.py:10
  497.5 96.2 %collective-permute-start.2 = (bf16[1536]{0:T(1024)(128)(2,1)S(1)}, bf16[1536]{0:T(1024)(128)(2,1)S(1)}, u32[]{:S(2)}, u32[]{:S(2)}) collective-permute-start(bf16[1536]{0:T(1024)(128)(2,1)S(1)} %reshape.42), channel_id=1, source_target_pairs={{4,0},{8,4},{12,8},{16,12},{20,16},{24,20},{28,24},{5,1},{9,5},{13... | collective-permute-start | bytes 9224 | tf_op jit(solution)/shard_map/ppermute | solution.py:10
  607.1 1.4 copy-start.6
  608.5 12.9 %copy-start = (bf16[384,1536]{1,0:T(8,128)(2,1)S(1)}, bf16[384,1536]{1,0:T(8,128)(2,1)}, u32[]{:S(2)}) copy-start(bf16[384,1536]{1,0:T(8,128)(2,1)} %broadcast_select_fusion) | copy-start | bytes 3538948
  626.8 50.8 %collective-permute-start.8 = (bf16[384,1536]{1,0:T(8,128)(2,1)}, bf16[384,1536]{1,0:T(8,128)(2,1)S(1)}, u32[]{:S(2)}, u32[]{:S(2)}) collective-permute-start(bf16[384,1536]{1,0:T(8,128)(2,1)} %fusion.12), channel_id=1, source_target_pairs={{0,8},{4,12},{8,16},{12,20},{16,24},{20,28},{1,9},{5,13},{9,17},{1... | collective-permute-start | bytes 3538952 | tf_op jit(solution)/shard_map/ppermute | solution.py:10
  636.6 42.1 %collective-permute-start.7 = (bf16[384,1536]{1,0:T(8,128)(2,1)}, bf16[384,1536]{1,0:T(8,128)(2,1)S(1)}, u32[]{:S(2)}, u32[]{:S(2)}) collective-permute-start(bf16[384,1536]{1,0:T(8,128)(2,1)} %convolution_convert_fusion), channel_id=1, source_target_pairs={{0,8},{4,12},{8,16},{12,20},{16,24},{20,28},{1,9},{5,13},{9,17},{1... | collective-permute-start | bytes 3538952 | tf_op jit(solution)/shard_map/ppermute | solution.py:10
  638.5 39.1 %collective-permute-start.6 = (bf16[1536]{0:T(1024)(128)(2,1)S(1)}, bf16[1536]{0:T(1024)(128)(2,1)S(1)}, u32[]{:S(2)}, u32[]{:S(2)}) collective-permute-start(bf16[1536]{0:T(1024)(128)(2,1)S(1)} %reshape.44), channel_id=1, source_target_pairs={{8,0},{12,4},{16,8},{20,12},{24,16},{28,20},{9,1},{13,5},{17,9},{2... | collective-permute-start | bytes 9224 | tf_op jit(solution)/shard_map/ppermute | solution.py:10
  642.0 36.7 %copy-start.7 = (f32[384,1536]{1,0:T(8,128)S(1)}, f32[384,1536]{1,0:T(8,128)}, u32[]{:S(2)}) copy-start(f32[384,1536]{1,0:T(8,128)} %copy-done.6) | copy-start | bytes 7077892
Sparse Core Ops, SparseCore 0:
  10.6 168.2 all-gather.5
  184.4 87.4 all-gather.7
  397.0 88.6 all-gather.9
where the time goes:
time: 700 us; the launch traced here: 691 us
  waiting for transfers between devices  567 us (81%)
  matrix products  48.2 us (7%)
  starting transfers between devices  27.3 us (4%)
  blocking collectives  18.5 us (3%)
  between operations  14 us (2%)
  local copies, waits for them, and re-layouts  10.5 us (2%)
    ppermute x9, waiting for transfers between devices, passed_along(): return lax.ppermute(block, axis, route)  223 us
    all_gather x2, waiting for transfers between devices, reduce_level(): own_full = lax.all_gather(link, 'space', axis=0, tiled=True)  176 us
    all_gather x1, waiting for transfers between devices, on_device(): piece_rows = lax.all_gather(couple_pair, 'space', axis=1, tiled=True)  168 us
    dot_general x5, matrix products, outer_form(): jnp.einsum('ik,jk->ij', left_side, right_side, preferred_element_type=jnp...  27.8 us
    ppermute x9, starting transfers between devices, passed_along(): return lax.ppermute(block, axis, route)  27.2 us
    all_gather x2, blocking collectives, reduce_level(): scale_full = lax.all_gather(scale_local, 'space', axis=0, tiled=True)  18.5 us
  transfers between devices with their start and end apart: 12, of which 8 were waited for; matrix products, arithmetic and copies ran while one was open for 5% of the time, Pallas kernels for 0%

commit v1 on v0

v1 whole, which is shorter than its diff:
```python
import jax
import jax.numpy as jnp
from jax import lax
from jax.sharding import PartitionSpec as P

BF16 = jnp.bfloat16
F32 = jnp.float32


def scaled_by(matrix, factors):
    return (matrix.astype(F32) * factors.astype(F32)[None, :]).astype(BF16)


def row_scaled_by(matrix, factors):
    return (matrix.astype(F32) * factors.astype(F32)[:, None]).astype(BF16)


def dot_nt(left, right):
    return lax.dot_general(left, right, (((1,), (1,)), ((), ())), preferred_element_type=F32)


def dot_nn(left, right):
    return lax.dot_general(left, right, (((1,), (0,)), ((), ())), preferred_element_type=F32)


def dot_tn(left, right):
    return lax.dot_general(left, right, (((0,), (0,)), ((), ())), preferred_element_type=F32)


def line_gather(blocks, axis):
    size = lax.axis_size(axis)
    place = lax.axis_index(axis)
    ahead, back = list(blocks), list(blocks)
    from_before, from_after = {}, {}
    for step in range(1, size):
        up = [(j, j + 1) for j in range(step - 1, size - 1)]
        down = [(j, j - 1) for j in range(1, size - step + 1)]
        for which in range(len(blocks)):
            ahead[which] = lax.ppermute(ahead[which], axis, up)
            back[which] = lax.ppermute(back[which], axis, down)
        from_before[step] = list(ahead)
        from_after[step] = list(back)
    gathered = []
    for which, block in enumerate(blocks):
        rows = block.shape[0]
        whole = jnp.zeros((size * rows,) + block.shape[1:], block.dtype)
        whole = lax.dynamic_update_slice_in_dim(whole, block, place * rows, 0)
        for step in range(1, size):
            piece = jnp.where(
                place >= step, from_before[step][which], from_after[size - step][which]
            )
            at = (place + size - step) % size
            whole = lax.dynamic_update_slice_in_dim(whole, piece, at * rows, 0)
        gathered.append(whole)
    return gathered


def on_device(sep_block, own_couple, prev_couple, inner_diag):
    separator = sep_block[0]
    own_rows = own_couple[0]
    prev_rows = prev_couple[0]
    reciprocal = 1.0 / inner_diag[0]
    rows, order = own_rows.shape
    row_start = lax.axis_index("space") * rows
    partition = lax.axis_index("tm")
    parts = lax.axis_size("tm")

    def level_route(distance, sign):
        pivots = range(distance - 1, parts, 2 * distance)
        route = [(p, p + sign * distance) for p in pivots]
        return [(a, b) for a, b in route if 0 <= b < parts]

    own_full, prev_full = line_gather([own_rows, prev_rows], "space")

    own_scaled = scaled_by(own_rows, reciprocal)
    prev_scaled = scaled_by(prev_rows, reciprocal)
    own_diag = jnp.sum(own_scaled.astype(F32) * own_rows.astype(F32), axis=1)
    prev_diag = jnp.sum(prev_scaled.astype(F32) * prev_rows.astype(F32), axis=1)
    row_ids = lax.broadcasted_iota(jnp.int32, separator.shape, 0) + row_start
    col_ids = lax.broadcasted_iota(jnp.int32, separator.shape, 1)
    sep_diag = jnp.sum(jnp.where(row_ids == col_ids, separator, 0.0), axis=1)
    earlier = [(p, p - 1) for p in range(1, parts)]
    diag_rows = sep_diag - own_diag - lax.ppermute(prev_diag, "tm", earlier)
    (diag,) = line_gather([diag_rows], "space")

    link = (-dot_nt(scaled_by(prev_full, reciprocal), own_full)).astype(BF16)
    link = jnp.where(partition == 0, jnp.zeros_like(link), link)
    link_rows = lax.dynamic_slice_in_dim(link, row_start, rows, 0)

    own_form = dot_nt(own_scaled, own_full)
    prev_form = dot_nt(prev_scaled, prev_full)

    scale = (1.0 / jnp.maximum(diag, 1.0)).astype(BF16)
    pivot_link, pivot_scale = lax.ppermute((link, scale), "tm", level_route(1, 1))
    next_link = (-dot_nn(scaled_by(pivot_link, pivot_scale), link)).astype(BF16)
    left_form = dot_nt(scaled_by(link_rows, scale), link)
    left_diag = jnp.sum(scaled_by(link, scale).astype(F32) * link.astype(F32), axis=1)
    link_cols = lax.dynamic_slice_in_dim(link, row_start, rows, 1)
    right_form = dot_tn(row_scaled_by(link_cols, pivot_scale), link)
    right_diag = jnp.sum(row_scaled_by(link, pivot_scale).astype(F32) * link.astype(F32), axis=0)
    is_pivot = partition % 2 == 0
    is_receiver = partition % 2 == 1
    to_earlier = jnp.where(is_pivot, prev_form + left_form, prev_form).astype(BF16)
    from_later = lax.ppermute(to_earlier, "tm", earlier)
    schur = separator - own_form - from_later.astype(F32)
    schur = jnp.where(is_receiver, schur - right_form, schur)
    diag = diag - lax.ppermute(left_diag, "tm", level_route(1, -1)) - right_diag
    next_rows = lax.dynamic_slice_in_dim(next_link, row_start, rows, 0)
    out_link = jnp.where(is_receiver, next_rows, link_rows)

    scale = (1.0 / jnp.maximum(diag, 1.0)).astype(BF16)
    pivot_rows, pivot_scale = lax.ppermute((next_rows, scale), "tm", level_route(2, 1))
    left_form = dot_nt(scaled_by(next_rows, scale), next_link).astype(BF16)
    from_later = lax.ppermute(left_form, "tm", level_route(2, -1))
    next_cols = lax.dynamic_slice_in_dim(next_link, row_start, rows, 1)
    right_form = dot_tn(row_scaled_by(next_cols, pivot_scale), next_link)
    last_rows = (-dot_nn(scaled_by(pivot_rows, pivot_scale), next_link)).astype(BF16)
    is_receiver = partition % 4 == 3
    schur = jnp.where(is_receiver, schur - from_later.astype(F32) - right_form, schur)
    out_link = jnp.where(is_receiver, last_rows, out_link)
    return (schur[None], out_link[None])


def solution(mesh):
    placed = (P("tm", "space", None), P("tm", "space", None), P("tm", "space", None), P("tm", None))
    return jax.shard_map(
        on_device,
        mesh=mesh,
        in_specs=placed,
        out_specs=(P("tm", "space", None), P("tm", "space", None)),
        check_vma=False,
    )
```

time: 700 us -> 287 us (0.41)
  the two profiles are of different devices: /device:TPU:3 before, /device:TPU:19 now
where the time goes in v1:
time: 287 us; the launch traced here: 286 us
  waiting for transfers between devices  149 us (52%)
  matrix products  53.9 us (19%)
  starting transfers between devices  52.9 us (18%)
  other arithmetic  21.3 us (7%)
  local copies, waits for them, and re-layouts  7.43 us (3%)
    ppermute x9, waiting for transfers between devices, line_gather(): ahead[which] = lax.ppermute(ahead[which], axis, up)  90.2 us
    ppermute x9, waiting for transfers between devices, line_gather(): back[which] = lax.ppermute(back[which], axis, down)  38.5 us
    dot_general x5, matrix products, dot_nt(): lax.dot_general(left, right, (((1,), (1,)), ((), ())), preferred_element_...  31.8 us
    ppermute x9, starting transfers between devices, line_gather(): back[which] = lax.ppermute(back[which], axis, down)  18.3 us
    ppermute x1, waiting for transfers between devices, on_device(): from_later = lax.ppermute(to_earlier, 'tm', earlier)  17.4 us
    ppermute x9, starting transfers between devices, line_gather(): ahead[which] = lax.ppermute(ahead[which], axis, up)  17.2 us
    dot_general x2, matrix products, dot_nn(): lax.dot_general(left, right, (((1,), (0,)), ((), ())), preferred_element_...  15.2 us
    dynamic_update_slice x9, other arithmetic, line_gather(): whole = lax.dynamic_update_slice_in_dim(whole, piece, at * rows, 0)  14.6 us
  transfers between devices with their start and end apart: 26, of which 10 were waited for; matrix products, arithmetic and copies ran while one was open for 21% of the time, Pallas kernels for 0%

profile of v1, /device:TPU:19, one launch (start us, length us, event | category | flops | bytes accessed | tf_op | source)
XLA Modules:
  0.0 285.6 jit_solution(14492773771545378084)
XLA Ops:
  0.6 2.2 collective-permute-start.1
  2.9 2.1 collective-permute-start.7
  4.9 3.5 %collective-permute-start.6 = (bf16[384,1536]{1,0:T(8,128)(2,1)}, bf16[384,1536]{1,0:T(8,128)(2,1)}, u32[]{:S(2)}, u32[]{:S(2)}) collective-permute-start(bf16[384,1536]{1,0:T(8,128)(2,1)} %bitcast.35), channel_id=1, source_target_pairs={{0,1},{1,2},{2,3},{4,5},{5,6},{6,7},{8,9},{9,10},{10,11},{12,13},{... | collective-permute-start | bytes 3538952 | tf_op jit(solution)/shard_map/ppermute | solution.py:39
  8.5 1.9 collective-permute-start
  10.4 0.7 divide_reduce_fusion
  11.1 2.9 %fusion.12 = (f32[384]{0:T(512)}, f32[384]{0:T(512)S(1)}) fusion(f32[1536]{0:T(1024)S(1)} %divide_reduce_fusion, bf16[1,384,1536]{2,1,0:T(8,128)(2,1)} %param.5, bf16[1,384,1536]{2,1,0:T(8,128)(2,1)} %param.6), kind=kLoop, calls=%fused_computation.29 | loop fusion | flops 7077120 | bytes 2368512 | tf_op jit(solution)/shard_map/reduce_sum | solution.py:77
  14.0 3.2 %collective-permute-start.12 = (f32[384]{0:T(512)S(1)}, f32[384]{0:T(512)}, u32[]{:S(2)}, u32[]{:S(2)}) collective-permute-start(f32[384]{0:T(512)S(1)} %get-tuple-element.5), channel_id=1, source_target_pairs={{4,0},{8,4},{12,8},{16,12},{20,16},{24,20},{28,24},{5,1},{9,5},{13... | collective-permute-start | bytes 4616 | tf_op jit(solution)/shard_map/ppermute | solution.py:83
  17.2 12.6 %collective-permute-done.1 = bf16[384,1536]{1,0:T(8,128)(2,1)} collective-permute-done((bf16[384,1536]{1,0:T(8,128)(2,1)}, bf16[384,1536]{1,0:T(8,128)(2,1)}, u32[]{:S(2)}, u32[]{:S(2)}) %collective-permute-start.1) | collective-permute-done | bytes 1179680 | tf_op jit(solution)/shard_map/ppermute | solution.py:40
  29.8 3.1 %collective-permute-start.2 = (bf16[384,1536]{1,0:T(8,128)(2,1)}, bf16[384,1536]{1,0:T(8,128)(2,1)}, u32[]{:S(2)}, u32[]{:S(2)}) collective-permute-start(bf16[384,1536]{1,0:T(8,128)(2,1)} %collective-permute-done.1), channel_id=1, source_target_pairs={{1,0},{2,1},{5,4},{6,5},{9,8},{10,9},{13,12},{14,13},{17,16},{18,1... | collective-permute-start | bytes 3538952 | tf_op jit(solution)/shard_map/ppermute | solution.py:40
  32.9 1.0 fusion.16
  33.9 0.8 fusion.40
  34.7 2.0 collective-permute-start.13
  36.8 22.0 %collective-permute-done.13 = f32[384]{0:T(512)S(1)} collective-permute-done((f32[384]{0:T(512)S(1)}, f32[384]{0:T(512)S(1)}, u32[]{:S(2)}, u32[]{:S(2)}) %collective-permute-start.13) | collective-permute-done | bytes 1568 | tf_op jit(solution)/shard_map/ppermute | solution.py:39
  58.7 2.2 collective-permute-start.14
  60.9 17.4 %collective-permute-done.14 = f32[384]{0:T(512)S(1)} collective-permute-done((f32[384]{0:T(512)S(1)}, f32[384]{0:T(512)S(1)}, u32[]{:S(2)}, u32[]{:S(2)}) %collective-permute-start.14) | collective-permute-done | bytes 1568 | tf_op jit(solution)/shard_map/ppermute | solution.py:40
  78.4 1.9 collective-permute-start.17
  80.3 2.6 collective-permute-done.17
  82.8 1.7 collective-permute-start.15
  84.5 3.0 %collective-permute-start.8 = (bf16[384,1536]{1,0:T(8,128)(2,1)S(1)}, bf16[384,1536]{1,0:T(8,128)(2,1)}, u32[]{:S(2)}, u32[]{:S(2)}) collective-permute-start(bf16[384,1536]{1,0:T(8,128)(2,1)S(1)} %collective-permute-done.7), channel_id=1, source_target_pairs={{1,0},{2,1},{5,4},{6,5},{9,8},{10,9},{13,12},{14,13},{17,16},{18,1... | collective-permute-start | bytes 3538952 | tf_op jit(solution)/shard_map/ppermute | solution.py:40
  87.5 2.5 broadcast.23.clone
  90.0 1.1 constant_dynamic-update-slice_fusion.1
  91.1 0.7 collective-permute-start.16
  91.8 1.3 collective-permute-start.18
  93.1 0.1 select_dynamic-update-slice_fusion.8
  93.2 1.9 collective-permute-start.10
  95.2 1.9 collective-permute-start.4
  97.1 1.7 collective-permute-start.3
  98.8 0.1 select_dynamic-update-slice_fusion.7
  98.9 0.1 select_dynamic-update-slice_fusion.6
  99.0 0.6 fusion.39
  99.6 1.4 collective-permute-start.20
  101.0 8.4 %collective-permute-done.8 = bf16[384,1536]{1,0:T(8,128)(2,1)} collective-permute-done((bf16[384,1536]{1,0:T(8,128)(2,1)S(1)}, bf16[384,1536]{1,0:T(8,128)(2,1)}, u32[]{:S(2)}, u32[]{:S(2)}) %collective-permute-start.8) | collective-permute-done | bytes 1179680 | tf_op jit(solution)/shard_map/ppermute | solution.py:40
  109.5 1.7 collective-permute-start.9
  111.2 2.5 broadcast.23.clone.1
  113.7 1.1 constant_dynamic-update-slice_fusion
  114.8 0.7 convert_element_type.139
  115.5 20.0 %collective-permute-done.10 = bf16[384,1536]{1,0:T(8,128)(2,1)} collective-permute-done((bf16[384,1536]{1,0:T(8,128)(2,1)}, bf16[384,1536]{1,0:T(8,128)(2,1)}, u32[]{:S(2)}, u32[]{:S(2)}) %collective-permute-start.10) | collective-permute-done | bytes 1179680 | tf_op jit(solution)/shard_map/ppermute | solution.py:39
  135.6 1.4 collective-permute-start.11
  136.9 23.9 %collective-permute-done.4 = bf16[384,1536]{1,0:T(8,128)(2,1)} collective-permute-done((bf16[384,1536]{1,0:T(8,128)(2,1)}, bf16[384,1536]{1,0:T(8,128)(2,1)}, u32[]{:S(2)}, u32[]{:S(2)}) %collective-permute-start.4) | collective-permute-done | bytes 1179680 | tf_op jit(solution)/shard_map/ppermute | solution.py:39
  160.8 1.4 collective-permute-start.5
  162.2 2.6 select_dynamic-update-slice_fusion.5
  164.8 2.6 select_dynamic-update-slice_fusion.4
  167.4 2.6 select_dynamic-update-slice_fusion.2
  170.0 2.6 select_dynamic-update-slice_fusion.1
  172.6 21.8 %collective-permute-done.5 = bf16[384,1536]{1,0:T(8,128)(2,1)S(1)} collective-permute-done((bf16[384,1536]{1,0:T(8,128)(2,1)}, bf16[384,1536]{1,0:T(8,128)(2,1)S(1)}, u32[]{:S(2)}, u32[]{:S(2)}) %collective-permute-start.5) | collective-permute-done | bytes 1179680 | tf_op jit(solution)/shard_map/ppermute | solution.py:39
  194.3 2.7 select_dynamic-update-slice_fusion.3
  197.0 1.3 select_dynamic-update-slice_fusion
  198.3 14.4 %fusion.1 = (f32[1536]{0:T(1024)S(1)}, f32[1536]{0:T(1024)S(1)}, bf16[1536,1536]{1,0:T(8,128)(2,1)}) fusion(f32[1536]{0:T(1024)S(1)} %copy-done.6, f32[1536]{0:T(1024)S(1)} %convert_element_type.139, bf16[1536,1536]{1,0:T(8,128)(2,1)} %select_dynamic-update-slice_fusion.3, bf16[1536,1536]{1,0:T(8,128)(2,1)} %select_dynamic-update-slice_fusion, ...), kind=kOutput, calls=%fused_computation.5 | convolution fusion | flops 7287862272 | bytes 14186497 | tf_op jit(solution)/shard_map/dot_general | solution.py:19
  212.7 1.3 collective-permute-start.21
  214.0 1.5 collective-permute-start.22
  215.5 4.7 %fusion.17 = f32[384,1536]{1,0:T(8,128)S(1)} fusion(bf16[1536,1536]{1,0:T(8,128)(2,1)} %get-tuple-element.12, f32[1536]{0:T(1024)S(1)} %copy-done.7, s32[]{:T(128)S(6)} %select_n.157), kind=kOutput, calls=%fused_computation.42 | convolution fusion | flops 1813708800 | bytes 8263684 | tf_op jit(solution)/shard_map/dot_general | solution.py:19
  220.2 4.4 %fusion.15 = bf16[384,1536]{1,0:T(8,128)(2,1)S(1)} fusion(f32[384,1536]{1,0:T(8,128)S(1)} %fusion.17, bf16[1536,1536]{1,0:T(8,128)(2,1)} %select_dynamic-update-slice_fusion, f32[1536]{0:T(1024)S(1)} %divide_reduce_fusion, pred[]{:T(512)S(6)} %eq.30, bf16[1,384,1536]{2,1,0:T(8,128)(2,1)S(1)} %copy-done), kind=kOutput, calls=%fused_computation.32 | convolution fusion | flops 1815478272 | bytes 9443329 | tf_op jit(solution)/shard_map/dot_general | solution.py:19
  224.6 1.3 collective-permute-start.24
  226.0 10.7 %negate_convert_fusion = bf16[1536,1536]{1,0:T(8,128)(2,1)S(1)} fusion(bf16[1536,1536]{1,0:T(8,128)(2,1)} %get-tuple-element.12, bf16[1536,1536]{1,0:T(8,128)(2,1)} %collective-permute-done.21, f32[1536]{0:T(1024)S(1)} %copy-done.5), kind=kOutput, calls=%fused_computation.8 | convolution fusion | flops 7259553792 | bytes 14161920 | tf_op jit(solution)/shard_map/dot_general | solution.py:23
  236.8 1.3 collective-permute-start.25
  238.1 4.8 %fusion.18 = f32[384,1536]{1,0:T(8,128)S(1)} fusion(bf16[1536,1536]{1,0:T(8,128)(2,1)} %get-tuple-element.12, f32[1536]{0:T(1024)S(1)} %copy-done.5, s32[]{:T(128)S(6)} %select_n.157), kind=kOutput, calls=%fused_computation.43 | convolution fusion | flops 1813708800 | bytes 8263684 | tf_op jit(solution)/shard_map/dot_general | solution.py:27
  242.9 6.0 %collective-permute-start.19 = (bf16[384,1536]{1,0:T(8,128)(2,1)S(1)}, bf16[384,1536]{1,0:T(8,128)(2,1)S(1)}, u32[]{:S(2)}, u32[]{:S(2)}) collective-permute-start(bf16[384,1536]{1,0:T(8,128)(2,1)S(1)} %fusion.15), channel_id=1, source_target_pairs={{4,0},{8,4},{12,8},{16,12},{20,16},{24,20},{28,24},{5,1},{9,5},{13... | collective-permute-start | bytes 3538952 | tf_op jit(solution)/shard_map/ppermute | solution.py:104
  248.9 2.0 convolution_convert_fusion
  251.0 1.5 collective-permute-start.23
  252.5 2.1 fusion.19
  254.6 4.5 %fusion.10 = bf16[1,384,1536]{2,1,0:T(8,128)(2,1)} fusion(bf16[1536,1536]{1,0:T(8,128)(2,1)S(1)} %negate_convert_fusion, bf16[384,1536]{1,0:T(8,128)(2,1)S(1)} %collective-permute-done.25, bf16[384,1536]{1,0:T(8,128)(2,1)S(1)} %constant_dynamic-slice_fusion, f32[1536]{0:T(1024)S(1)} %convert_element_type.156, pred[]{:T(512)S(6)} %eq.29, pred[]{:T(512)S(6)} %eq.28, ...), kind=kOutput, calls=%fused_computation.27 | convolution fusion | flops 1816068096 | bytes 9443334 | tf_op jit(solution)/shard_map/dot_general | solution.py:23
  259.1 17.4 %collective-permute-done.19 = bf16[384,1536]{1,0:T(8,128)(2,1)S(1)} collective-permute-done((bf16[384,1536]{1,0:T(8,128)(2,1)S(1)}, bf16[384,1536]{1,0:T(8,128)(2,1)S(1)}, u32[]{:S(2)}, u32[]{:S(2)}) %collective-permute-start.19) | collective-permute-done | bytes 1179680 | tf_op jit(solution)/shard_map/ppermute | solution.py:104
  276.6 2.8 collective-permute-done.23
  279.3 6.2 %select_bitcast_fusion = f32[1,384,1536]{2,1,0:T(8,128)} fusion(f32[384,1536]{1,0:T(8,128)S(1)} %fusion.19, f32[384,1536]{1,0:T(8,128)S(1)} %fusion.18, bf16[1536,1536]{1,0:T(8,128)(2,1)} %select_dynamic-update-slice_fusion.3, f32[1,384,1536]{2,1,0:T(8,128)S(1)} %copy-done.3, bf16[384,1536]{1,0:T(8,128)(2,1)S(1)} %collective-permute-done.23, ...), kind=kOutput, calls=%fused_computation.36 | convolution fusion | flops 1819017216 | bytes 17700866 | tf_op jit(solution)/shard_map/dot_general | solution.py:19
  (37 shorter events, 0.2 us)
Async XLA Ops:
  0.6 32.3 %copy-start.2 = (f32[1,384,1536]{2,1,0:T(8,128)S(1)}, f32[1,384,1536]{2,1,0:T(8,128)}, u32[]{:S(2)}) copy-start(f32[1,384,1536]{2,1,0:T(8,128)} %param.4) | copy-start | bytes 7077892
  0.6 29.2 %collective-permute-start.1 = (bf16[384,1536]{1,0:T(8,128)(2,1)}, bf16[384,1536]{1,0:T(8,128)(2,1)}, u32[]{:S(2)}, u32[]{:S(2)}) collective-permute-start(bf16[384,1536]{1,0:T(8,128)(2,1)} %bitcast.36), channel_id=1, source_target_pairs={{1,0},{2,1},{3,2},{5,4},{6,5},{7,6},{9,8},{10,9},{11,10},{13,12},{... | collective-permute-start | bytes 3538952 | tf_op jit(solution)/shard_map/ppermute | solution.py:40
  2.9 81.6 %collective-permute-start.7 = (bf16[384,1536]{1,0:T(8,128)(2,1)}, bf16[384,1536]{1,0:T(8,128)(2,1)S(1)}, u32[]{:S(2)}, u32[]{:S(2)}) collective-permute-start(bf16[384,1536]{1,0:T(8,128)(2,1)} %bitcast.34), channel_id=1, source_target_pairs={{1,0},{2,1},{3,2},{5,4},{6,5},{7,6},{9,8},{10,9},{11,10},{13,12},{... | collective-permute-start | bytes 3538952 | tf_op jit(solution)/shard_map/ppermute | solution.py:40
  4.9 88.3 %collective-permute-start.6 = (bf16[384,1536]{1,0:T(8,128)(2,1)}, bf16[384,1536]{1,0:T(8,128)(2,1)}, u32[]{:S(2)}, u32[]{:S(2)}) collective-permute-start(bf16[384,1536]{1,0:T(8,128)(2,1)} %bitcast.35), channel_id=1, source_target_pairs={{0,1},{1,2},{2,3},{4,5},{5,6},{6,7},{8,9},{9,10},{10,11},{12,13},{... | collective-permute-start | bytes 3538952 | tf_op jit(solution)/shard_map/ppermute | solution.py:39
  8.5 86.7 %collective-permute-start = (bf16[384,1536]{1,0:T(8,128)(2,1)}, bf16[384,1536]{1,0:T(8,128)(2,1)}, u32[]{:S(2)}, u32[]{:S(2)}) collective-permute-start(bf16[384,1536]{1,0:T(8,128)(2,1)} %bitcast.37), channel_id=1, source_target_pairs={{0,1},{1,2},{2,3},{4,5},{5,6},{6,7},{8,9},{9,10},{10,11},{12,13},{... | collective-permute-start | bytes 3538952 | tf_op jit(solution)/shard_map/ppermute | solution.py:39
  14.0 19.9 %collective-permute-start.12 = (f32[384]{0:T(512)S(1)}, f32[384]{0:T(512)}, u32[]{:S(2)}, u32[]{:S(2)}) collective-permute-start(f32[384]{0:T(512)S(1)} %get-tuple-element.5), channel_id=1, source_target_pairs={{4,0},{8,4},{12,8},{16,12},{20,16},{24,20},{28,24},{5,1},{9,5},{13... | collective-permute-start | bytes 4616 | tf_op jit(solution)/shard_map/ppermute | solution.py:83
  29.8 67.3 %collective-permute-start.2 = (bf16[384,1536]{1,0:T(8,128)(2,1)}, bf16[384,1536]{1,0:T(8,128)(2,1)}, u32[]{:S(2)}, u32[]{:S(2)}) collective-permute-start(bf16[384,1536]{1,0:T(8,128)(2,1)} %collective-permute-done.1), channel_id=1, source_target_pairs={{1,0},{2,1},{5,4},{6,5},{9,8},{10,9},{13,12},{14,13},{17,16},{18,1... | collective-permute-start | bytes 3538952 | tf_op jit(solution)/shard_map/ppermute | solution.py:40
  34.7 55.3 %copy-start.1 = (bf16[1,384,1536]{2,1,0:T(8,128)(2,1)S(1)}, bf16[1,384,1536]{2,1,0:T(8,128)(2,1)}, u32[]{:S(2)}) copy-start(bf16[1,384,1536]{2,1,0:T(8,128)(2,1)} %param.5) | copy-start | bytes 3538948
  34.7 24.0 %collective-permute-start.13 = (f32[384]{0:T(512)S(1)}, f32[384]{0:T(512)S(1)}, u32[]{:S(2)}, u32[]{:S(2)}) collective-permute-start(f32[384]{0:T(512)S(1)} %get-tuple-element.11), channel_id=1, source_target_pairs={{0,1},{1,2},{2,3},{4,5},{5,6},{6,7},{8,9},{9,10},{10,11},{12,13},{... | collective-permute-start | bytes 4616 | tf_op jit(solution)/shard_map/ppermute | solution.py:39
  58.7 19.6 %collective-permute-start.14 = (f32[384]{0:T(512)S(1)}, f32[384]{0:T(512)S(1)}, u32[]{:S(2)}, u32[]{:S(2)}) collective-permute-start(f32[384]{0:T(512)S(1)} %get-tuple-element.11), channel_id=1, source_target_pairs={{1,0},{2,1},{3,2},{5,4},{6,5},{7,6},{9,8},{10,9},{11,10},{13,12},{... | collective-permute-start | bytes 4616 | tf_op jit(solution)/shard_map/ppermute | solution.py:40
  78.4 4.5 %collective-permute-start.17 = (f32[384]{0:T(512)S(1)}, f32[384]{0:T(512)S(1)}, u32[]{:S(2)}, u32[]{:S(2)}) collective-permute-start(f32[384]{0:T(512)S(1)} %collective-permute-done.13), channel_id=1, source_target_pairs={{1,2},{2,3},{5,6},{6,7},{9,10},{10,11},{13,14},{14,15},{17,18},{18... | collective-permute-start | bytes 4616 | tf_op jit(solution)/shard_map/ppermute | solution.py:39
  82.8 8.3 %collective-permute-start.15 = (f32[384]{0:T(512)S(1)}, f32[384]{0:T(512)S(1)}, u32[]{:S(2)}, u32[]{:S(2)}) collective-permute-start(f32[384]{0:T(512)S(1)} %collective-permute-done.14), channel_id=1, source_target_pairs={{1,0},{2,1},{5,4},{6,5},{9,8},{10,9},{13,12},{14,13},{17,16},{18,1... | collective-permute-start | bytes 4616 | tf_op jit(solution)/shard_map/ppermute | solution.py:40
  84.5 25.0 %collective-permute-start.8 = (bf16[384,1536]{1,0:T(8,128)(2,1)S(1)}, bf16[384,1536]{1,0:T(8,128)(2,1)}, u32[]{:S(2)}, u32[]{:S(2)}) collective-permute-start(bf16[384,1536]{1,0:T(8,128)(2,1)S(1)} %collective-permute-done.7), channel_id=1, source_target_pairs={{1,0},{2,1},{5,4},{6,5},{9,8},{10,9},{13,12},{14,13},{17,16},{18,1... | collective-permute-start | bytes 3538952 | tf_op jit(solution)/shard_map/ppermute | solution.py:40
  91.1 0.7 collective-permute-start.16
  91.8 7.1 %collective-permute-start.18 = (f32[384]{0:T(512)S(1)}, f32[384]{0:T(512)S(1)}, u32[]{:S(2)}, u32[]{:S(2)}) collective-permute-start(f32[384]{0:T(512)S(1)} %collective-permute-done.17), channel_id=1, source_target_pairs={{2,3},{6,7},{10,11},{14,15},{18,19},{22,23},{26,27},{30,31}} | collective-permute-start | bytes 4616 | tf_op jit(solution)/shard_map/ppermute | solution.py:39
  93.2 42.3 %collective-permute-start.10 = (bf16[384,1536]{1,0:T(8,128)(2,1)}, bf16[384,1536]{1,0:T(8,128)(2,1)}, u32[]{:S(2)}, u32[]{:S(2)}) collective-permute-start(bf16[384,1536]{1,0:T(8,128)(2,1)} %collective-permute-done.6), channel_id=1, source_target_pairs={{1,2},{2,3},{5,6},{6,7},{9,10},{10,11},{13,14},{14,15},{17,18},{18... | collective-permute-start | bytes 3538952 | tf_op jit(solution)/shard_map/ppermute | solution.py:39
  95.2 65.7 %collective-permute-start.4 = (bf16[384,1536]{1,0:T(8,128)(2,1)}, bf16[384,1536]{1,0:T(8,128)(2,1)}, u32[]{:S(2)}, u32[]{:S(2)}) collective-permute-start(bf16[384,1536]{1,0:T(8,128)(2,1)} %collective-permute-done), channel_id=1, source_target_pairs={{1,2},{2,3},{5,6},{6,7},{9,10},{10,11},{13,14},{14,15},{17,18},{18... | collective-permute-start | bytes 3538952 | tf_op jit(solution)/shard_map/ppermute | solution.py:39
  97.1 65.1 %collective-permute-start.3 = (bf16[384,1536]{1,0:T(8,128)(2,1)}, bf16[384,1536]{1,0:T(8,128)(2,1)}, u32[]{:S(2)}, u32[]{:S(2)}) collective-permute-start(bf16[384,1536]{1,0:T(8,128)(2,1)} %collective-permute-done.2), channel_id=1, source_target_pairs={{1,0},{5,4},{9,8},{13,12},{17,16},{21,20},{25,24},{29,28}} | collective-permute-start | bytes 3538952 | tf_op jit(solution)/shard_map/ppermute | solution.py:40
  99.6 14.1 %copy-start = (bf16[1,384,1536]{2,1,0:T(8,128)(2,1)S(1)}, bf16[1,384,1536]{2,1,0:T(8,128)(2,1)}, u32[]{:S(2)}) copy-start(bf16[1,384,1536]{2,1,0:T(8,128)(2,1)} %param.6) | copy-start | bytes 3538948
  99.6 15.2 %collective-permute-start.20 = (bf16[1536]{0:T(1024)(128)(2,1)}, bf16[1536]{0:T(1024)(128)(2,1)}, u32[]{:S(2)}, u32[]{:S(2)}) collective-permute-start(bf16[1536]{0:T(1024)(128)(2,1)} %get-tuple-element.9), channel_id=1, source_target_pairs={{0,4},{8,12},{16,20},{24,28},{1,5},{9,13},{17,21},{25,29},{2,6},{1... | collective-permute-start | bytes 9224 | tf_op jit(solution)/shard_map/ppermute | solution.py:94
  109.5 57.9 %collective-permute-start.9 = (bf16[384,1536]{1,0:T(8,128)(2,1)}, bf16[384,1536]{1,0:T(8,128)(2,1)}, u32[]{:S(2)}, u32[]{:S(2)}) collective-permute-start(bf16[384,1536]{1,0:T(8,128)(2,1)} %collective-permute-done.8), channel_id=1, source_target_pairs={{1,0},{5,4},{9,8},{13,12},{17,16},{21,20},{25,24},{29,28}} | collective-permute-start | bytes 3538952 | tf_op jit(solution)/shard_map/ppermute | solution.py:40
  115.5 82.8 %copy-start.4 = (f32[1536]{0:T(1024)}, f32[1536]{0:T(1024)S(1)}, u32[]{:S(2)}) copy-start(f32[1536]{0:T(1024)S(1)} %convert_element_type.139) | copy-start | bytes 18436
  135.6 61.4 %collective-permute-start.11 = (bf16[384,1536]{1,0:T(8,128)(2,1)}, bf16[384,1536]{1,0:T(8,128)(2,1)S(1)}, u32[]{:S(2)}, u32[]{:S(2)}) collective-permute-start(bf16[384,1536]{1,0:T(8,128)(2,1)} %collective-permute-done.10), channel_id=1, source_target_pairs={{2,3},{6,7},{10,11},{14,15},{18,19},{22,23},{26,27},{30,31}} | collective-permute-start | bytes 3538952 | tf_op jit(solution)/shard_map/ppermute | solution.py:39
  160.8 33.5 %collective-permute-start.5 = (bf16[384,1536]{1,0:T(8,128)(2,1)}, bf16[384,1536]{1,0:T(8,128)(2,1)S(1)}, u32[]{:S(2)}, u32[]{:S(2)}) collective-permute-start(bf16[384,1536]{1,0:T(8,128)(2,1)} %collective-permute-done.4), channel_id=1, source_target_pairs={{2,3},{6,7},{10,11},{14,15},{18,19},{22,23},{26,27},{30,31}} | collective-permute-start | bytes 3538952 | tf_op jit(solution)/shard_map/ppermute | solution.py:39
  197.0 1.3 copy-start.6
  198.3 17.2 %copy-start.7 = (f32[1536]{0:T(1024)S(1)}, f32[1536]{0:T(1024)}, u32[]{:S(2)}) copy-start(f32[1536]{0:T(1024)} %get-tuple-element.8) | copy-start | bytes 18436
  212.7 13.3 %collective-permute-start.21 = (bf16[1536,1536]{1,0:T(8,128)(2,1)}, bf16[1536,1536]{1,0:T(8,128)(2,1)}, u32[]{:S(2)}, u32[]{:S(2)}) collective-permute-start(bf16[1536,1536]{1,0:T(8,128)(2,1)} %get-tuple-element.12), channel_id=1, source_target_pairs={{0,4},{8,12},{16,20},{24,28},{1,5},{9,13},{17,21},{25,29},{2,6},{1... | collective-permute-start | bytes 14155784 | tf_op jit(solution)/shard_map/ppermute | solution.py:94
  214.0 10.6 %collective-permute-start.22 = (f32[1536]{0:T(1024)S(1)}, f32[1536]{0:T(1024)S(1)}, u32[]{:S(2)}, u32[]{:S(2)}) collective-permute-start(f32[1536]{0:T(1024)S(1)} %get-tuple-element.2), channel_id=1, source_target_pairs={{8,4},{16,12},{24,20},{9,5},{17,13},{25,21},{10,6},{18,14},{26,22}... | collective-permute-start | bytes 18440 | tf_op jit(solution)/shard_map/ppermute | solution.py:107
  220.2 5.7 %copy-start.5 = (f32[1536]{0:T(1024)S(1)}, f32[1536]{0:T(1024)}, u32[]{:S(2)}) copy-start(f32[1536]{0:T(1024)} %copy-done.4) | copy-start | bytes 18436
  224.6 24.3 %collective-permute-start.24 = (bf16[1536]{0:T(1024)(128)(2,1)S(1)}, bf16[1536]{0:T(1024)(128)(2,1)S(1)}, u32[]{:S(2)}, u32[]{:S(2)}) collective-permute-start(bf16[1536]{0:T(1024)(128)(2,1)S(1)} %get-tuple-element.7), channel_id=1, source_target_pairs={{4,12},{20,28},{5,13},{21,29},{6,14},{22,30},{7,15},{23,31}} | collective-permute-start | bytes 9224 | tf_op jit(solution)/shard_map/ppermute | solution.py:112
  236.8 17.9 %collective-permute-start.25 = (bf16[384,1536]{1,0:T(8,128)(2,1)S(1)}, bf16[384,1536]{1,0:T(8,128)(2,1)S(1)}, u32[]{:S(2)}, u32[]{:S(2)}) collective-permute-start(bf16[384,1536]{1,0:T(8,128)(2,1)S(1)} %constant_dynamic-slice_fusion), channel_id=1, source_target_pairs={{4,12},{20,28},{5,13},{21,29},{6,14},{22,30},{7,15},{23,31}} | collective-permute-start | bytes 3538952 | tf_op jit(solution)/shard_map/ppermute | solution.py:112
  242.9 33.7 %collective-permute-start.19 = (bf16[384,1536]{1,0:T(8,128)(2,1)S(1)}, bf16[384,1536]{1,0:T(8,128)(2,1)S(1)}, u32[]{:S(2)}, u32[]{:S(2)}) collective-permute-start(bf16[384,1536]{1,0:T(8,128)(2,1)S(1)} %fusion.15), channel_id=1, source_target_pairs={{4,0},{8,4},{12,8},{16,12},{20,16},{24,20},{28,24},{5,1},{9,5},{13... | collective-permute-start | bytes 3538952 | tf_op jit(solution)/shard_map/ppermute | solution.py:104
  251.0 28.4 %collective-permute-start.23 = (bf16[384,1536]{1,0:T(8,128)(2,1)S(1)}, bf16[384,1536]{1,0:T(8,128)(2,1)S(1)}, u32[]{:S(2)}, u32[]{:S(2)}) collective-permute-start(bf16[384,1536]{1,0:T(8,128)(2,1)S(1)} %convolution_convert_fusion), channel_id=1, source_target_pairs={{20,12},{21,13},{22,14},{23,15}} | collective-permute-start | bytes 3538952 | tf_op jit(solution)/shard_map/ppermute | solution.py:114
  254.6 24.7 %copy-start.3 = (f32[1,384,1536]{2,1,0:T(8,128)S(1)}, f32[1,384,1536]{2,1,0:T(8,128)}, u32[]{:S(2)}) copy-start(f32[1,384,1536]{2,1,0:T(8,128)} %param.4) | copy-start | bytes 7077892

commit v2 on v1

v2 whole, which is shorter than its diff:
```python
import jax
import jax.numpy as jnp
from jax import lax
from jax.sharding import PartitionSpec as P

BF16 = jnp.bfloat16
F32 = jnp.float32
EXTRA = 16


def scaled_by(matrix, factors):
    return (matrix.astype(F32) * factors.astype(F32)[None, :]).astype(BF16)


def row_scaled_by(matrix, factors):
    return (matrix.astype(F32) * factors.astype(F32)[:, None]).astype(BF16)


def dot_nt(left, right):
    return lax.dot_general(left, right, (((1,), (1,)), ((), ())), preferred_element_type=F32)


def dot_nn(left, right):
    return lax.dot_general(left, right, (((1,), (0,)), ((), ())), preferred_element_type=F32)


def dot_tn(left, right):
    return lax.dot_general(left, right, (((0,), (0,)), ((), ())), preferred_element_type=F32)


def rows_of(scale):
    return jnp.broadcast_to(scale[None, :], (8, scale.shape[0]))


def on_device(sep_block, own_couple, prev_couple, inner_diag):
    separator = sep_block[0]
    own_rows = own_couple[0]
    prev_rows = prev_couple[0]
    reciprocal = 1.0 / inner_diag[0]
    rows, order = own_rows.shape
    place = lax.axis_index("space")
    size = lax.axis_size("space")
    row_start = place * rows
    partition = lax.axis_index("tm")
    parts = lax.axis_size("tm")

    def between(block, route):
        return lax.ppermute(block, "tm", [(a, b) for a, b in route if 0 <= b < parts])

    even = range(0, parts, 2)
    pivots = range(1, parts, 4)
    everyone = range(parts)

    def one_step(ahead, back, step):
        up = [(j, j + 1) for j in range(step - 1, size - 1)]
        down = [(j, j - 1) for j in range(1, size - step + 1)]
        return lax.ppermute(ahead, "space", up), lax.ppermute(back, "space", down)

    def block_at(arrived, spot):
        block = arrived[0][0]
        for step in range(1, size):
            if spot + step < size:
                block = jnp.where(place == spot + step, arrived[step][0], block)
            if spot - step >= 0:
                block = jnp.where(place == spot - step, arrived[step][1], block)
        return block

    own_arrived = [(own_rows, own_rows)]
    own_arrived.append(one_step(own_rows, own_rows, 1))

    own_scaled = scaled_by(own_rows, reciprocal)
    prev_scaled = scaled_by(prev_rows, reciprocal)
    own_sum = jnp.sum(own_scaled.astype(F32) * own_rows.astype(F32), axis=1)
    prev_sum = jnp.sum(prev_scaled.astype(F32) * prev_rows.astype(F32), axis=1)
    row_ids = lax.broadcasted_iota(jnp.int32, separator.shape, 0) + row_start
    col_ids = lax.broadcasted_iota(jnp.int32, separator.shape, 1)
    sep_diag = jnp.sum(jnp.where(row_ids == col_ids, separator, 0.0), axis=1)
    diag_rows = sep_diag - own_sum - between(prev_sum, [(p, p - 1) for p in everyone])
    high = lax.reduce_precision(diag_rows, 8, 7)
    words = jnp.stack([high, diag_rows - high]).astype(BF16)
    prev_long = jnp.concatenate([prev_rows, jnp.pad(words, ((0, EXTRA - 2), (0, order - rows)))])
    prev_arrived = [(prev_long, prev_long)]
    prev_arrived.append(one_step(prev_long, prev_long, 1))
    for step in range(2, size):
        own_arrived.append(one_step(*own_arrived[-1], step))
        prev_arrived.append(one_step(*prev_arrived[-1], step))

    own_full = jnp.concatenate([block_at(own_arrived, spot) for spot in range(size)])

    left_side = place < size // 2
    late = jnp.where(left_side, size - 1, 0)
    late_start = late * rows
    before = [list(pair) for pair in prev_arrived[:-1]]
    before.append([jnp.zeros_like(prev_long)] * 2)
    prev_blocks = [block_at(before, spot) for spot in range(size)]
    prev_first = jnp.concatenate([block[:rows] for block in prev_blocks])
    prev_late = jnp.where(left_side, block_at(prev_arrived, size - 1), block_at(prev_arrived, 0))

    def diag_of(block):
        return block[rows, :rows].astype(F32) + block[rows + 1, :rows].astype(F32)

    diag = jnp.concatenate([diag_of(block) for block in prev_blocks])
    diag = lax.dynamic_update_slice_in_dim(diag, diag_of(prev_late), late_start, 0)
    prev_late = prev_late[:rows]

    is_first = partition == 0
    own_form = dot_nt(own_scaled, own_full)
    prev_form = dot_nt(prev_scaled, prev_first)
    link = (-dot_nt(scaled_by(prev_first, reciprocal), own_full)).astype(BF16)
    link = jnp.where(is_first, jnp.zeros_like(link), link)
    pivot_link = between(link, [(p, p + 1) for p in even])

    link_late = (-dot_nt(scaled_by(prev_late, reciprocal), own_full)).astype(BF16)
    link_late = jnp.where(is_first, jnp.zeros_like(link_late), link_late)
    pivot_late = between(link_late, [(p, p + 1) for p in even])
    link = lax.dynamic_update_slice_in_dim(link, link_late, late_start, 0)
    pivot_link = lax.dynamic_update_slice_in_dim(pivot_link, pivot_late, late_start, 0)
    prev_form = lax.dynamic_update_slice_in_dim(
        prev_form, dot_nt(prev_scaled, prev_late), late_start, 1
    )

    is_pivot = partition % 2 == 0
    is_receiver = partition % 2 == 1
    scale = (1.0 / jnp.maximum(diag, 1.0)).astype(BF16)
    pivot_scale = between(scale, [(p, p + 1) for p in even])
    left_diag = between(dot_nt(rows_of(scale), link * link)[0], [(p, p - 1) for p in even])
    next_link = (-dot_nn(scaled_by(pivot_link, pivot_scale), link)).astype(BF16)
    next_rows = lax.dynamic_slice_in_dim(next_link, row_start, rows, 0)
    pivot_rows = between(next_rows, [(p, p + 2) for p in pivots if p != 1])

    right_diag = dot_nn(rows_of(pivot_scale), link * link)[0]
    next_diag = diag - left_diag - right_diag
    next_scale = (1.0 / jnp.maximum(next_diag, 1.0)).astype(BF16)
    next_pivot_scale = between(next_scale, [(p, p + 2) for p in pivots])
    left_next = dot_nt(scaled_by(next_rows, next_scale), next_link).astype(BF16)
    from_pivot = between(left_next, [(p, p - 2) for p in pivots])

    link_rows = lax.dynamic_slice_in_dim(link, row_start, rows, 0)
    left_form = dot_nt(scaled_by(link_rows, scale), link)
    to_earlier = jnp.where(is_pivot, prev_form + left_form, prev_form).astype(BF16)
    from_later = between(to_earlier, [(p, p - 1) for p in everyone])
    link_cols = lax.dynamic_slice_in_dim(link, row_start, rows, 1)
    right_form = dot_tn(row_scaled_by(link_cols, pivot_scale), link)
    schur = separator - own_form - from_later.astype(F32)
    schur = jnp.where(is_receiver, schur - right_form, schur)

    is_last = partition % 4 == 3
    next_cols = lax.dynamic_slice_in_dim(next_link, row_start, rows, 1)
    right_next = dot_tn(row_scaled_by(next_cols, next_pivot_scale), next_link)
    last_rows = (-dot_nn(scaled_by(pivot_rows, next_pivot_scale), next_link)).astype(BF16)
    schur = jnp.where(is_last, schur - from_pivot.astype(F32) - right_next, schur)
    out_link = jnp.where(is_last, last_rows, jnp.where(is_receiver, next_rows, link_rows))
    return (schur[None], out_link[None])


def solution(mesh):
    placed = (P("tm", "space", None), P("tm", "space", None), P("tm", "space", None), P("tm", None))
    return jax.shard_map(
        on_device,
        mesh=mesh,
        in_specs=placed,
        out_specs=(P("tm", "space", None), P("tm", "space", None)),
        check_vma=False,
    )
```

time: 287 us -> 283 us (0.986)
  the two profiles are of different devices: /device:TPU:19 before, /device:TPU:3 now
where the time goes in v2:
time: 283 us; the launch traced here: 282 us
  waiting for transfers between devices  146 us (52%)
  matrix products  69.9 us (25%)
  starting transfers between devices  39.8 us (14%)
  other arithmetic  17.4 us (6%)
  local copies, waits for them, and re-layouts  7.86 us (3%)
    ppermute x12, waiting for transfers between devices, one_step(): return (lax.ppermute(ahead, 'space', up), lax.ppermute(back, 'space', down))  124 us
    dot_general x8, matrix products, dot_nt(): lax.dot_general(left, right, (((1,), (1,)), ((), ())), preferred_element_...  44.7 us
    ppermute x12, starting transfers between devices, one_step(): return (lax.ppermute(ahead, 'space', up), lax.ppermute(back, 'space', down))  22.6 us
    ppermute x9, waiting for transfers between devices, between(): lax.ppermute(block, 'tm', [(a, b) for a, b in route if 0 <= b < parts])  22.3 us
    dot_general x3, matrix products, dot_nn(): lax.dot_general(left, right, (((1,), (0,)), ((), ())), preferred_element_...  18.3 us
    ppermute x9, starting transfers between devices, between(): lax.ppermute(block, 'tm', [(a, b) for a, b in route if 0 <= b < parts])  17.2 us
    dot_general x2, matrix products, dot_tn(): lax.dot_general(left, right, (((0,), (0,)), ((), ())), preferred_element_...  6.93 us
  transfers between devices with their start and end apart: 21, of which 10 were waited for; matrix products, arithmetic and copies ran while one was open for 19% of the time, Pallas kernels for 0%

profile of v2, /device:TPU:3, one launch (start us, length us, event | category | flops | bytes accessed | tf_op | source)
XLA Modules:
  0.0 282.5 jit_solution(12627209268942459766)
XLA Ops:
  0.6 3.3 %collective-permute-start = (bf16[384,1536]{1,0:T(8,128)(2,1)}, bf16[384,1536]{1,0:T(8,128)(2,1)S(1)}, u32[]{:S(2)}, u32[]{:S(2)}) collective-permute-start(bf16[384,1536]{1,0:T(8,128)(2,1)} %bitcast.41), channel_id=1, source_target_pairs={{0,1},{1,2},{2,3},{4,5},{5,6},{6,7},{8,9},{9,10},{10,11},{12,13},{... | collective-permute-start | bytes 3538952 | tf_op jit(solution)/shard_map/ppermute | solution.py:57
  3.9 1.3 collective-permute-start.3
  5.2 0.7 divide_reduce_fusion
  5.9 2.4 fusion.15
  8.4 2.9 %collective-permute-start.6 = (f32[384]{0:T(512)S(1)}, f32[384]{0:T(512)}, u32[]{:S(2)}, u32[]{:S(2)}) collective-permute-start(f32[384]{0:T(512)S(1)} %get-tuple-element.3), channel_id=1, source_target_pairs={{4,0},{8,4},{12,8},{16,12},{20,16},{24,20},{28,24},{5,1},{9,5},{13... | collective-permute-start | bytes 4616 | tf_op jit(solution)/shard_map/ppermute | solution.py:48
  11.3 2.1 fusion.18
  13.4 0.9 collective-permute-done.6
  14.3 0.7 reduce-precision_convert_fusion
  15.1 1.3 collective-permute-start.9
  16.4 4.7 %collective-permute-start.7 = (bf16[400,1536]{1,0:T(8,128)(2,1)S(1)}, bf16[400,1536]{1,0:T(8,128)(2,1)S(1)}, u32[]{:S(2)}, u32[]{:S(2)}) collective-permute-start(bf16[400,1536]{1,0:T(8,128)(2,1)S(1)} %pad_maximum_fusion.2), channel_id=1, source_target_pairs={{0,1},{1,2},{2,3},{4,5},{5,6},{6,7},{8,9},{9,10},{10,11},{12,13},{... | collective-permute-start | bytes 3686408 | tf_op jit(solution)/shard_map/ppermute | solution.py:57
  21.1 7.7 %collective-permute-done = bf16[384,1536]{1,0:T(8,128)(2,1)S(1)} collective-permute-done((bf16[384,1536]{1,0:T(8,128)(2,1)}, bf16[384,1536]{1,0:T(8,128)(2,1)S(1)}, u32[]{:S(2)}, u32[]{:S(2)}) %collective-permute-start) | collective-permute-done | bytes 1179680 | tf_op jit(solution)/shard_map/ppermute | solution.py:57
  28.8 1.8 collective-permute-start.1
  30.5 2.1 collective-permute-done.3
  32.6 1.3 collective-permute-start.4
  33.9 24.9 %collective-permute-done.9 = bf16[400,1536]{1,0:T(8,128)(2,1)S(1)} collective-permute-done((bf16[400,1536]{1,0:T(8,128)(2,1)S(1)}, bf16[400,1536]{1,0:T(8,128)(2,1)S(1)}, u32[]{:S(2)}, u32[]{:S(2)}) %collective-permute-start.9) | collective-permute-done | bytes 1228832 | tf_op jit(solution)/shard_map/ppermute | solution.py:57
  58.9 1.0 copy-done.8
  59.9 1.3 collective-permute-start.10
  61.2 1.7 collective-permute-start.8
  63.0 1.7 collective-permute-start.2
  64.7 19.6 %collective-permute-done.4 = bf16[384,1536]{1,0:T(8,128)(2,1)} collective-permute-done((bf16[384,1536]{1,0:T(8,128)(2,1)}, bf16[384,1536]{1,0:T(8,128)(2,1)}, u32[]{:S(2)}, u32[]{:S(2)}) %collective-permute-start.4) | collective-permute-done | bytes 1179680 | tf_op jit(solution)/shard_map/ppermute | solution.py:57
  84.3 1.3 collective-permute-start.5
  85.5 25.0 %collective-permute-done.10 = bf16[400,1536]{1,0:T(8,128)(2,1)} collective-permute-done((bf16[400,1536]{1,0:T(8,128)(2,1)S(1)}, bf16[400,1536]{1,0:T(8,128)(2,1)}, u32[]{:S(2)}, u32[]{:S(2)}) %collective-permute-start.10) | collective-permute-done | bytes 1228832 | tf_op jit(solution)/shard_map/ppermute | solution.py:57
  110.6 1.3 collective-permute-start.11
  111.9 1.7 collective-permute-start.12
  113.6 22.2 %collective-permute-done.5 = bf16[384,1536]{1,0:T(8,128)(2,1)} collective-permute-done((bf16[384,1536]{1,0:T(8,128)(2,1)}, bf16[384,1536]{1,0:T(8,128)(2,1)}, u32[]{:S(2)}, u32[]{:S(2)}) %collective-permute-start.5) | collective-permute-done | bytes 1179680 | tf_op jit(solution)/shard_map/ppermute | solution.py:57
  135.9 3.9 %select_select_fusion.8 = (bf16[384,1536]{1,0:T(8,128)(2,1)}, bf16[384,1536]{1,0:T(8,128)(2,1)}, bf16[384,1536]{1,0:T(8,128)(2,1)}, bf16[384,1536]{1,0:T(8,128)(2,1)}) fusion(bf16[384,1536]{1,0:T(8,128)(2,1)} %collective-permute-done.2, bf16[384,1536]{1,0:T(8,128)(2,1)} %collective-permute-done.1, bf16[384,1536]{1,0:T(8,128)(2,1)S(1)} %collective-permute-done, ...), kind=kLoop, calls=%fused_computation.65 | loop fusion | flops 7077888 | bytes 12976132 | tf_op jit(solution)/shard_map/jit(_where)/select_n | solution.py:63
  139.7 22.5 %collective-permute-done.11 = bf16[400,1536]{1,0:T(8,128)(2,1)} collective-permute-done((bf16[400,1536]{1,0:T(8,128)(2,1)}, bf16[400,1536]{1,0:T(8,128)(2,1)}, u32[]{:S(2)}, u32[]{:S(2)}) %collective-permute-start.11) | collective-permute-done | bytes 1228832 | tf_op jit(solution)/shard_map/ppermute | solution.py:57
  162.2 4.1 %select_select_fusion = (bf16[400,1536]{1,0:T(8,128)(2,1)}, bf16[400,1536]{1,0:T(8,128)(2,1)S(1)}, bf16[400,1536]{1,0:T(8,128)(2,1)S(1)}, bf16[400,1536]{1,0:T(8,128)(2,1)S(1)}, bf16[400,1536]{1,0:T(8,128)(2,1)S(1)}) fusion(bf16[400,1536]{1,0:T(8,128)(2,1)} %collective-permute-done.12, bf16[400,1536]{1,0:T(8,128)(2,1)} %collective-permute-done.11, ...), kind=kLoop, calls=%fused_computation.46 | loop fusion | flops 10444800 | bytes 14745605 | tf_op jit(solution)/shard_map/jit(_where)/select_n | solution.py:97
  166.7 1.3 slice.72
  168.1 0.4 copy-done.3
  168.6 1.1 slice.73
  169.7 1.1 slice.74
  170.8 13.2 %fusion = bf16[1536,1536]{1,0:T(8,128)(2,1)} fusion(f32[1536]{0:T(1024)S(1)} %divide_reduce_fusion, pred[]{:T(512)S(6)} %eq.29, bf16[384,1536]{1,0:T(8,128)(2,1)S(1)} %slice.75, bf16[384,1536]{1,0:T(8,128)(2,1)} %slice.74, bf16[384,1536]{1,0:T(8,128)(2,1)} %slice.73, bf16[384,1536]{1,0:T(8,128)(2,1)} %slice.72, bf16[384,1536]{1,0:T(8,128)(2,1)} %get-tuple-element.16, ...), kind=kOutput, calls=%fused_computation.4 | convolution fusion | flops 7297302528 | bytes 14161921 | tf_op jit(solution)/shard_map/dot_general | solution.py:20
  183.9 1.3 collective-permute-start.15
  185.3 0.8 fusion.55
  186.0 0.8 fusion.61
  186.8 0.8 fusion.59
  187.6 0.8 fusion.53
  188.4 0.3 dynamic_update_slice.14
  188.7 1.6 collective-permute-start.14
  190.3 6.2 %fusion.31 = f32[384,1536]{1,0:T(8,128)S(1)} fusion(f32[1536]{0:T(1024)S(1)} %divide_reduce_fusion, bf16[384,1536]{1,0:T(8,128)(2,1)} %copy-done.12, bf16[384,1536]{1,0:T(8,128)(2,1)} %slice.74, bf16[384,1536]{1,0:T(8,128)(2,1)} %slice.73, bf16[384,1536]{1,0:T(8,128)(2,1)} %slice.72, bf16[1,384,1536]{2,1,0:T(8,128)(2,1)S(1)} %copy-done), kind=kOutput, calls=%fused_computation.67 | convolution fusion | flops 1832583168 | bytes 8263680 | tf_op jit(solution)/shard_map/dot_general | solution.py:20
  196.6 0.8 convolution_dynamic-update-slice_fusion
  197.4 0.4 copy-done.13
  197.8 0.4 copy-done.14
  198.2 0.4 copy-done.15
  198.5 6.7 %constant_dynamic-update-slice_fusion.1 = (bf16[1536,1536]{1,0:T(8,128)(2,1)}, bf16[384,1536]{1,0:T(8,128)(2,1)S(1)}) fusion(bf16[1536,1536]{1,0:T(8,128)(2,1)} %fusion, s32[]{:T(128)S(6)} %select_n.256, bf16[384,1536]{1,0:T(8,128)(2,1)S(1)} %copy-done.16, bf16[384,1536]{1,0:T(8,128)(2,1)S(1)} %copy-done.15, bf16[384,1536]{1,0:T(8,128)(2,1)S(1)} %copy-done.14, ...), kind=kOutput, calls=%fused_computation.95 | convolution fusion | flops 1834352640 | bytes 8265733 | tf_op jit(solution)/shard_map/dot_general | solution.py:20
  205.3 3.7 %fusion.33 = f32[1536]{0:T(1024)S(1)} fusion(bf16[1,1536]{1,0:T(2,128)(2,1)S(1)} %reshape.35, bf16[1536,1536]{1,0:T(8,128)(2,1)} %get-tuple-element.19), kind=kOutput, calls=%fused_computation.68 | convolution fusion | flops 7077888 | bytes 4727808 | tf_op jit(solution)/shard_map/dot_general | solution.py:20
  208.9 1.3 collective-permute-start.17
  210.2 1.3 collective-permute-start.16
  211.5 4.8 %fusion.10 = bf16[384,1536]{1,0:T(8,128)(2,1)S(1)} fusion(f32[384,1536]{1,0:T(8,128)S(1)} %convolution_dynamic-update-slice_fusion, bf16[1536,1536]{1,0:T(8,128)(2,1)} %get-tuple-element.19, f32[1536]{0:T(1024)S(1)} %get-tuple-element.4, pred[]{:T(512)S(6)} %eq.27, s32[]{:T(128)S(6)} %select_n.261), kind=kOutput, calls=%fused_computation.26 | convolution fusion | flops 1815478272 | bytes 9443333 | tf_op jit(solution)/shard_map/dot_general | solution.py:20
  216.3 3.1 %fusion.36 = f32[1536]{0:T(1024)S(1)} fusion(bf16[1,1536]{1,0:T(2,128)(2,1)S(1)} %reshape.36, bf16[1536,1536]{1,0:T(8,128)(2,1)} %get-tuple-element.19), kind=kOutput, calls=%fused_computation.69 | convolution fusion | flops 7077888 | bytes 4727808 | tf_op jit(solution)/shard_map/dot_general | solution.py:24
  219.4 1.3 collective-permute-start.19
  220.7 1.1 constant_dynamic-update-slice_fusion
  221.8 10.7 %negate_convert_fusion = bf16[1536,1536]{1,0:T(8,128)(2,1)S(1)} fusion(bf16[1536,1536]{1,0:T(8,128)(2,1)} %get-tuple-element.19, bf16[1536,1536]{1,0:T(8,128)(2,1)} %constant_dynamic-update-slice_fusion, f32[1536]{0:T(1024)S(1)} %convert_element_type.184), kind=kOutput, calls=%fused_computation | convolution fusion | flops 7259553792 | bytes 14161920 | tf_op jit(solution)/shard_map/dot_general | solution.py:24
  232.6 1.0 collective-permute-start.20
  233.6 4.8 %fusion.19 = f32[384,1536]{1,0:T(8,128)S(1)} fusion(bf16[1536,1536]{1,0:T(8,128)(2,1)} %get-tuple-element.19, f32[1536]{0:T(1024)S(1)} %convert_element_type.184, s32[]{:T(128)S(6)} %select_n.261), kind=kOutput, calls=%fused_computation.53 | convolution fusion | flops 1813708800 | bytes 8263684 | tf_op jit(solution)/shard_map/dot_general | solution.py:28
  238.4 5.3 %collective-permute-start.13 = (bf16[384,1536]{1,0:T(8,128)(2,1)S(1)}, bf16[384,1536]{1,0:T(8,128)(2,1)S(1)}, u32[]{:S(2)}, u32[]{:S(2)}) collective-permute-start(bf16[384,1536]{1,0:T(8,128)(2,1)S(1)} %fusion.10), channel_id=1, source_target_pairs={{4,0},{8,4},{12,8},{16,12},{20,16},{24,20},{28,24},{5,1},{9,5},{13... | collective-permute-start | bytes 3538952 | tf_op jit(solution)/shard_map/ppermute | solution.py:48
  243.8 2.0 convolution_convert_fusion
  245.8 1.3 collective-permute-start.18
  247.1 2.1 fusion.20
  249.3 4.5 %fusion.12 = bf16[1,384,1536]{2,1,0:T(8,128)(2,1)} fusion(bf16[1536,1536]{1,0:T(8,128)(2,1)S(1)} %negate_convert_fusion, bf16[384,1536]{1,0:T(8,128)(2,1)S(1)} %collective-permute-done.20, bf16[384,1536]{1,0:T(8,128)(2,1)S(1)} %constant_dynamic-slice_fusion, f32[1536]{0:T(1024)S(1)} %convert_element_type.196, pred[]{:T(512)S(6)} %eq.22, pred[]{:T(512)S(6)} %eq.21, ...), kind=kOutput, calls=%fused_computation.28 | convolution fusion | flops 1816068096 | bytes 9443334 | tf_op jit(solution)/shard_map/dot_general | solution.py:24
  253.8 17.7 %collective-permute-done.13 = bf16[384,1536]{1,0:T(8,128)(2,1)S(1)} collective-permute-done((bf16[384,1536]{1,0:T(8,128)(2,1)S(1)}, bf16[384,1536]{1,0:T(8,128)(2,1)S(1)}, u32[]{:S(2)}, u32[]{:S(2)}) %collective-permute-start.13) | collective-permute-done | bytes 1179680 | tf_op jit(solution)/shard_map/ppermute | solution.py:48
  271.4 3.8 %collective-permute-done.18 = bf16[384,1536]{1,0:T(8,128)(2,1)S(1)} collective-permute-done((bf16[384,1536]{1,0:T(8,128)(2,1)S(1)}, bf16[384,1536]{1,0:T(8,128)(2,1)S(1)}, u32[]{:S(2)}, u32[]{:S(2)}) %collective-permute-start.18) | collective-permute-done | bytes 1179680 | tf_op jit(solution)/shard_map/ppermute | solution.py:48
  275.2 7.3 %select_bitcast_fusion = f32[1,384,1536]{2,1,0:T(8,128)} fusion(f32[384,1536]{1,0:T(8,128)S(1)} %fusion.20, f32[384,1536]{1,0:T(8,128)S(1)} %fusion.19, f32[1,384,1536]{2,1,0:T(8,128)S(1)} %copy-done.6, bf16[384,1536]{1,0:T(8,128)(2,1)S(1)} %collective-permute-done.18, bf16[384,1536]{1,0:T(8,128)(2,1)S(1)} %collective-permute-done.13, ...), kind=kOutput, calls=%fused_computation.37 | convolution fusion | flops 1837891584 | bytes 17700866 | tf_op jit(solution)/shard_map/dot_general | solution.py:20
  (59 shorter events, 0.7 us)
Async XLA Ops:
  0.6 28.1 %collective-permute-start = (bf16[384,1536]{1,0:T(8,128)(2,1)}, bf16[384,1536]{1,0:T(8,128)(2,1)S(1)}, u32[]{:S(2)}, u32[]{:S(2)}) collective-permute-start(bf16[384,1536]{1,0:T(8,128)(2,1)} %bitcast.41), channel_id=1, source_target_pairs={{0,1},{1,2},{2,3},{4,5},{5,6},{6,7},{8,9},{9,10},{10,11},{12,13},{... | collective-permute-start | bytes 3538952 | tf_op jit(solution)/shard_map/ppermute | solution.py:57
  3.9 28.7 %collective-permute-start.3 = (bf16[384,1536]{1,0:T(8,128)(2,1)}, bf16[384,1536]{1,0:T(8,128)(2,1)}, u32[]{:S(2)}, u32[]{:S(2)}) collective-permute-start(bf16[384,1536]{1,0:T(8,128)(2,1)} %bitcast.42), channel_id=1, source_target_pairs={{1,0},{2,1},{3,2},{5,4},{6,5},{7,6},{9,8},{10,9},{11,10},{13,12},{... | collective-permute-start | bytes 3538952 | tf_op jit(solution)/shard_map/ppermute | solution.py:57
  5.9 9.0 %copy-start = (bf16[1,384,1536]{2,1,0:T(8,128)(2,1)S(1)}, bf16[1,384,1536]{2,1,0:T(8,128)(2,1)}, u32[]{:S(2)}) copy-start(bf16[1,384,1536]{2,1,0:T(8,128)(2,1)} %param.6) | copy-start | bytes 3538948
  8.4 5.9 %collective-permute-start.6 = (f32[384]{0:T(512)S(1)}, f32[384]{0:T(512)}, u32[]{:S(2)}, u32[]{:S(2)}) collective-permute-start(f32[384]{0:T(512)S(1)} %get-tuple-element.3), channel_id=1, source_target_pairs={{4,0},{8,4},{12,8},{16,12},{20,16},{24,20},{28,24},{5,1},{9,5},{13... | collective-permute-start | bytes 4616 | tf_op jit(solution)/shard_map/ppermute | solution.py:48
  11.2 124.6 %copy-start.4 = (bf16[1,384,1536]{2,1,0:T(8,128)(2,1)S(1)}, bf16[1,384,1536]{2,1,0:T(8,128)(2,1)}, u32[]{:S(2)}) copy-start(bf16[1,384,1536]{2,1,0:T(8,128)(2,1)} %param.5) | copy-start | bytes 3538948
  15.0 96.9 %copy-start.17 = (bf16[16,1536]{1,0:T(8,128)(2,1)}, bf16[16,1536]{1,0:T(8,128)(2,1)S(1)}, u32[]{:S(2)}) copy-start(bf16[16,1536]{1,0:T(8,128)(2,1)S(1)} %fusion.47) | copy-start | bytes 147460
  15.1 43.8 %collective-permute-start.9 = (bf16[400,1536]{1,0:T(8,128)(2,1)S(1)}, bf16[400,1536]{1,0:T(8,128)(2,1)S(1)}, u32[]{:S(2)}, u32[]{:S(2)}) collective-permute-start(bf16[400,1536]{1,0:T(8,128)(2,1)S(1)} %pad_maximum_fusion.2), channel_id=1, source_target_pairs={{1,0},{2,1},{3,2},{5,4},{6,5},{7,6},{9,8},{10,9},{11,10},{13,12},{... | collective-permute-start | bytes 3686408 | tf_op jit(solution)/shard_map/ppermute | solution.py:57
  16.4 44.8 %collective-permute-start.7 = (bf16[400,1536]{1,0:T(8,128)(2,1)S(1)}, bf16[400,1536]{1,0:T(8,128)(2,1)S(1)}, u32[]{:S(2)}, u32[]{:S(2)}) collective-permute-start(bf16[400,1536]{1,0:T(8,128)(2,1)S(1)} %pad_maximum_fusion.2), channel_id=1, source_target_pairs={{0,1},{1,2},{2,3},{4,5},{5,6},{6,7},{8,9},{9,10},{10,11},{12,13},{... | collective-permute-start | bytes 3686408 | tf_op jit(solution)/shard_map/ppermute | solution.py:57
  28.8 34.2 %collective-permute-start.1 = (bf16[384,1536]{1,0:T(8,128)(2,1)S(1)}, bf16[384,1536]{1,0:T(8,128)(2,1)}, u32[]{:S(2)}, u32[]{:S(2)}) collective-permute-start(bf16[384,1536]{1,0:T(8,128)(2,1)S(1)} %collective-permute-done), channel_id=1, source_target_pairs={{1,2},{2,3},{5,6},{6,7},{9,10},{10,11},{13,14},{14,15},{17,18},{18... | collective-permute-start | bytes 3538952 | tf_op jit(solution)/shard_map/ppermute | solution.py:57
  32.6 51.6 %collective-permute-start.4 = (bf16[384,1536]{1,0:T(8,128)(2,1)}, bf16[384,1536]{1,0:T(8,128)(2,1)}, u32[]{:S(2)}, u32[]{:S(2)}) collective-permute-start(bf16[384,1536]{1,0:T(8,128)(2,1)} %collective-permute-done.3), channel_id=1, source_target_pairs={{1,0},{2,1},{5,4},{6,5},{9,8},{10,9},{13,12},{14,13},{17,16},{18,1... | collective-permute-start | bytes 3538952 | tf_op jit(solution)/shard_map/ppermute | solution.py:57
  58.9 1.0 copy-start.8
  59.9 50.7 %collective-permute-start.10 = (bf16[400,1536]{1,0:T(8,128)(2,1)S(1)}, bf16[400,1536]{1,0:T(8,128)(2,1)}, u32[]{:S(2)}, u32[]{:S(2)}) collective-permute-start(bf16[400,1536]{1,0:T(8,128)(2,1)S(1)} %collective-permute-done.9), channel_id=1, source_target_pairs={{1,0},{2,1},{5,4},{6,5},{9,8},{10,9},{13,12},{14,13},{17,16},{18,1... | collective-permute-start | bytes 3686408 | tf_op jit(solution)/shard_map/ppermute | solution.py:57
  61.2 49.4 %copy-start.10 = (bf16[400,1536]{1,0:T(8,128)(2,1)}, bf16[400,1536]{1,0:T(8,128)(2,1)S(1)}, u32[]{:S(2)}) copy-start(bf16[400,1536]{1,0:T(8,128)(2,1)S(1)} %collective-permute-done.7) | copy-start | bytes 3686404
  61.2 50.7 %collective-permute-start.8 = (bf16[400,1536]{1,0:T(8,128)(2,1)S(1)}, bf16[400,1536]{1,0:T(8,128)(2,1)}, u32[]{:S(2)}, u32[]{:S(2)}) collective-permute-start(bf16[400,1536]{1,0:T(8,128)(2,1)S(1)} %collective-permute-done.7), channel_id=1, source_target_pairs={{1,2},{2,3},{5,6},{6,7},{9,10},{10,11},{13,14},{14,15},{17,18},{18... | collective-permute-start | bytes 3686408 | tf_op jit(solution)/shard_map/ppermute | solution.py:57
  63.0 50.7 %collective-permute-start.2 = (bf16[384,1536]{1,0:T(8,128)(2,1)}, bf16[384,1536]{1,0:T(8,128)(2,1)}, u32[]{:S(2)}, u32[]{:S(2)}) collective-permute-start(bf16[384,1536]{1,0:T(8,128)(2,1)} %collective-permute-done.1), channel_id=1, source_target_pairs={{2,3},{6,7},{10,11},{14,15},{18,19},{22,23},{26,27},{30,31}} | collective-permute-start | bytes 3538952 | tf_op jit(solution)/shard_map/ppermute | solution.py:57
  84.3 51.6 %collective-permute-start.5 = (bf16[384,1536]{1,0:T(8,128)(2,1)}, bf16[384,1536]{1,0:T(8,128)(2,1)}, u32[]{:S(2)}, u32[]{:S(2)}) collective-permute-start(bf16[384,1536]{1,0:T(8,128)(2,1)} %collective-permute-done.4), channel_id=1, source_target_pairs={{1,0},{5,4},{9,8},{13,12},{17,16},{21,20},{25,24},{29,28}} | collective-permute-start | bytes 3538952 | tf_op jit(solution)/shard_map/ppermute | solution.py:57
  110.6 51.6 %collective-permute-start.11 = (bf16[400,1536]{1,0:T(8,128)(2,1)}, bf16[400,1536]{1,0:T(8,128)(2,1)}, u32[]{:S(2)}, u32[]{:S(2)}) collective-permute-start(bf16[400,1536]{1,0:T(8,128)(2,1)} %collective-permute-done.10), channel_id=1, source_target_pairs={{1,0},{5,4},{9,8},{13,12},{17,16},{21,20},{25,24},{29,28}} | collective-permute-start | bytes 3686408 | tf_op jit(solution)/shard_map/ppermute | solution.py:57
  111.9 50.3 %collective-permute-start.12 = (bf16[400,1536]{1,0:T(8,128)(2,1)}, bf16[400,1536]{1,0:T(8,128)(2,1)}, u32[]{:S(2)}, u32[]{:S(2)}) collective-permute-start(bf16[400,1536]{1,0:T(8,128)(2,1)} %collective-permute-done.8), channel_id=1, source_target_pairs={{2,3},{6,7},{10,11},{14,15},{18,19},{22,23},{26,27},{30,31}} | collective-permute-start | bytes 3686408 | tf_op jit(solution)/shard_map/ppermute | solution.py:57
  113.6 48.6 %copy-start.9 = (bf16[400,1536]{1,0:T(8,128)(2,1)S(1)}, bf16[400,1536]{1,0:T(8,128)(2,1)}, u32[]{:S(2)}) copy-start(bf16[400,1536]{1,0:T(8,128)(2,1)} %copy-done.8) | copy-start | bytes 3686404
  113.6 48.6 %copy-start.11 = (bf16[400,1536]{1,0:T(8,128)(2,1)S(1)}, bf16[400,1536]{1,0:T(8,128)(2,1)}, u32[]{:S(2)}) copy-start(bf16[400,1536]{1,0:T(8,128)(2,1)} %copy-done.10) | copy-start | bytes 3686404
  113.6 48.6 %copy-start.18 = (bf16[16,1536]{1,0:T(8,128)(2,1)S(1)}, bf16[16,1536]{1,0:T(8,128)(2,1)}, u32[]{:S(2)}) copy-start(bf16[16,1536]{1,0:T(8,128)(2,1)} %copy-done.17) | copy-start | bytes 147460
  166.4 2.2 copy-start.1
  166.5 1.5 copy-start.2
  166.5 1.9 copy-start.3
  166.6 4.1 %copy-start.12 = (bf16[384,1536]{1,0:T(8,128)(2,1)}, bf16[384,1536]{1,0:T(8,128)(2,1)S(1)}, u32[]{:S(2)}) copy-start(bf16[384,1536]{1,0:T(8,128)(2,1)S(1)} %slice.75) | copy-start | bytes 3538948
  183.9 13.5 %collective-permute-start.15 = (bf16[1536,1536]{1,0:T(8,128)(2,1)}, bf16[1536,1536]{1,0:T(8,128)(2,1)}, u32[]{:S(2)}, u32[]{:S(2)}) collective-permute-start(bf16[1536,1536]{1,0:T(8,128)(2,1)} %fusion), channel_id=1, source_target_pairs={{0,4},{8,12},{16,20},{24,28},{1,5},{9,13},{17,21},{25,29},{2,6},{1... | collective-permute-start | bytes 14155784 | tf_op jit(solution)/shard_map/ppermute | solution.py:48
  188.7 7.9 %copy-start.7 = (bf16[400,1536]{1,0:T(8,128)(2,1)S(1)}, bf16[400,1536]{1,0:T(8,128)(2,1)}, u32[]{:S(2)}) copy-start(bf16[400,1536]{1,0:T(8,128)(2,1)} %get-tuple-element.8) | copy-start | bytes 3686404
  188.7 8.7 %collective-permute-start.14 = (bf16[1536]{0:T(1024)(128)(2,1)S(1)}, bf16[1536]{0:T(1024)(128)(2,1)S(1)}, u32[]{:S(2)}, u32[]{:S(2)}) collective-permute-start(bf16[1536]{0:T(1024)(128)(2,1)S(1)} %get-tuple-element.5), channel_id=1, source_target_pairs={{0,4},{8,12},{16,20},{24,28},{1,5},{9,13},{17,21},{25,29},{2,6},{1... | collective-permute-start | bytes 9224 | tf_op jit(solution)/shard_map/ppermute | solution.py:48
  190.3 7.1 %copy-start.16 = (bf16[384,1536]{1,0:T(8,128)(2,1)S(1)}, bf16[384,1536]{1,0:T(8,128)(2,1)}, u32[]{:S(2)}) copy-start(bf16[384,1536]{1,0:T(8,128)(2,1)} %get-tuple-element.16) | copy-start | bytes 3538948
  196.6 1.3 copy-start.13
  196.6 1.6 copy-start.14
  196.6 2.0 copy-start.15
  208.9 10.4 %collective-permute-start.17 = (f32[1536]{0:T(1024)S(1)}, f32[1536]{0:T(1024)S(1)}, u32[]{:S(2)}, u32[]{:S(2)}) collective-permute-start(f32[1536]{0:T(1024)S(1)} %fusion.33), channel_id=1, source_target_pairs={{8,4},{16,12},{24,20},{9,5},{17,13},{25,21},{10,6},{18,14},{26,22}... | collective-permute-start | bytes 18440 | tf_op jit(solution)/shard_map/ppermute | solution.py:48
  210.2 10.5 %collective-permute-start.16 = (bf16[384,1536]{1,0:T(8,128)(2,1)S(1)}, bf16[384,1536]{1,0:T(8,128)(2,1)S(1)}, u32[]{:S(2)}, u32[]{:S(2)}) collective-permute-start(bf16[384,1536]{1,0:T(8,128)(2,1)S(1)} %get-tuple-element.20), channel_id=1, source_target_pairs={{0,4},{8,12},{16,20},{24,28},{1,5},{9,13},{17,21},{25,29},{2,6},{1... | collective-permute-start | bytes 3538952 | tf_op jit(solution)/shard_map/ppermute | solution.py:48
  219.4 24.4 %collective-permute-start.19 = (bf16[1536]{0:T(1024)(128)(2,1)S(1)}, bf16[1536]{0:T(1024)(128)(2,1)S(1)}, u32[]{:S(2)}, u32[]{:S(2)}) collective-permute-start(bf16[1536]{0:T(1024)(128)(2,1)S(1)} %get-tuple-element.7), channel_id=1, source_target_pairs={{4,12},{20,28},{5,13},{21,29},{6,14},{22,30},{7,15},{23,31}} | collective-permute-start | bytes 9224 | tf_op jit(solution)/shard_map/ppermute | solution.py:48
  232.6 16.6 %collective-permute-start.20 = (bf16[384,1536]{1,0:T(8,128)(2,1)S(1)}, bf16[384,1536]{1,0:T(8,128)(2,1)S(1)}, u32[]{:S(2)}, u32[]{:S(2)}) collective-permute-start(bf16[384,1536]{1,0:T(8,128)(2,1)S(1)} %constant_dynamic-slice_fusion), channel_id=1, source_target_pairs={{20,28},{21,29},{22,30},{23,31}} | collective-permute-start | bytes 3538952 | tf_op jit(solution)/shard_map/ppermute | solution.py:48
  238.4 33.0 %collective-permute-start.13 = (bf16[384,1536]{1,0:T(8,128)(2,1)S(1)}, bf16[384,1536]{1,0:T(8,128)(2,1)S(1)}, u32[]{:S(2)}, u32[]{:S(2)}) collective-permute-start(bf16[384,1536]{1,0:T(8,128)(2,1)S(1)} %fusion.10), channel_id=1, source_target_pairs={{4,0},{8,4},{12,8},{16,12},{20,16},{24,20},{28,24},{5,1},{9,5},{13... | collective-permute-start | bytes 3538952 | tf_op jit(solution)/shard_map/ppermute | solution.py:48
  245.8 29.4 %collective-permute-start.18 = (bf16[384,1536]{1,0:T(8,128)(2,1)S(1)}, bf16[384,1536]{1,0:T(8,128)(2,1)S(1)}, u32[]{:S(2)}, u32[]{:S(2)}) collective-permute-start(bf16[384,1536]{1,0:T(8,128)(2,1)S(1)} %convolution_convert_fusion), channel_id=1, source_target_pairs={{20,12},{21,13},{22,14},{23,15}} | collective-permute-start | bytes 3538952 | tf_op jit(solution)/shard_map/ppermute | solution.py:48
  249.2 25.9 %copy-start.5 = (bf16[1,384,1536]{2,1,0:T(8,128)(2,1)S(1)}, bf16[1,384,1536]{2,1,0:T(8,128)(2,1)}, u32[]{:S(2)}) copy-start(bf16[1,384,1536]{2,1,0:T(8,128)(2,1)} %param.5) | copy-start | bytes 3538948
  249.3 25.9 %copy-start.6 = (f32[1,384,1536]{2,1,0:T(8,128)S(1)}, f32[1,384,1536]{2,1,0:T(8,128)}, u32[]{:S(2)}) copy-start(f32[1,384,1536]{2,1,0:T(8,128)} %param.4) | copy-start | bytes 7077892

commit v3 on v2

v3 whole, which is shorter than its diff:
```python
import jax
import jax.numpy as jnp
from jax import lax
from jax.experimental import pallas as pl
from jax.experimental.pallas import tpu as pltpu
from jax.sharding import PartitionSpec as P

BF16 = jnp.bfloat16
F32 = jnp.float32

ANY = pl.BlockSpec(memory_space=pl.ANY)


def after(block, *others):
    def body(*refs):
        del refs

    return pl.pallas_call(
        body,
        out_shape=jax.ShapeDtypeStruct(block.shape, block.dtype),
        in_specs=[ANY] * (1 + len(others)),
        out_specs=ANY,
        input_output_aliases={0: 0},
    )(block, *others)


def early_forms_kernel(
    flags, prev_whole, prev_rows, own_rows, own, prev, separator, scale, scale_here, pivot_scale,
    link, first, partial, form, left_diag, right_diag,
):
    part = jnp.where(flags[0] == 1, 0.0, -dot_nt(prev_whole[...], own[...])).astype(BF16)
    link[...] = part
    first[...] = (part.astype(F32) * scale_here[0:1].astype(F32)).astype(BF16)
    partial[...] = separator[...] - dot_nt(own_rows[...], own[...])
    form[...] = dot_nt(prev_rows[...], prev[...])
    square = part * part
    right_diag[...] = dot_nn(pivot_scale[...], square)

    @pl.when(pl.program_id(0) == 0)
    def _():
        left_diag[...] = jnp.zeros_like(left_diag)

    left_diag[...] += dot_nt(scale_here[...], square)


def early_forms(flags, prev_whole, prev_rows, own_rows, own, prev, separator, scale, pivot_scale):
    rows, order = own_rows.shape
    width = 256
    whole = lambda shape: pl.BlockSpec(shape, lambda j, f: (0, 0))
    down = lambda count: pl.BlockSpec((width, count), lambda j, f: (j, 0))
    along = lambda count: pl.BlockSpec((count, width), lambda j, f: (0, j))
    return pl.pallas_call(
        early_forms_kernel,
        out_shape=[
            jax.ShapeDtypeStruct((order, order), BF16),
            jax.ShapeDtypeStruct((order, order), BF16),
            jax.ShapeDtypeStruct((rows, order), F32),
            jax.ShapeDtypeStruct((rows, order), F32),
            jax.ShapeDtypeStruct((8, order), F32),
            jax.ShapeDtypeStruct((8, order), F32),
        ],
        grid_spec=pltpu.PrefetchScalarGridSpec(
            num_scalar_prefetch=1,
            grid=(order // width,),
            in_specs=[
                whole((order, order)),
                whole((rows, order)),
                whole((rows, order)),
                down(order),
                down(order),
                along(rows),
                whole((8, order)),
                along(8),
                whole((8, order)),
            ],
            out_specs=[
                along(order),
                along(order),
                along(rows),
                along(rows),
                whole((8, order)),
                along(8),
            ],
        ),
        compiler_params=pltpu.CompilerParams(vmem_limit_bytes=32 * 1024 * 1024),
        cost_estimate=pl.CostEstimate(flops=0, bytes_accessed=0, transcendentals=0),
    )(flags, prev_whole, prev_rows, own_rows, own, prev, separator, scale, scale, pivot_scale)


def scaled_by(matrix, factors):
    return (matrix.astype(F32) * factors.astype(F32)[None, :]).astype(BF16)


def row_scaled_by(matrix, factors):
    return (matrix.astype(F32) * factors.astype(F32)[:, None]).astype(BF16)


def dot_nt(left, right):
    return lax.dot_general(left, right, (((1,), (1,)), ((), ())), preferred_element_type=F32)


def dot_nn(left, right):
    return lax.dot_general(left, right, (((1,), (0,)), ((), ())), preferred_element_type=F32)


def dot_tn(left, right):
    return lax.dot_general(left, right, (((0,), (0,)), ((), ())), preferred_element_type=F32)


def rows_of(scale):
    return jnp.broadcast_to(scale[None, :], (8, scale.shape[0]))


def on_device(sep_block, own_couple, prev_couple, inner_diag):
    separator = sep_block[0]
    own_rows = own_couple[0]
    prev_rows = prev_couple[0]
    reciprocal = 1.0 / inner_diag[0]
    rows, order = own_rows.shape
    place = lax.axis_index("space")
    size = lax.axis_size("space")
    row_start = place * rows
    partition = lax.axis_index("tm")
    parts = lax.axis_size("tm")

    def between(block, route):
        return lax.ppermute(block, "tm", [(a, b) for a, b in route if 0 <= b < parts])

    even = range(0, parts, 2)
    pivots = range(1, parts, 4)
    everyone = range(parts)

    def one_step(ahead, back, step):
        up = [(j, j + 1) for j in range(step - 1, size - 1)]
        down = [(j, j - 1) for j in range(1, size - step + 1)]
        return lax.ppermute(ahead, "space", up), lax.ppermute(back, "space", down)

    def block_at(arrived, spot):
        block = arrived[0][0]
        for step in range(1, size):
            if spot + step < size:
                block = jnp.where(place == spot + step, arrived[step][0], block)
            if spot - step >= 0:
                block = jnp.where(place == spot - step, arrived[step][1], block)
        return block

    own_arrived = [(own_rows, own_rows)]
    prev_arrived = [(prev_rows, prev_rows)]
    for step in range(1, size):
        own_arrived.append(one_step(*own_arrived[-1], step))
        prev_arrived.append(one_step(*prev_arrived[-1], step))

    own_scaled = scaled_by(own_rows, reciprocal)
    prev_scaled = scaled_by(prev_rows, reciprocal)
    own_sum = jnp.sum(own_scaled.astype(F32) * own_rows.astype(F32), axis=1)
    prev_sum = jnp.sum(prev_scaled.astype(F32) * prev_rows.astype(F32), axis=1)
    row_ids = lax.broadcasted_iota(jnp.int32, separator.shape, 0) + row_start
    col_ids = lax.broadcasted_iota(jnp.int32, separator.shape, 1)
    sep_diag = jnp.sum(jnp.where(row_ids == col_ids, separator, 0.0), axis=1)
    diag_rows = sep_diag - own_sum - between(prev_sum, [(p, p - 1) for p in everyone])
    diag = jnp.zeros((order,), F32)
    diag = lax.dynamic_update_slice_in_dim(diag, diag_rows, row_start, 0)
    for shift in range(1, size):
        ring = [(j, (j + shift) % size) for j in range(size)]
        piece = lax.ppermute(diag_rows, "space", ring)
        at = (place + size - shift) % size
        diag = lax.dynamic_update_slice_in_dim(diag, piece, at * rows, 0)
    scale = (1.0 / jnp.maximum(diag, 1.0)).astype(BF16)
    pivot_scale = between(scale, [(p, p + 1) for p in even])

    left_side = place < size // 2
    late_start = jnp.where(left_side, size - 1, 0) * rows
    is_end = jnp.logical_or(place == 0, place == size - 1)
    own_full = jnp.concatenate([block_at(own_arrived, spot) for spot in range(size)])
    before = prev_arrived[:-1] + [(jnp.zeros_like(prev_rows),) * 2]
    prev_blocks = [block_at(before, spot) for spot in range(size)]
    prev_first = jnp.concatenate(prev_blocks)
    prev_far = jnp.where(left_side, prev_blocks[-1], prev_blocks[0])
    prev_first, prev_far = lax.optimization_barrier((prev_first, prev_far))

    is_first = partition == 0
    is_pivot = partition % 2 == 0
    is_receiver = partition % 2 == 1
    flags = jnp.stack([is_first, is_end, left_side]).astype(jnp.int32)
    link, first, partial, prev_form, left_diag, right_diag = early_forms(
        flags, scaled_by(prev_first, reciprocal), prev_scaled, own_scaled, own_full, prev_first,
        separator, rows_of(scale), rows_of(pivot_scale),
    )

    flags = after(flags, link)
    end_block = jnp.where(flags[2] == 1, prev_arrived[-1][1], prev_arrived[-1][0])
    prev_late = jnp.where(flags[1] == 1, end_block, prev_far)
    link_late = (-dot_nt(scaled_by(prev_late, reciprocal), own_full)).astype(BF16)
    link_late = jnp.where(is_first, jnp.zeros_like(link_late), link_late)
    link = lax.dynamic_update_slice_in_dim(link, link_late, late_start, 0)
    first_late = scaled_by(link_late, scale)
    first = lax.dynamic_update_slice_in_dim(first, first_late, late_start, 0)
    pivot_first = between(first, [(p, p + 1) for p in even])
    late_square = link_late * link_late
    left_diag = lax.dynamic_update_slice_in_dim(
        left_diag[0], dot_nt(rows_of(scale), late_square)[0], late_start, 0
    )
    left_diag = between(left_diag, [(p, p - 1) for p in even])
    late_scale = lax.dynamic_slice_in_dim(pivot_scale, late_start, rows, 0)
    late_scale = jnp.where(is_end, late_scale, jnp.zeros_like(late_scale))
    right_diag = right_diag[0] + dot_nn(rows_of(late_scale), late_square)[0]
    prev_form = lax.dynamic_update_slice_in_dim(
        prev_form, dot_nt(prev_scaled, prev_late), late_start, 1
    )

    first_rows = lax.dynamic_slice_in_dim(first, row_start, rows, 0)
    left_form = dot_nt(first_rows, link)
    to_earlier = jnp.where(is_pivot, prev_form + left_form, prev_form).astype(BF16)
    from_later = between(to_earlier, [(p, p - 1) for p in everyone])
    next_link = (-dot_nn(pivot_first, link)).astype(BF16)
    next_rows = lax.dynamic_slice_in_dim(next_link, row_start, rows, 0)
    pivot_rows = between(next_rows, [(p, p + 2) for p in pivots if p != 1])

    next_diag = diag - left_diag - right_diag
    next_scale = (1.0 / jnp.maximum(next_diag, 1.0)).astype(BF16)
    next_pivot_scale = between(next_scale, [(p, p + 2) for p in pivots])
    left_next = dot_nt(scaled_by(next_rows, next_scale), next_link).astype(BF16)
    from_pivot = between(left_next, [(p, p - 2) for p in pivots])

    link_cols = lax.dynamic_slice_in_dim(link, row_start, rows, 1)
    right_form = dot_tn(row_scaled_by(link_cols, pivot_scale), link)

    is_last = partition % 4 == 3
    next_cols = lax.dynamic_slice_in_dim(next_link, row_start, rows, 1)
    right_next = dot_tn(row_scaled_by(next_cols, next_pivot_scale), next_link)
    last_rows = (-dot_nn(scaled_by(pivot_rows, next_pivot_scale), next_link)).astype(BF16)
    link_rows = lax.dynamic_slice_in_dim(link, row_start, rows, 0)
    out_link = jnp.where(is_last, last_rows, jnp.where(is_receiver, next_rows, link_rows))
    updates = jnp.where(is_last, right_form + right_next, jnp.where(is_receiver, right_form, 0.0))
    updates = lax.optimization_barrier(updates)
    schur = partial - updates - from_later.astype(F32) - from_pivot.astype(F32)
    return (schur[None], out_link[None])


def solution(mesh):
    placed = (P("tm", "space", None), P("tm", "space", None), P("tm", "space", None), P("tm", None))
    return jax.shard_map(
        on_device,
        mesh=mesh,
        in_specs=placed,
        out_specs=(P("tm", "space", None), P("tm", "space", None)),
        check_vma=False,
    )
```

time: 283 us -> 289 us (1.021)
  waiting for transfers between devices: 146 us -> 116 us
  starting transfers between devices: 39.8 us -> 69.6 us
  matrix products: 69.9 us -> 41 us
  Pallas kernels: 0 us -> 22.6 us
  local copies, waits for them, and re-layouts: 7.86 us -> 14 us
  other arithmetic: 17.4 us -> 22.4 us
    ppermute x12, waiting for transfers between devices: 124 us -> 81.7 us  [one_step(): return (lax.ppermute(ahead, 'space', up), lax.ppermute(back, 'space', down))]
    ppermute x0 -> x3, starting transfers between devices: none -> 28.7 us  [on_device(): piece = lax.ppermute(diag_rows, 'space', ring)]
    dot_general x8 -> x5, matrix products: 44.7 us -> 18.6 us  [dot_nt(): lax.dot_general(left, right, (((1,), (1,)), ((), ())), preferred_element_...]
    pallas_call x0 -> x2, Pallas kernels: none -> 22.6 us  [the longest x1 22.6 us: early_forms(): pl.pallas_call(early_forms_kernel, out_shape=[jax.ShapeDtypeStruct((order...]
    ppermute x0 -> x3, waiting for transfers between devices: none -> 10.8 us  [on_device(): piece = lax.ppermute(diag_rows, 'space', ring)]
    unnamed x38 -> x60, local copies, waits for them, and re-layouts: 2.76 us -> 7.81 us
    convert_element_type x2 -> x3, other arithmetic: 0.02 us -> 3.9 us  [scaled_by(): return (matrix.astype(F32) * factors.astype(F32)[None, :]).astype(BF16)]
    add x4 -> x0, other arithmetic: 3.15 us -> none  [diag_of(): return block[rows, :rows].astype(F32) + block[rows + 1, :rows].astype(F32)]
  transfers between devices with their start and end apart: 21 -> 23, of which waited for: 10 -> 9; matrix products, arithmetic and copies ran while one was open for 19% -> 20% of each run, Pallas kernels for 0% -> 8%
where the time goes in v3:
time: 289 us; the launch traced here: 288 us
  waiting for transfers between devices  116 us (40%)
  starting transfers between devices  69.6 us (24%)
  matrix products  41 us (14%)
  Pallas kernels  22.6 us (8%)
  other arithmetic  22.4 us (8%)
  local copies, waits for them, and re-layouts  14 us (5%)
    ppermute x12, waiting for transfers between devices, one_step(): return (lax.ppermute(ahead, 'space', up), lax.ppermute(back, 'space', down))  81.7 us
    ppermute x3, starting transfers between devices, on_device(): piece = lax.ppermute(diag_rows, 'space', ring)  28.7 us
    ppermute x8, waiting for transfers between devices, between(): lax.ppermute(block, 'tm', [(a, b) for a, b in route if 0 <= b < parts])  23.7 us
    pallas_call x1, Pallas kernels, early_forms(): pl.pallas_call(early_forms_kernel, out_shape=[jax.ShapeDtypeStruct((order...  22.6 us
    ppermute x12, starting transfers between devices, one_step(): return (lax.ppermute(ahead, 'space', up), lax.ppermute(back, 'space', down))  22.1 us
    ppermute x8, starting transfers between devices, between(): lax.ppermute(block, 'tm', [(a, b) for a, b in route if 0 <= b < parts])  18.7 us
    dot_general x5, matrix products, dot_nt(): lax.dot_general(left, right, (((1,), (1,)), ((), ())), preferred_element_...  18.6 us
    dot_general x3, matrix products, dot_nn(): lax.dot_general(left, right, (((1,), (0,)), ((), ())), preferred_element_...  15.5 us
  transfers between devices with their start and end apart: 23, of which 9 were waited for; matrix products, arithmetic and copies ran while one was open for 20% of the time, Pallas kernels for 8%

profile of v3, /device:TPU:3, one launch (start us, length us, event | category | flops | bytes accessed | tf_op | source)
XLA Modules:
  0.0 288.4 jit_solution(11453249403842579834)
XLA Ops:
  0.6 4.3 %collective-permute-start = (bf16[384,1536]{1,0:T(8,128)(2,1)}, bf16[384,1536]{1,0:T(8,128)(2,1)}, u32[]{:S(2)}, u32[]{:S(2)}) collective-permute-start(bf16[384,1536]{1,0:T(8,128)(2,1)} %bitcast.42), channel_id=1, source_target_pairs={{0,1},{1,2},{2,3},{4,5},{5,6},{6,7},{8,9},{9,10},{10,11},{12,13},{... | collective-permute-start | bytes 3538952 | tf_op jit(solution)/shard_map/ppermute | solution.py:136
  4.9 1.3 collective-permute-start.2
  6.2 5.0 %collective-permute-start.4 = (bf16[384,1536]{1,0:T(8,128)(2,1)}, bf16[384,1536]{1,0:T(8,128)(2,1)}, u32[]{:S(2)}, u32[]{:S(2)}) collective-permute-start(bf16[384,1536]{1,0:T(8,128)(2,1)} %bitcast.44), channel_id=1, source_target_pairs={{0,1},{1,2},{2,3},{4,5},{5,6},{6,7},{8,9},{9,10},{10,11},{12,13},{... | collective-permute-start | bytes 3538952 | tf_op jit(solution)/shard_map/ppermute | solution.py:136
  11.2 1.3 collective-permute-start.7
  12.5 0.7 divide_reduce_fusion
  13.2 15.5 %collective-permute-done = bf16[384,1536]{1,0:T(8,128)(2,1)} collective-permute-done((bf16[384,1536]{1,0:T(8,128)(2,1)}, bf16[384,1536]{1,0:T(8,128)(2,1)}, u32[]{:S(2)}, u32[]{:S(2)}) %collective-permute-start) | collective-permute-done | bytes 1179680 | tf_op jit(solution)/shard_map/ppermute | solution.py:136
  28.8 1.7 collective-permute-start.1
  30.5 3.1 %collective-permute-done.2 = bf16[384,1536]{1,0:T(8,128)(2,1)} collective-permute-done((bf16[384,1536]{1,0:T(8,128)(2,1)}, bf16[384,1536]{1,0:T(8,128)(2,1)}, u32[]{:S(2)}, u32[]{:S(2)}) %collective-permute-start.2) | collective-permute-done | bytes 1179680 | tf_op jit(solution)/shard_map/ppermute | solution.py:136
  33.6 1.3 collective-permute-start.3
  34.9 3.3 %fusion.10 = (f32[384]{0:T(512)S(1)}, f32[384]{0:T(512)S(1)}, bf16[384,1536]{1,0:T(8,128)(2,1)S(1)}, bf16[384,1536]{1,0:T(8,128)(2,1)}) fusion(f32[1536]{0:T(1024)S(1)} %divide_reduce_fusion, bf16[1,384,1536]{2,1,0:T(8,128)(2,1)} %param.5, bf16[1,384,1536]{2,1,0:T(8,128)(2,1)} %param.6), kind=kLoop, calls=%fused_computation.23 | loop fusion | flops 7077120 | bytes 4727808 | tf_op jit(solution)/shard_map/reduce_sum | solution.py:155
  38.2 5.2 %collective-permute-start.10 = (f32[384]{0:T(512)S(1)}, f32[384]{0:T(512)S(1)}, u32[]{:S(2)}, u32[]{:S(2)}) collective-permute-start(f32[384]{0:T(512)S(1)} %get-tuple-element.19), channel_id=1, source_target_pairs={{4,0},{8,4},{12,8},{16,12},{20,16},{24,20},{28,24},{5,1},{9,5},{13... | collective-permute-start | bytes 4616 | tf_op jit(solution)/shard_map/ppermute | solution.py:127
  43.9 1.9 collective-permute-done.10
  45.8 0.6 copy-done.29
  46.4 1.3 fusion.31
  47.7 2.4 collective-permute-start.11
  50.0 9.5 %collective-permute-done.11 = f32[384]{0:T(512)S(1)} collective-permute-done((f32[384]{0:T(512)}, f32[384]{0:T(512)S(1)}, u32[]{:S(2)}, u32[]{:S(2)}) %collective-permute-start.11) | collective-permute-done | bytes 1568 | tf_op jit(solution)/shard_map/ppermute | solution.py:165
  59.5 23.1 %collective-permute-start.12 = (f32[384]{0:T(512)}, f32[384]{0:T(512)}, u32[]{:S(2)}, u32[]{:S(2)}) collective-permute-start(f32[384]{0:T(512)} %get-tuple-element.25), channel_id=1, source_target_pairs={{0,2},{1,3},{2,0},{3,1},{4,6},{5,7},{6,4},{7,5},{8,10},{9,11},{10,... | collective-permute-start | bytes 4616 | tf_op jit(solution)/shard_map/ppermute | solution.py:165
  82.7 1.3 collective-permute-done.12
  83.9 3.3 %collective-permute-start.13 = (f32[384]{0:T(512)}, f32[384]{0:T(512)}, u32[]{:S(2)}, u32[]{:S(2)}) collective-permute-start(f32[384]{0:T(512)} %get-tuple-element.25), channel_id=1, source_target_pairs={{0,3},{1,0},{2,1},{3,2},{4,7},{5,4},{6,5},{7,6},{8,11},{9,8},{10,9... | collective-permute-start | bytes 4616 | tf_op jit(solution)/shard_map/ppermute | solution.py:165
  87.4 0.8 dynamic_update_slice.26
  88.3 0.9 dynamic_update_slice.27
  89.2 0.6 fusion.30
  89.8 1.3 collective-permute-start.14
  91.1 0.7 collective-permute-start.5
  91.8 1.3 collective-permute-start.8
  93.1 3.8 %broadcast_select_fusion = (bf16[384,1536]{1,0:T(8,128)(2,1)}, bf16[384,1536]{1,0:T(8,128)(2,1)S(1)}, bf16[384,1536]{1,0:T(8,128)(2,1)S(1)}, bf16[384,1536]{1,0:T(8,128)(2,1)S(1)}, bf16[384,1536]{1,0:T(8,128)(2,1)S(1)}) fusion(pred[]{:T(512)} %lt.51, bf16[384,1536]{1,0:T(8,128)(2,1)} %collective-permute-done.1, bf16[384,1536]{1,0:T(8,128)(2,1)} %collective-permute-done, ...), kind=kLoop, calls=%fused_computation.53 | loop fusion | flops 7667712 | bytes 11796485 | tf_op jit(solution)/shard_map/jit(_where)/select_n | solution.py:178
  97.3 1.6 collective-permute-start.15
  98.8 1.7 collective-permute-start.16
  100.5 0.7 collective-permute-start.6
  101.3 17.1 %collective-permute-done.8 = bf16[384,1536]{1,0:T(8,128)(2,1)S(1)} collective-permute-done((bf16[384,1536]{1,0:T(8,128)(2,1)}, bf16[384,1536]{1,0:T(8,128)(2,1)S(1)}, u32[]{:S(2)}, u32[]{:S(2)}) %collective-permute-start.8) | collective-permute-done | bytes 1179680 | tf_op jit(solution)/shard_map/ppermute | solution.py:136
  118.3 1.3 collective-permute-start.9
  119.6 3.3 %multiply_convert_fusion.prev_whole = bf16[1536,1536]{1,0:T(8,128)(2,1)} fusion(bf16[1536,1536]{1,0:T(8,128)(2,1)S(1)} %pad_maximum_fusion.prev, f32[1536]{0:T(1024)S(1)} %copy-done.25), kind=kLoop, calls=%fused_computation.1 | loop fusion | flops 7077888 | bytes 9443328 | tf_op jit(solution)/shard_map/convert_element_type | solution.py:91
  122.9 46.0 %collective-permute-done.9 = bf16[384,1536]{1,0:T(8,128)(2,1)S(1)} collective-permute-done((bf16[384,1536]{1,0:T(8,128)(2,1)S(1)}, bf16[384,1536]{1,0:T(8,128)(2,1)S(1)}, u32[]{:S(2)}, u32[]{:S(2)}) %collective-permute-start.9) | collective-permute-done | bytes 1179680 | tf_op jit(solution)/shard_map/ppermute | solution.py:136
  168.9 1.9 select_select_fusion.4
  170.9 2.4 pad_maximum_fusion.1.own
  175.1 22.6 %shard_map.59 = (bf16[1536,1536]{1,0:T(8,128)(2,1)}, bf16[1536,1536]{1,0:T(8,128)(2,1)}, f32[384,1536]{1,0:T(8,128)S(1)}, f32[384,1536]{1,0:T(8,128)S(1)}, f32[8,1536]{1,0:T(8,128)S(1)}, /*index=5*/f32[8,1536]{1,0:T(8,128)S(1)}) custom-call(s32[3]{0:T(128)S(1)} %add_convert_fusion.flags.refs_0_, bf16[1536,1536]{1,0:T(8,128)(2,1)} %multiply_convert_fusion.prev_whole, ...), custom_call_target="tpu_custom_call" | custom-call | tf_op jit(solution)/shard_map/pallas_call | solution.py:52
  197.6 1.4 copy-done.2
  199.0 0.6 copy-done.4
  199.6 0.6 copy-done.7
  200.3 1.4 copy-done.8
  201.7 1.4 fusion.32
  204.5 1.6 select_select_fusion
  206.8 0.7 copy-done.20
  207.5 7.9 %constant_dynamic-update-slice_fusion = (bf16[1536,1536]{1,0:T(8,128)(2,1)}, bf16[1536,1536]{1,0:T(8,128)(2,1)}, bf16[384,1536]{1,0:T(8,128)(2,1)}) fusion(bf16[1536,1536]{1,0:T(8,128)(2,1)} %get-tuple-element.12.refs_1_, s32[]{:T(128)S(6)} %select_n.272, bf16[1536,1536]{1,0:T(8,128)(2,1)} %get-tuple-element.14, f32[1536]{0:T(1024)} %get-tuple-element.22, ...), kind=kOutput, calls=%fused_computation.69 | convolution fusion | flops 1836122112 | bytes 9454084 | tf_op jit(solution)/shard_map/dot_general | solution.py:99
  215.4 1.5 collective-permute-start.17
  217.0 0.6 convert_element_type.119
  217.6 1.4 slice_reduce_fusion
  219.0 1.7 convolution_reduce_fusion
  220.7 1.4 dynamic_update_slice.30
  222.1 1.3 collective-permute-start.18
  223.4 2.1 convolution_dynamic-update-slice_fusion
  225.5 4.8 %fusion.3 = bf16[384,1536]{1,0:T(8,128)(2,1)S(1)} fusion(f32[384,1536]{1,0:T(8,128)S(1)} %convolution_dynamic-update-slice_fusion, bf16[1536,1536]{1,0:T(8,128)(2,1)} %get-tuple-element.37, bf16[1536,1536]{1,0:T(8,128)(2,1)} %get-tuple-element.38, s32[]{:T(128)S(6)} %select_n.256, pred[]{:T(512)S(6)} %eq.80), kind=kOutput, calls=%fused_computation.16 | convolution fusion | flops 1813708800 | bytes 9437189 | tf_op jit(solution)/shard_map/dot_general | solution.py:99
  230.6 2.1 collective-permute-done.18
  232.7 1.3 collective-permute-start.19
  234.0 4.8 %fusion.11 = f32[384,1536]{1,0:T(8,128)S(1)} fusion(bf16[1536,1536]{1,0:T(8,128)(2,1)} %get-tuple-element.37, f32[1536]{0:T(1024)S(1)} %copy-done.28, s32[]{:T(128)S(6)} %select_n.256), kind=kOutput, calls=%fused_computation.34 | convolution fusion | flops 1813708800 | bytes 8263684 | tf_op jit(solution)/shard_map/dot_general | solution.py:107
  238.9 6.0 %collective-permute-start.20 = (bf16[384,1536]{1,0:T(8,128)(2,1)S(1)}, bf16[384,1536]{1,0:T(8,128)(2,1)S(1)}, u32[]{:S(2)}, u32[]{:S(2)}) collective-permute-start(bf16[384,1536]{1,0:T(8,128)(2,1)S(1)} %fusion.3), channel_id=1, source_target_pairs={{4,0},{8,4},{12,8},{16,12},{20,16},{24,20},{28,24},{5,1},{9,5},{13... | collective-permute-start | bytes 3538952 | tf_op jit(solution)/shard_map/ppermute | solution.py:127
  244.9 10.8 %negate_convert_fusion = bf16[1536,1536]{1,0:T(8,128)(2,1)S(1)} fusion(bf16[1536,1536]{1,0:T(8,128)(2,1)} %collective-permute-done.17, bf16[1536,1536]{1,0:T(8,128)(2,1)} %get-tuple-element.37), kind=kOutput, calls=%fused_computation | convolution fusion | flops 7252475904 | bytes 14155776 | tf_op jit(solution)/shard_map/dot_general | solution.py:103
  255.8 0.7 collective-permute-start.22
  256.5 2.0 convolution_convert_fusion
  258.5 1.5 collective-permute-start.21
  260.1 2.1 fusion
  262.2 4.4 %fusion.5 = bf16[1,384,1536]{2,1,0:T(8,128)(2,1)} fusion(bf16[1536,1536]{1,0:T(8,128)(2,1)S(1)} %negate_convert_fusion, bf16[384,1536]{1,0:T(8,128)(2,1)S(1)} %collective-permute-done.22, bf16[384,1536]{1,0:T(8,128)(2,1)S(1)} %constant_dynamic-slice_fusion, bf16[1536,1536]{1,0:T(8,128)(2,1)} %get-tuple-element.37, s32[]{:T(128)S(6)} %select_n.256, ...), kind=kOutput, calls=%fused_computation.18 | convolution fusion | flops 1816068096 | bytes 9443334 | tf_op jit(solution)/shard_map/dot_general | solution.py:103
  266.7 19.7 %collective-permute-done.21 = bf16[384,1536]{1,0:T(8,128)(2,1)S(1)} collective-permute-done((bf16[384,1536]{1,0:T(8,128)(2,1)S(1)}, bf16[384,1536]{1,0:T(8,128)(2,1)S(1)}, u32[]{:S(2)}, u32[]{:S(2)}) %collective-permute-start.21) | collective-permute-done | bytes 1179680 | tf_op jit(solution)/shard_map/ppermute | solution.py:127
  286.4 2.1 subtract_bitcast_fusion
  (84 shorter events, 4.1 us)
Async XLA Ops:
  0.6 28.1 %collective-permute-start = (bf16[384,1536]{1,0:T(8,128)(2,1)}, bf16[384,1536]{1,0:T(8,128)(2,1)}, u32[]{:S(2)}, u32[]{:S(2)}) collective-permute-start(bf16[384,1536]{1,0:T(8,128)(2,1)} %bitcast.42), channel_id=1, source_target_pairs={{0,1},{1,2},{2,3},{4,5},{5,6},{6,7},{8,9},{9,10},{10,11},{12,13},{... | collective-permute-start | bytes 3538952 | tf_op jit(solution)/shard_map/ppermute | solution.py:136
  4.9 28.7 %collective-permute-start.2 = (bf16[384,1536]{1,0:T(8,128)(2,1)}, bf16[384,1536]{1,0:T(8,128)(2,1)}, u32[]{:S(2)}, u32[]{:S(2)}) collective-permute-start(bf16[384,1536]{1,0:T(8,128)(2,1)} %bitcast.43), channel_id=1, source_target_pairs={{1,0},{2,1},{3,2},{5,4},{6,5},{7,6},{9,8},{10,9},{11,10},{13,12},{... | collective-permute-start | bytes 3538952 | tf_op jit(solution)/shard_map/ppermute | solution.py:136
  6.2 84.9 %collective-permute-start.4 = (bf16[384,1536]{1,0:T(8,128)(2,1)}, bf16[384,1536]{1,0:T(8,128)(2,1)}, u32[]{:S(2)}, u32[]{:S(2)}) collective-permute-start(bf16[384,1536]{1,0:T(8,128)(2,1)} %bitcast.44), channel_id=1, source_target_pairs={{0,1},{1,2},{2,3},{4,5},{5,6},{6,7},{8,9},{9,10},{10,11},{12,13},{... | collective-permute-start | bytes 3538952 | tf_op jit(solution)/shard_map/ppermute | solution.py:136
  11.2 80.6 %collective-permute-start.7 = (bf16[384,1536]{1,0:T(8,128)(2,1)}, bf16[384,1536]{1,0:T(8,128)(2,1)}, u32[]{:S(2)}, u32[]{:S(2)}) collective-permute-start(bf16[384,1536]{1,0:T(8,128)(2,1)} %bitcast.45), channel_id=1, source_target_pairs={{1,0},{2,1},{3,2},{5,4},{6,5},{7,6},{9,8},{10,9},{11,10},{13,12},{... | collective-permute-start | bytes 3538952 | tf_op jit(solution)/shard_map/ppermute | solution.py:136
  13.2 25.0 %copy-start.24 = (f32[1536]{0:T(1024)}, f32[1536]{0:T(1024)S(1)}, u32[]{:S(2)}) copy-start(f32[1536]{0:T(1024)S(1)} %divide_reduce_fusion) | copy-start | bytes 18436
  13.2 30.3 %copy-start = (f32[1,384,1536]{2,1,0:T(8,128)S(1)}, f32[1,384,1536]{2,1,0:T(8,128)}, u32[]{:S(2)}) copy-start(f32[1,384,1536]{2,1,0:T(8,128)} %param.4) | copy-start | bytes 7077892
  28.8 64.3 %collective-permute-start.1 = (bf16[384,1536]{1,0:T(8,128)(2,1)}, bf16[384,1536]{1,0:T(8,128)(2,1)}, u32[]{:S(2)}, u32[]{:S(2)}) collective-permute-start(bf16[384,1536]{1,0:T(8,128)(2,1)} %collective-permute-done), channel_id=1, source_target_pairs={{1,2},{2,3},{5,6},{6,7},{9,10},{10,11},{13,14},{14,15},{17,18},{18... | collective-permute-start | bytes 3538952 | tf_op jit(solution)/shard_map/ppermute | solution.py:136
  33.6 59.5 %collective-permute-start.3 = (bf16[384,1536]{1,0:T(8,128)(2,1)}, bf16[384,1536]{1,0:T(8,128)(2,1)}, u32[]{:S(2)}, u32[]{:S(2)}) collective-permute-start(bf16[384,1536]{1,0:T(8,128)(2,1)} %collective-permute-done.2), channel_id=1, source_target_pairs={{1,0},{2,1},{5,4},{6,5},{9,8},{10,9},{13,12},{14,13},{17,16},{18,1... | collective-permute-start | bytes 3538952 | tf_op jit(solution)/shard_map/ppermute | solution.py:136
  38.2 7.6 %collective-permute-start.10 = (f32[384]{0:T(512)S(1)}, f32[384]{0:T(512)S(1)}, u32[]{:S(2)}, u32[]{:S(2)}) collective-permute-start(f32[384]{0:T(512)S(1)} %get-tuple-element.19), channel_id=1, source_target_pairs={{4,0},{8,4},{12,8},{16,12},{20,16},{24,20},{28,24},{5,1},{9,5},{13... | collective-permute-start | bytes 4616 | tf_op jit(solution)/shard_map/ppermute | solution.py:127
  45.8 0.6 copy-start.29
  47.7 11.9 %collective-permute-start.11 = (f32[384]{0:T(512)}, f32[384]{0:T(512)S(1)}, u32[]{:S(2)}, u32[]{:S(2)}) collective-permute-start(f32[384]{0:T(512)} %get-tuple-element.25), channel_id=1, source_target_pairs={{0,1},{1,2},{2,3},{3,0},{4,5},{5,6},{6,7},{7,4},{8,9},{9,10},{10,1... | collective-permute-start | bytes 4616 | tf_op jit(solution)/shard_map/ppermute | solution.py:165
  59.5 24.4 %collective-permute-start.12 = (f32[384]{0:T(512)}, f32[384]{0:T(512)}, u32[]{:S(2)}, u32[]{:S(2)}) collective-permute-start(f32[384]{0:T(512)} %get-tuple-element.25), channel_id=1, source_target_pairs={{0,2},{1,3},{2,0},{3,1},{4,6},{5,7},{6,4},{7,5},{8,10},{9,11},{10,... | collective-permute-start | bytes 4616 | tf_op jit(solution)/shard_map/ppermute | solution.py:165
  82.7 92.4 %copy-start.6 = (s32[3]{0:T(128)}, s32[3]{0:T(128)S(1)}, u32[]{:S(2)}) copy-start(s32[3]{0:T(128)S(1)} %add_convert_fusion.flags.refs_0_) | copy-start | bytes 40
  83.9 4.3 %collective-permute-start.13 = (f32[384]{0:T(512)}, f32[384]{0:T(512)}, u32[]{:S(2)}, u32[]{:S(2)}) collective-permute-start(f32[384]{0:T(512)} %get-tuple-element.25), channel_id=1, source_target_pairs={{0,3},{1,0},{2,1},{3,2},{4,7},{5,4},{6,5},{7,6},{8,11},{9,8},{10,9... | collective-permute-start | bytes 4616 | tf_op jit(solution)/shard_map/ppermute | solution.py:165
  89.8 84.7 %collective-permute-start.14 = (bf16[1536]{0:T(1024)(128)(2,1)S(1)}, bf16[1536]{0:T(1024)(128)(2,1)S(1)}, u32[]{:S(2)}, u32[]{:S(2)}) collective-permute-start(bf16[1536]{0:T(1024)(128)(2,1)S(1)} %get-tuple-element.23), channel_id=1, source_target_pairs={{0,4},{8,12},{16,20},{24,28},{1,5},{9,13},{17,21},{25,29},{2,6},{1... | collective-permute-start | bytes 9224 | tf_op jit(solution)/shard_map/ppermute | solution.py:127
  91.1 9.5 %collective-permute-start.5 = (bf16[384,1536]{1,0:T(8,128)(2,1)}, bf16[384,1536]{1,0:T(8,128)(2,1)S(1)}, u32[]{:S(2)}, u32[]{:S(2)}) collective-permute-start(bf16[384,1536]{1,0:T(8,128)(2,1)} %collective-permute-done.4), channel_id=1, source_target_pairs={{1,2},{2,3},{5,6},{6,7},{9,10},{10,11},{13,14},{14,15},{17,18},{18... | collective-permute-start | bytes 3538952 | tf_op jit(solution)/shard_map/ppermute | solution.py:136
  91.8 26.5 %collective-permute-start.8 = (bf16[384,1536]{1,0:T(8,128)(2,1)}, bf16[384,1536]{1,0:T(8,128)(2,1)S(1)}, u32[]{:S(2)}, u32[]{:S(2)}) collective-permute-start(bf16[384,1536]{1,0:T(8,128)(2,1)} %collective-permute-done.7), channel_id=1, source_target_pairs={{1,0},{2,1},{5,4},{6,5},{9,8},{10,9},{13,12},{14,13},{17,16},{18,1... | collective-permute-start | bytes 3538952 | tf_op jit(solution)/shard_map/ppermute | solution.py:136
  96.9 22.7 %copy-start.25 = (f32[1536]{0:T(1024)S(1)}, f32[1536]{0:T(1024)}, u32[]{:S(2)}) copy-start(f32[1536]{0:T(1024)} %copy-done.24) | copy-start | bytes 18436
  97.2 25.7 %copy-start.10 = (bf16[1536,1536]{1,0:T(8,128)(2,1)}, bf16[1536,1536]{1,0:T(8,128)(2,1)S(1)}, u32[]{:S(2)}) copy-start(bf16[1536,1536]{1,0:T(8,128)(2,1)S(1)} %pad_maximum_fusion.prev) | copy-start | bytes 14155780
  97.3 71.6 %copy-start.22 = (bf16[1,384,1536]{2,1,0:T(8,128)(2,1)S(1)}, bf16[1,384,1536]{2,1,0:T(8,128)(2,1)}, u32[]{:S(2)}) copy-start(bf16[1,384,1536]{2,1,0:T(8,128)(2,1)} %param.5) | copy-start | bytes 3538948
  97.3 107.2 %collective-permute-start.15 = (bf16[384,1536]{1,0:T(8,128)(2,1)}, bf16[384,1536]{1,0:T(8,128)(2,1)}, u32[]{:S(2)}, u32[]{:S(2)}) collective-permute-start(bf16[384,1536]{1,0:T(8,128)(2,1)} %collective-permute-done.3), channel_id=1, source_target_pairs={{1,0},{5,4},{9,8},{13,12},{17,16},{21,20},{25,24},{29,28}} | collective-permute-start | bytes 3538952 | tf_op jit(solution)/shard_map/ppermute | solution.py:136
  98.8 105.6 %collective-permute-start.16 = (bf16[384,1536]{1,0:T(8,128)(2,1)}, bf16[384,1536]{1,0:T(8,128)(2,1)}, u32[]{:S(2)}, u32[]{:S(2)}) collective-permute-start(bf16[384,1536]{1,0:T(8,128)(2,1)} %collective-permute-done.1), channel_id=1, source_target_pairs={{2,3},{6,7},{10,11},{14,15},{18,19},{22,23},{26,27},{30,31}} | collective-permute-start | bytes 3538952 | tf_op jit(solution)/shard_map/ppermute | solution.py:136
  100.5 22.4 %collective-permute-start.6 = (bf16[384,1536]{1,0:T(8,128)(2,1)S(1)}, bf16[384,1536]{1,0:T(8,128)(2,1)S(1)}, u32[]{:S(2)}, u32[]{:S(2)}) collective-permute-start(bf16[384,1536]{1,0:T(8,128)(2,1)S(1)} %collective-permute-done.5), channel_id=1, source_target_pairs={{2,3},{6,7},{10,11},{14,15},{18,19},{22,23},{26,27},{30,31}} | collective-permute-start | bytes 3538952 | tf_op jit(solution)/shard_map/ppermute | solution.py:136
  118.3 50.6 %collective-permute-start.9 = (bf16[384,1536]{1,0:T(8,128)(2,1)S(1)}, bf16[384,1536]{1,0:T(8,128)(2,1)S(1)}, u32[]{:S(2)}, u32[]{:S(2)}) collective-permute-start(bf16[384,1536]{1,0:T(8,128)(2,1)S(1)} %collective-permute-done.8), channel_id=1, source_target_pairs={{1,0},{5,4},{9,8},{13,12},{17,16},{21,20},{25,24},{29,28}} | collective-permute-start | bytes 3538952 | tf_op jit(solution)/shard_map/ppermute | solution.py:136
  170.8 2.5 copy-start.13
  170.8 2.8 copy-start.15
  170.8 3.2 %copy-start.17 = (bf16[384,1536]{1,0:T(8,128)(2,1)}, bf16[384,1536]{1,0:T(8,128)(2,1)S(1)}, u32[]{:S(2)}) copy-start(bf16[384,1536]{1,0:T(8,128)(2,1)S(1)} %get-tuple-element.33) | copy-start | bytes 3538948
  170.8 3.6 %copy-start.19 = (bf16[384,1536]{1,0:T(8,128)(2,1)}, bf16[384,1536]{1,0:T(8,128)(2,1)S(1)}, u32[]{:S(2)}) copy-start(bf16[384,1536]{1,0:T(8,128)(2,1)S(1)} %get-tuple-element.34) | copy-start | bytes 3538948
  170.8 4.2 %copy-start.1 = (bf16[384,1536]{1,0:T(8,128)(2,1)S(1)}, bf16[384,1536]{1,0:T(8,128)(2,1)}, u32[]{:S(2)}) copy-start(bf16[384,1536]{1,0:T(8,128)(2,1)} %get-tuple-element.36.prev_rows) | copy-start | bytes 3538948
  174.5 0.6 copy-start.26
  197.6 1.4 copy-start.2
  199.0 0.6 copy-start.4
  199.6 0.6 copy-start.7
  200.3 1.4 copy-start.8
  201.7 2.8 copy-start.11
  204.4 1.6 copy-start.14
  204.5 2.0 copy-start.16
  204.5 2.3 copy-start.18
  204.5 3.0 %copy-start.20 = (bf16[384,1536]{1,0:T(8,128)(2,1)S(1)}, bf16[384,1536]{1,0:T(8,128)(2,1)}, u32[]{:S(2)}) copy-start(bf16[384,1536]{1,0:T(8,128)(2,1)} %copy-done.19) | copy-start | bytes 3538948
  206.1 9.3 %copy-start.23 = (bf16[384,1536]{1,0:T(8,128)(2,1)}, bf16[384,1536]{1,0:T(8,128)(2,1)S(1)}, u32[]{:S(2)}) copy-start(bf16[384,1536]{1,0:T(8,128)(2,1)S(1)} %select_select_fusion) | copy-start | bytes 3538948
  207.5 9.4 %copy-start.27 = (bf16[1536]{0:T(1024)(128)(2,1)S(1)}, bf16[1536]{0:T(1024)(128)(2,1)}, u32[]{:S(2)}) copy-start(bf16[1536]{0:T(1024)(128)(2,1)} %copy-done.26) | copy-start | bytes 9220
  207.5 15.9 %copy-start.9 = (f32[384,1536]{1,0:T(8,128)S(1)}, f32[384,1536]{1,0:T(8,128)}, u32[]{:S(2)}) copy-start(f32[384,1536]{1,0:T(8,128)} %copy-done.8) | copy-start | bytes 7077892
  207.5 15.9 %copy-start.12 = (bf16[1,384,1536]{2,1,0:T(8,128)(2,1)S(1)}, bf16[1,384,1536]{2,1,0:T(8,128)(2,1)}, u32[]{:S(2)}) copy-start(bf16[1,384,1536]{2,1,0:T(8,128)(2,1)} %param.6) | copy-start | bytes 3538948
  215.4 29.5 %collective-permute-start.17 = (bf16[1536,1536]{1,0:T(8,128)(2,1)}, bf16[1536,1536]{1,0:T(8,128)(2,1)}, u32[]{:S(2)}, u32[]{:S(2)}) collective-permute-start(bf16[1536,1536]{1,0:T(8,128)(2,1)} %get-tuple-element.38), channel_id=1, source_target_pairs={{0,4},{8,12},{16,20},{24,28},{1,5},{9,13},{17,21},{25,29},{2,6},{1... | collective-permute-start | bytes 14155784 | tf_op jit(solution)/shard_map/ppermute | solution.py:127
  222.1 10.6 %collective-permute-start.18 = (f32[1536]{0:T(1024)}, f32[1536]{0:T(1024)S(1)}, u32[]{:S(2)}, u32[]{:S(2)}) collective-permute-start(f32[1536]{0:T(1024)} %dynamic_update_slice.30), channel_id=1, source_target_pairs={{8,4},{16,12},{24,20},{9,5},{17,13},{25,21},{10,6},{18,14},{26,22}... | collective-permute-start | bytes 18440 | tf_op jit(solution)/shard_map/ppermute | solution.py:127
  225.5 4.9 %copy-start.5 = (f32[8,1536]{1,0:T(8,128)S(1)}, f32[8,1536]{1,0:T(8,128)}, u32[]{:S(2)}) copy-start(f32[8,1536]{1,0:T(8,128)} %copy-done.4) | copy-start | bytes 147460
  225.5 4.9 %copy-start.21 = (bf16[384,1536]{1,0:T(8,128)(2,1)S(1)}, bf16[384,1536]{1,0:T(8,128)(2,1)}, u32[]{:S(2)}) copy-start(bf16[384,1536]{1,0:T(8,128)(2,1)} %get-tuple-element.41) | copy-start | bytes 3538948
  225.5 8.5 %copy-start.28 = (f32[1536]{0:T(1024)S(1)}, f32[1536]{0:T(1024)}, u32[]{:S(2)}) copy-start(f32[1536]{0:T(1024)} %convert_element_type.119) | copy-start | bytes 18436
  232.7 12.1 %collective-permute-start.19 = (bf16[1536]{0:T(1024)(128)(2,1)S(1)}, bf16[1536]{0:T(1024)(128)(2,1)S(1)}, u32[]{:S(2)}, u32[]{:S(2)}) collective-permute-start(bf16[1536]{0:T(1024)(128)(2,1)S(1)} %get-tuple-element.21), channel_id=1, source_target_pairs={{4,12},{20,28},{5,13},{21,29},{6,14},{22,30},{7,15},{23,31}} | collective-permute-start | bytes 9224 | tf_op jit(solution)/shard_map/ppermute | solution.py:127
  238.9 27.8 %collective-permute-start.20 = (bf16[384,1536]{1,0:T(8,128)(2,1)S(1)}, bf16[384,1536]{1,0:T(8,128)(2,1)S(1)}, u32[]{:S(2)}, u32[]{:S(2)}) collective-permute-start(bf16[384,1536]{1,0:T(8,128)(2,1)S(1)} %fusion.3), channel_id=1, source_target_pairs={{4,0},{8,4},{12,8},{16,12},{20,16},{24,20},{28,24},{5,1},{9,5},{13... | collective-permute-start | bytes 3538952 | tf_op jit(solution)/shard_map/ppermute | solution.py:127
  255.8 6.5 %collective-permute-start.22 = (bf16[384,1536]{1,0:T(8,128)(2,1)S(1)}, bf16[384,1536]{1,0:T(8,128)(2,1)S(1)}, u32[]{:S(2)}, u32[]{:S(2)}) collective-permute-start(bf16[384,1536]{1,0:T(8,128)(2,1)S(1)} %constant_dynamic-slice_fusion), channel_id=1, source_target_pairs={{20,28},{21,29},{22,30},{23,31}} | collective-permute-start | bytes 3538952 | tf_op jit(solution)/shard_map/ppermute | solution.py:127
  258.5 27.8 %collective-permute-start.21 = (bf16[384,1536]{1,0:T(8,128)(2,1)S(1)}, bf16[384,1536]{1,0:T(8,128)(2,1)S(1)}, u32[]{:S(2)}, u32[]{:S(2)}) collective-permute-start(bf16[384,1536]{1,0:T(8,128)(2,1)S(1)} %convolution_convert_fusion), channel_id=1, source_target_pairs={{20,12},{21,13},{22,14},{23,15}} | collective-permute-start | bytes 3538952 | tf_op jit(solution)/shard_map/ppermute | solution.py:127
  262.2 24.2 %copy-start.3 = (f32[384,1536]{1,0:T(8,128)S(1)}, f32[384,1536]{1,0:T(8,128)}, u32[]{:S(2)}) copy-start(f32[384,1536]{1,0:T(8,128)} %copy-done.2) | copy-start | bytes 7077892

commit v4 on v2

v4 whole, which is shorter than its diff:
```python
import functools

import jax
import jax.numpy as jnp
from jax import lax
from jax.experimental import pallas as pl
from jax.experimental.pallas import tpu as pltpu
from jax.sharding import PartitionSpec as P

BF16 = jnp.bfloat16
F32 = jnp.float32
EXTRA = 16
WIDTH = 256

ANY = pl.BlockSpec(memory_space=pl.ANY)
SHAPE = jax.ShapeDtypeStruct
FREE = pl.CostEstimate(flops=0, bytes_accessed=0, transcendentals=0)


def after(block, *others):
    def body(*refs):
        del refs

    return pl.pallas_call(
        body,
        out_shape=SHAPE(block.shape, block.dtype),
        in_specs=[ANY] * (1 + len(others)),
        out_specs=ANY,
        input_output_aliases={0: 0},
    )(block, *others)


def scaled_by(matrix, factors):
    return (matrix.astype(F32) * factors.astype(F32)[None, :]).astype(BF16)


def row_scaled_by(matrix, factors):
    return (matrix.astype(F32) * factors.astype(F32)[:, None]).astype(BF16)


def dot_nt(left, right):
    return lax.dot_general(left, right, (((1,), (1,)), ((), ())), preferred_element_type=F32)


def dot_nn(left, right):
    return lax.dot_general(left, right, (((1,), (0,)), ((), ())), preferred_element_type=F32)


def dot_tn(left, right):
    return lax.dot_general(left, right, (((0,), (0,)), ((), ())), preferred_element_type=F32)


def rows_of(scale):
    return jnp.broadcast_to(scale[None, :], (8, scale.shape[0]))


def whole_spec(shape):
    return pl.BlockSpec(shape, lambda j, f: (0,) * len(shape))


def along_spec(count):
    return pl.BlockSpec((count, WIDTH), lambda j, f: (0, j))


def down_spec(count):
    return pl.BlockSpec((WIDTH, count), lambda j, f: (j, 0))


def early_kernel(
    size, flags, prev_whole, prev_rows, own_rows, prev, separator, scale, scale_here, pivot_scale, *refs
):
    sources = refs[: 2 * size - 1]
    (link, first, partial, update, left_diag, right_diag, own_out, own, form, sems) = refs[2 * size - 1 :]
    rows = separator.shape[0]
    step = pl.program_id(0)
    here = pl.ds(pl.multiple_of(step * WIDTH, WIDTH), WIDTH)
    place = flags[2]

    def copies():
        for spot in range(size):
            for by, source in enumerate(sources):
                distance = (by + 1) // 2 if by % 2 else -(by // 2)
                target = own.at[pl.ds(spot * rows, rows)]
                copy = pltpu.make_async_copy(source.at[pl.ds(0, rows)], target, sems.at[spot])
                yield place - spot == distance, copy

    @pl.when(step == 0)
    def _():
        for chosen, copy in copies():
            pl.when(chosen)(copy.start)
        for chosen, copy in copies():
            pl.when(chosen)(copy.wait)
        pltpu.make_async_copy(own, own_out, sems.at[size]).start()
        left_diag[...] = jnp.zeros_like(left_diag)
        form[...] = jnp.zeros_like(form)

    block = own[here, :]
    part = jnp.where(flags[0] == 1, 0.0, -dot_nt(prev_whole[...], block)).astype(BF16)
    link[...] = part
    scaled = part * scale_here[0:1]
    first[...] = scaled
    partial[...] = separator[...] - dot_nt(own_rows[...], block)
    square = part * part
    right_diag[...] = dot_nn(pivot_scale[...], square)
    left_diag[...] += dot_nt(scale_here[...], square)

    @pl.when(flags[1] == 1)
    def _():
        mine = first[pl.ds(pl.multiple_of(place * rows, rows), rows), :]
        form[...] += dot_nt(mine, part)

    form[:, here] += dot_nt(prev_rows[...], prev[...])

    @pl.when(step == pl.num_programs(0) - 1)
    def _():
        update[...] = form[...].astype(BF16)
        pltpu.make_async_copy(own, own_out, sems.at[size]).wait()


def early_forms(flags, prev_whole, prev_rows, own_rows, prev, separator, scale, pivot_scale, sources):
    rows, order = own_rows.shape
    size = order // rows
    return pl.pallas_call(
        functools.partial(early_kernel, size),
        out_shape=[
            SHAPE((order, order), BF16),
            SHAPE((order, order), BF16),
            SHAPE((rows, order), F32),
            SHAPE((rows, order), BF16),
            SHAPE((8, order), F32),
            SHAPE((8, order), F32),
            SHAPE((order, order), BF16),
        ],
        grid_spec=pltpu.PrefetchScalarGridSpec(
            num_scalar_prefetch=1,
            grid=(order // WIDTH,),
            in_specs=[
                whole_spec((order, order)),
                whole_spec((rows, order)),
                whole_spec((rows, order)),
                down_spec(order),
                along_spec(rows),
                whole_spec((8, order)),
                along_spec(8),
                whole_spec((8, order)),
            ]
            + [ANY] * len(sources),
            out_specs=[
                along_spec(order),
                along_spec(order),
                along_spec(rows),
                whole_spec((rows, order)),
                whole_spec((8, order)),
                along_spec(8),
                ANY,
            ],
            scratch_shapes=[
                pltpu.VMEM((order, order), BF16),
                pltpu.VMEM((rows, order), F32),
                pltpu.SemaphoreType.DMA((size + 1,)),
            ],
        ),
        compiler_params=pltpu.CompilerParams(vmem_limit_bytes=40 * 1024 * 1024),
        cost_estimate=FREE,
    )(flags, prev_whole, prev_rows, own_rows, prev, separator, scale, scale, pivot_scale, *sources)


def late_kernel(
    size, flags, reciprocal, prev_rows, own, scale, late_scale, from_below, from_above, far, link_in, first_in,
    link, first, corner, left_diag, right_diag, raw, scaled, late, late_first, mine, sems,
):
    del link_in, first_in
    rows = raw.shape[0]
    place = flags[2]
    step = pl.program_id(0)
    here = pl.ds(pl.multiple_of(step * WIDTH, WIDTH), WIDTH)
    low = place < size // 2
    late_start = pl.multiple_of(jnp.where(low, (size - 1) * rows, 0), rows)
    late_rows = pl.ds(late_start, rows)
    my_rows = pl.ds(pl.multiple_of(place * rows, rows), rows)

    @pl.when(step == 0)
    def _():
        fetch = pltpu.make_async_copy(first.at[my_rows], mine, sems.at[1])
        fetch.start()
        for chosen, source in (
            (place == 0, from_above),
            (place == size - 1, from_below),
            (jnp.logical_and(place != 0, place != size - 1), far),
        ):
            copy = pltpu.make_async_copy(source, raw, sems.at[0])
            pl.when(chosen)(copy.start)
            pl.when(chosen)(copy.wait)
        fetch.wait()
        scaled[...] = (raw[...].astype(F32) * reciprocal[0:1]).astype(BF16)

    part = jnp.where(flags[0] == 1, 0.0, -dot_nt(scaled[...], own[...])).astype(BF16)
    late[:, here] = part
    late_first[:, here] = part * scale[0:1, here]

    @pl.when(step == pl.num_programs(0) - 1)
    def _():
        copies = [
            pltpu.make_async_copy(late, link.at[late_rows], sems.at[0]),
            pltpu.make_async_copy(late_first, first.at[late_rows], sems.at[1]),
        ]
        for copy in copies:
            copy.start()
        whole = late[...]
        square = whole * whole
        keep = jnp.where(flags[1] == 1, 1.0, 0.0)
        corner[...] = (dot_nt(prev_rows[...], raw[...]) + keep * dot_nt(mine[...], whole)).astype(BF16)
        left_diag[...] = dot_nt(scale[...], square)
        right_diag[...] = dot_nn(late_scale[...], square)
        for copy in copies:
            copy.wait()


def late_forms(flags, reciprocal, prev_rows, own, scale, late_scale, from_below, from_above, far, link, first):
    rows, order = prev_rows.shape
    size = order // rows
    return pl.pallas_call(
        functools.partial(late_kernel, size),
        out_shape=[
            SHAPE((order, order), BF16),
            SHAPE((order, order), BF16),
            SHAPE((rows, rows), BF16),
            SHAPE((8, rows), F32),
            SHAPE((8, order), F32),
        ],
        grid_spec=pltpu.PrefetchScalarGridSpec(
            num_scalar_prefetch=1,
            grid=(order // WIDTH,),
            in_specs=[
                whole_spec((8, order)),
                whole_spec((rows, order)),
                down_spec(order),
                whole_spec((8, order)),
                whole_spec((8, rows)),
                ANY,
                ANY,
                ANY,
                ANY,
                ANY,
            ],
            out_specs=[
                ANY,
                ANY,
                whole_spec((rows, rows)),
                whole_spec((8, rows)),
                whole_spec((8, order)),
            ],
            scratch_shapes=[
                pltpu.VMEM((rows, order), BF16),
                pltpu.VMEM((rows, order), BF16),
                pltpu.VMEM((rows, order), BF16),
                pltpu.VMEM((rows, order), BF16),
                pltpu.VMEM((rows, order), BF16),
                pltpu.SemaphoreType.DMA((2,)),
            ],
        ),
        input_output_aliases={9: 0, 10: 1},
        compiler_params=pltpu.CompilerParams(vmem_limit_bytes=24 * 1024 * 1024),
    )(flags, reciprocal, prev_rows, own, scale, late_scale, from_below, from_above, far, link, first)


def on_device(sep_block, own_couple, prev_couple, inner_diag):
    separator = sep_block[0]
    own_rows = own_couple[0]
    prev_rows = prev_couple[0]
    reciprocal = 1.0 / inner_diag[0]
    rows, order = own_rows.shape
    place = lax.axis_index("space")
    size = lax.axis_size("space")
    row_start = place * rows
    partition = lax.axis_index("tm")
    parts = lax.axis_size("tm")

    def between(block, route):
        return lax.ppermute(block, "tm", [(a, b) for a, b in route if 0 <= b < parts])

    even = range(0, parts, 2)
    pivots = range(1, parts, 4)
    everyone = range(parts)

    def one_step(ahead, back, step):
        up = [(j, j + 1) for j in range(step - 1, size - 1)]
        down = [(j, j - 1) for j in range(1, size - step + 1)]
        return lax.ppermute(ahead, "space", up), lax.ppermute(back, "space", down)

    def block_at(arrived, spot):
        block = arrived[0][0]
        for step in range(1, len(arrived)):
            if spot + step < size:
                block = jnp.where(place == spot + step, arrived[step][0], block)
            if spot - step >= 0:
                block = jnp.where(place == spot - step, arrived[step][1], block)
        return block

    own_arrived = [(own_rows, own_rows)]
    own_arrived.append(one_step(own_rows, own_rows, 1))

    own_scaled = scaled_by(own_rows, reciprocal)
    prev_scaled = scaled_by(prev_rows, reciprocal)
    own_sum = jnp.sum(own_scaled.astype(F32) * own_rows.astype(F32), axis=1)
    prev_sum = jnp.sum(prev_scaled.astype(F32) * prev_rows.astype(F32), axis=1)
    row_ids = lax.broadcasted_iota(jnp.int32, separator.shape, 0) + row_start
    col_ids = lax.broadcasted_iota(jnp.int32, separator.shape, 1)
    sep_diag = jnp.sum(jnp.where(row_ids == col_ids, separator, 0.0), axis=1)
    diag_rows = sep_diag - own_sum - between(prev_sum, [(p, p - 1) for p in everyone])
    high = lax.reduce_precision(diag_rows, 8, 7)
    words = jnp.stack([high, diag_rows - high]).astype(BF16)
    words = jnp.pad(words, ((0, EXTRA - 2), (0, order - rows)))
    words_arrived = [(words, words)]
    words_arrived.append(one_step(words, words, 1))
    prev_rows = after(prev_rows, *words_arrived[1])
    prev_arrived = [(prev_rows, prev_rows)]
    prev_arrived.append(one_step(prev_rows, prev_rows, 1))
    longer = [jnp.concatenate(pair) for pair in zip(own_arrived[1], words_arrived[1])]
    for step in range(2, size):
        longer = one_step(*longer, step)
        own_arrived.append(longer)
        words_arrived.append(tuple(block[rows:] for block in longer))
        prev_arrived.append(one_step(*prev_arrived[-1], step))

    words = [block_at(words_arrived, spot) for spot in range(size)]
    diag = jnp.concatenate([word[0, :rows].astype(F32) + word[1, :rows].astype(F32) for word in words])
    scale = (1.0 / jnp.maximum(diag, 1.0)).astype(BF16)
    pivot_scale = between(scale, [(p, p + 1) for p in even])

    left_side = place < size // 2
    late_start = jnp.where(left_side, size - 1, 0) * rows
    is_end = jnp.logical_or(place == 0, place == size - 1)
    prev_blocks = [block_at(prev_arrived[:-1], spot) for spot in range(size)]
    zero = jnp.zeros_like(prev_rows)
    prev_blocks[0] = jnp.where(place == size - 1, zero, prev_blocks[0])
    prev_blocks[-1] = jnp.where(place == 0, zero, prev_blocks[-1])
    prev_first = jnp.concatenate(prev_blocks)
    prev_far = jnp.where(left_side, prev_blocks[-1], prev_blocks[0])

    is_first = partition == 0
    is_pivot = partition % 2 == 0
    is_receiver = partition % 2 == 1
    flags = jnp.stack([is_first.astype(jnp.int32), is_pivot.astype(jnp.int32), place])
    sources = [own_rows]
    for up, down in own_arrived[1:]:
        sources += [up, down]
    link, first, partial, update, left_diag, right_diag, own_full = early_forms(
        flags, scaled_by(prev_first, reciprocal), prev_scaled, own_scaled, prev_first,
        separator, rows_of(scale), rows_of(pivot_scale), sources,
    )

    late_scale = lax.dynamic_slice_in_dim(pivot_scale, late_start, rows, 0)
    late_scale = jnp.where(is_end, late_scale, jnp.zeros_like(late_scale))
    link, first, corner, left_late, right_late = late_forms(
        flags, rows_of(reciprocal), prev_scaled, own_full, rows_of(scale), rows_of(late_scale),
        prev_arrived[-1][0], prev_arrived[-1][1], prev_far, link, first,
    )
    pivot_first = between(first, [(p, p + 1) for p in even])
    left_diag = lax.dynamic_update_slice_in_dim(left_diag[0], left_late[0], late_start, 0)
    left_diag = between(left_diag, [(p, p - 1) for p in even])
    right_diag = right_diag[0] + right_late[0]
    to_earlier = lax.dynamic_update_slice_in_dim(update, corner, late_start, 1)
    from_later = between(to_earlier, [(p, p - 1) for p in everyone])

    next_link = (-dot_nn(pivot_first, link)).astype(BF16)
    next_rows = lax.dynamic_slice_in_dim(next_link, row_start, rows, 0)
    pivot_rows = between(next_rows, [(p, p + 2) for p in pivots if p != 1])

    next_diag = diag - left_diag - right_diag
    next_scale = (1.0 / jnp.maximum(next_diag, 1.0)).astype(BF16)
    next_pivot_scale = between(next_scale, [(p, p + 2) for p in pivots])
    left_next = dot_nt(scaled_by(next_rows, next_scale), next_link).astype(BF16)
    from_pivot = between(left_next, [(p, p - 2) for p in pivots])

    link_cols = lax.dynamic_slice_in_dim(link, row_start, rows, 1)
    right_form = dot_tn(row_scaled_by(link_cols, pivot_scale), link)

    is_last = partition % 4 == 3
    next_cols = lax.dynamic_slice_in_dim(next_link, row_start, rows, 1)
    right_next = dot_tn(row_scaled_by(next_cols, next_pivot_scale), next_link)
    last_rows = (-dot_nn(scaled_by(pivot_rows, next_pivot_scale), next_link)).astype(BF16)
    link_rows = lax.dynamic_slice_in_dim(link, row_start, rows, 0)
    out_link = jnp.where(is_last, last_rows, jnp.where(is_receiver, next_rows, link_rows))
    updates = jnp.where(is_last, right_form + right_next, jnp.where(is_receiver, right_form, 0.0))
    updates = lax.optimization_barrier(updates)
    schur = partial - updates - from_later.astype(F32) - from_pivot.astype(F32)
    return (schur[None], out_link[None])


def solution(mesh):
    placed = (P("tm", "space", None), P("tm", "space", None), P("tm", "space", None), P("tm", None))
    return jax.shard_map(
        on_device,
        mesh=mesh,
        in_specs=placed,
        out_specs=(P("tm", "space", None), P("tm", "space", None)),
        check_vma=False,
    )
```

time: 283 us -> 260 us (0.919)
  matrix products: 69.9 us -> 21.5 us
  Pallas kernels: 0 us -> 33.2 us
  waiting for transfers between devices: 146 us -> 122 us
  other arithmetic: 17.4 us -> 23.1 us
  starting transfers between devices: 39.8 us -> 45.2 us
  local copies, waits for them, and re-layouts: 7.86 us -> 12 us
    dot_general x8 -> x1, matrix products: 44.7 us -> 2.02 us  [dot_nt(): lax.dot_general(left, right, (((1,), (1,)), ((), ())), preferred_element_...]
    pallas_call x0 -> x3, Pallas kernels: none -> 33.2 us  [the longest x1 25.5 us: early_forms(): pl.pallas_call(functools.partial(early_kernel, size), out_shape=[SHAPE((o...]
    ppermute x12 -> x14, waiting for transfers between devices: 124 us -> 95.7 us  [one_step(): return (lax.ppermute(ahead, 'space', up), lax.ppermute(back, 'space', down))]
    unnamed x38 -> x39, local copies, waits for them, and re-layouts: 2.76 us -> 9.97 us
    concatenate x2 -> x3, other arithmetic: 0.09 us -> 6.26 us  [the longest x2 3.83 us: on_device(): jnp.concatenate(pair)]
    dot_general x3 -> x2, matrix products: 18.3 us -> 12.4 us  [dot_nn(): lax.dot_general(left, right, (((1,), (0,)), ((), ())), preferred_element_...]
    ppermute x9 -> x8, waiting for transfers between devices: 22.3 us -> 26.4 us  [between(): lax.ppermute(block, 'tm', [(a, b) for a, b in route if 0 <= b < parts])]
    ppermute x12 -> x14, starting transfers between devices: 22.6 us -> 25.9 us  [one_step(): return (lax.ppermute(ahead, 'space', up), lax.ppermute(back, 'space', down))]
  transfers between devices with their start and end apart: 21 -> 22, of which waited for: 10 -> 10; matrix products, arithmetic and copies ran while one was open for 19% -> 17% of each run, Pallas kernels for 0% -> 10%
where the time goes in v4:
time: 260 us; the launch traced here: 258 us
  waiting for transfers between devices  122 us (47%)
  starting transfers between devices  45.2 us (17%)
  Pallas kernels  33.2 us (13%)
  other arithmetic  23.1 us (9%)
  matrix products  21.5 us (8%)
  local copies, waits for them, and re-layouts  12 us (5%)
    ppermute x14, waiting for transfers between devices, one_step(): return (lax.ppermute(ahead, 'space', up), lax.ppermute(back, 'space', down))  95.7 us
    ppermute x8, waiting for transfers between devices, between(): lax.ppermute(block, 'tm', [(a, b) for a, b in route if 0 <= b < parts])  26.4 us
    ppermute x14, starting transfers between devices, one_step(): return (lax.ppermute(ahead, 'space', up), lax.ppermute(back, 'space', down))  25.9 us
    pallas_call x1, Pallas kernels, early_forms(): pl.pallas_call(functools.partial(early_kernel, size), out_shape=[SHAPE((o...  25.5 us
    ppermute x8, starting transfers between devices, between(): lax.ppermute(block, 'tm', [(a, b) for a, b in route if 0 <= b < parts])  19.3 us
    dot_general x2, matrix products, dot_nn(): lax.dot_general(left, right, (((1,), (0,)), ((), ())), preferred_element_...  12.4 us
    unnamed x39, local copies, waits for them, and re-layouts  9.97 us
    pallas_call x1, Pallas kernels, late_forms(): pl.pallas_call(functools.partial(late_kernel, size), out_shape=[SHAPE((or...  7.78 us
  transfers between devices with their start and end apart: 22, of which 10 were waited for; matrix products, arithmetic and copies ran while one was open for 17% of the time, Pallas kernels for 10%

profile of v4, /device:TPU:3, one launch (start us, length us, event | category | flops | bytes accessed | tf_op | source)
XLA Modules:
  0.0 258.4 jit_solution(4423207302870496124)
XLA Ops:
  0.6 1.3 copy.15
  1.9 3.3 %collective-permute-start.7 = (bf16[384,1536]{1,0:T(8,128)(2,1)}, bf16[384,1536]{1,0:T(8,128)(2,1)S(1)}, u32[]{:S(2)}, u32[]{:S(2)}) collective-permute-start(bf16[384,1536]{1,0:T(8,128)(2,1)} %bitcast.5.refs_0_), channel_id=1, source_target_pairs={{0,1},{1,2},{2,3},{4,5},{5,6},{6,7},{8,9},{9,10},{10,11},{12,13},{... | collective-permute-start | bytes 3538952 | tf_op jit(solution)/shard_map/ppermute | solution.py:289
  5.2 1.3 collective-permute-start.10
  6.5 3.0 %fusion.4 = (f32[384]{0:T(512)S(1)}, f32[384]{0:T(512)S(1)}, bf16[384,1536]{1,0:T(8,128)(2,1)}, bf16[384,1536]{1,0:T(8,128)(2,1)S(1)}) fusion(f32[1536]{0:T(1024)S(1)} %divide_reduce_fusion, bf16[1,384,1536]{2,1,0:T(8,128)(2,1)} %param.5, bf16[1,384,1536]{2,1,0:T(8,128)(2,1)S(1)} %copy.15), kind=kLoop, calls=%fused_computation.14 | loop fusion | flops 7077120 | bytes 4727808 | tf_op jit(solution)/shard_map/reduce_sum | solution.py:305
  9.5 2.9 %collective-permute-start = (f32[384]{0:T(512)S(1)}, f32[384]{0:T(512)}, u32[]{:S(2)}, u32[]{:S(2)}) collective-permute-start(f32[384]{0:T(512)S(1)} %get-tuple-element.27), channel_id=1, source_target_pairs={{4,0},{8,4},{12,8},{16,12},{20,16},{24,20},{28,24},{5,1},{9,5},{13... | collective-permute-start | bytes 4616 | tf_op jit(solution)/shard_map/ppermute | solution.py:280
  12.4 2.1 select_reduce_fusion
  14.4 1.0 collective-permute-done
  15.4 0.7 reduce-precision_convert_fusion
  16.1 4.6 %collective-permute-start.1 = (bf16[16,1536]{1,0:T(8,128)(2,1)S(1)}, bf16[16,1536]{1,0:T(8,128)(2,1)}, u32[]{:S(2)}, u32[]{:S(2)}) collective-permute-start(bf16[16,1536]{1,0:T(8,128)(2,1)S(1)} %fusion.19), channel_id=1, source_target_pairs={{0,1},{1,2},{2,3},{4,5},{5,6},{6,7},{8,9},{9,10},{10,11},{12,13},{... | collective-permute-start | bytes 147464 | tf_op jit(solution)/shard_map/ppermute | solution.py:289
  20.7 1.3 collective-permute-start.2
  22.0 9.0 %collective-permute-done.1.refs_1_ = bf16[16,1536]{1,0:T(8,128)(2,1)} collective-permute-done((bf16[16,1536]{1,0:T(8,128)(2,1)S(1)}, bf16[16,1536]{1,0:T(8,128)(2,1)}, u32[]{:S(2)}, u32[]{:S(2)}) %collective-permute-start.1) | collective-permute-done | bytes 49184 | tf_op jit(solution)/shard_map/ppermute | solution.py:289
  31.0 3.9 %collective-permute-done.2.refs_2_ = bf16[16,1536]{1,0:T(8,128)(2,1)} collective-permute-done((bf16[16,1536]{1,0:T(8,128)(2,1)S(1)}, bf16[16,1536]{1,0:T(8,128)(2,1)}, u32[]{:S(2)}, u32[]{:S(2)}) %collective-permute-start.2) | collective-permute-done | bytes 49184 | tf_op jit(solution)/shard_map/ppermute | solution.py:289
  34.9 4.1 %collective-permute-start.3 = (bf16[384,1536]{1,0:T(8,128)(2,1)}, bf16[384,1536]{1,0:T(8,128)(2,1)}, u32[]{:S(2)}, u32[]{:S(2)}) collective-permute-start(bf16[384,1536]{1,0:T(8,128)(2,1)} %shard_map.59), channel_id=1, source_target_pairs={{0,1},{1,2},{2,3},{4,5},{5,6},{6,7},{8,9},{9,10},{10,11},{12,13},{... | collective-permute-start | bytes 3538952 | tf_op jit(solution)/shard_map/ppermute | solution.py:289
  39.0 1.3 collective-permute-start.5
  40.3 1.9 pad_maximum_fusion.1
  42.2 1.8 collective-permute-start.8
  44.0 1.9 pad_maximum_fusion.2
  46.0 1.3 collective-permute-start.11
  47.2 14.3 %collective-permute-done.3 = bf16[384,1536]{1,0:T(8,128)(2,1)} collective-permute-done((bf16[384,1536]{1,0:T(8,128)(2,1)}, bf16[384,1536]{1,0:T(8,128)(2,1)}, u32[]{:S(2)}, u32[]{:S(2)}) %collective-permute-start.3) | collective-permute-done | bytes 1179680 | tf_op jit(solution)/shard_map/ppermute | solution.py:289
  61.6 1.7 collective-permute-start.4
  63.3 3.2 %collective-permute-done.5 = bf16[384,1536]{1,0:T(8,128)(2,1)} collective-permute-done((bf16[384,1536]{1,0:T(8,128)(2,1)}, bf16[384,1536]{1,0:T(8,128)(2,1)}, u32[]{:S(2)}, u32[]{:S(2)}) %collective-permute-start.5) | collective-permute-done | bytes 1179680 | tf_op jit(solution)/shard_map/ppermute | solution.py:289
  66.4 1.3 collective-permute-start.6
  67.8 0.1 pad_add_fusion.flags
  67.8 0.7 collective-permute-start.9
  68.6 24.2 %collective-permute-done.11.refs_4_ = bf16[400,1536]{1,0:T(8,128)(2,1)} collective-permute-done((bf16[400,1536]{1,0:T(8,128)(2,1)}, bf16[400,1536]{1,0:T(8,128)(2,1)}, u32[]{:S(2)}, u32[]{:S(2)}) %collective-permute-start.11) | collective-permute-done | bytes 1228832 | tf_op jit(solution)/shard_map/ppermute | solution.py:289
  92.8 1.3 collective-permute-start.12
  94.1 0.7 collective-permute-start.14
  94.8 23.2 %collective-permute-done.6 = bf16[384,1536]{1,0:T(8,128)(2,1)} collective-permute-done((bf16[384,1536]{1,0:T(8,128)(2,1)}, bf16[384,1536]{1,0:T(8,128)(2,1)}, u32[]{:S(2)}, u32[]{:S(2)}) %collective-permute-start.6) | collective-permute-done | bytes 1179680 | tf_op jit(solution)/shard_map/ppermute | solution.py:289
  118.0 1.3 collective-permute-start.15
  119.3 3.0 %broadcast_select_fusion = (bf16[384,1536]{1,0:T(8,128)(2,1)S(1)}, bf16[384,1536]{1,0:T(8,128)(2,1)S(1)}, bf16[384,1536]{1,0:T(8,128)(2,1)S(1)}, bf16[384,1536]{1,0:T(8,128)(2,1)S(1)}, bf16[384,1536]{1,0:T(8,128)(2,1)S(1)}) fusion(pred[]{:T(512)S(6)} %lt.28, bf16[384,1536]{1,0:T(8,128)(2,1)} %collective-permute-done.4, ...), kind=kLoop, calls=%fused_computation.38 | loop fusion | flops 7667712 | bytes 11796485 | tf_op jit(solution)/shard_map/jit(_where)/select_n | solution.py:339
  122.3 3.2 %multiply_convert_fusion.prev_whole = bf16[1536,1536]{1,0:T(8,128)(2,1)} fusion(f32[1536]{0:T(1024)S(1)} %divide_reduce_fusion, bf16[384,1536]{1,0:T(8,128)(2,1)S(1)} %get-tuple-element.32, bf16[384,1536]{1,0:T(8,128)(2,1)S(1)} %get-tuple-element.34, bf16[384,1536]{1,0:T(8,128)(2,1)S(1)} %get-tuple-element.33, bf16[384,1536]{1,0:T(8,128)(2,1)S(1)} %get-tuple-element.31), kind=kLoop, calls=%fused_computation.1 | loop fusion | flops 23592960 | bytes 9443328 | tf_op jit(solution)/shard_map/convert_element_type | solution.py:34
  125.5 0.9 slice_select_fusion.1
  126.4 17.9 %collective-permute-done.12.refs_6_ = bf16[400,1536]{1,0:T(8,128)(2,1)S(1)} collective-permute-done((bf16[400,1536]{1,0:T(8,128)(2,1)}, bf16[400,1536]{1,0:T(8,128)(2,1)S(1)}, u32[]{:S(2)}, u32[]{:S(2)}) %collective-permute-start.12) | collective-permute-done | bytes 1228832 | tf_op jit(solution)/shard_map/ppermute | solution.py:289
  144.3 0.9 select_select_fusion.5
  145.2 0.5 copy-done.10
  145.8 0.0 copy-done.12
  145.8 0.0 copy-start
  145.8 1.4 collective-permute-start.13
  147.2 2.4 pad_maximum_fusion.prev
  149.7 4.2 %collective-permute-done.13 = bf16[1536]{0:T(1024)(128)(2,1)S(1)} collective-permute-done((bf16[1536]{0:T(1024)(128)(2,1)S(1)}, bf16[1536]{0:T(1024)(128)(2,1)S(1)}, u32[]{:S(2)}, u32[]{:S(2)}) %collective-permute-start.13) | collective-permute-done | bytes 3104 | tf_op jit(solution)/shard_map/ppermute | solution.py:280
  153.8 25.5 %shard_map.60 = (bf16[1536,1536]{1,0:T(8,128)(2,1)}, bf16[1536,1536]{1,0:T(8,128)(2,1)}, f32[384,1536]{1,0:T(8,128)S(1)}, bf16[384,1536]{1,0:T(8,128)(2,1)S(1)},...) custom-call(s32[3]{0:T(128)S(1)} %pad_add_fusion.flags, ...), custom_call_target="tpu_custom_call" | custom-call | tf_op jit(solution)/shard_map/pallas_call | solution.py:123
  179.3 0.1 dynamic-slice_select_fusion
  179.5 3.5 %copy-done.1 = bf16[1536,1536]{1,0:T(8,128)(2,1)S(1)} copy-done((bf16[1536,1536]{1,0:T(8,128)(2,1)S(1)}, bf16[1536,1536]{1,0:T(8,128)(2,1)}, u32[]{:S(2)}) %copy-start.1) | copy-done | bytes 4718616
  183.0 2.3 copy-done.3
  185.3 7.8 %shard_map.61 = (bf16[1536,1536]{1,0:T(8,128)(2,1)S(1)}, bf16[1536,1536]{1,0:T(8,128)(2,1)}, bf16[384,384]{1,0:T(8,128)(2,1)S(1)}, f32[8,384]{1,0:T(8,128)S(1)}, f32[8,1536]{1,0:T(8,128)S(1)}) custom-call(s32[3]{0:T(128)S(1)} %pad_add_fusion.flags, f32[8,1536]{1,0:T(8,128)S(1)} %broadcast_in_dim.25.reciprocal, ...), custom_call_target="tpu_custom_call", output_to_operand_aliasing={{0}: (9, {}), {1}: (10, {})} | custom-call | tf_op jit(solution)/shard_map/pallas_call | solution.py:222
  193.1 2.2 copy-done.2
  195.4 1.3 collective-permute-start.16
  196.7 0.8 slice_reduce_fusion
  197.5 0.3 dynamic_update_slice.6
  197.8 1.3 collective-permute-start.17
  199.1 0.8 constant_dynamic-update-slice_fusion
  199.9 8.9 %collective-permute-start.19 = (bf16[384,1536]{1,0:T(8,128)(2,1)}, bf16[384,1536]{1,0:T(8,128)(2,1)S(1)}, u32[]{:S(2)}, u32[]{:S(2)}) collective-permute-start(bf16[384,1536]{1,0:T(8,128)(2,1)} %constant_dynamic-update-slice_fusion), channel_id=1, source_target_pairs={{4,0},{8,4},{12,8},{16,12},{20,16},{24,20},{28,24},{5,1},{9,5},{13... | collective-permute-start | bytes 3538952 | tf_op jit(solution)/shard_map/ppermute | solution.py:280
  208.8 0.8 add_reduce_fusion
  209.7 1.5 collective-permute-start.18
  211.2 4.9 %fusion.7 = f32[384,1536]{1,0:T(8,128)S(1)} fusion(bf16[1536,1536]{1,0:T(8,128)(2,1)} %copy-done.2, f32[1536]{0:T(1024)S(1)} %convert_element_type.148, s32[]{:T(128)S(6)} %select_n.228), kind=kOutput, calls=%fused_computation.27 | convolution fusion | flops 1813708800 | bytes 8263684 | tf_op jit(solution)/shard_map/dot_general | solution.py:50
  216.1 9.3 %negate_convert_fusion = bf16[1536,1536]{1,0:T(8,128)(2,1)S(1)} fusion(bf16[1536,1536]{1,0:T(8,128)(2,1)} %collective-permute-done.16, bf16[1536,1536]{1,0:T(8,128)(2,1)S(1)} %bitcast.22), kind=kOutput, calls=%fused_computation | convolution fusion | flops 7252475904 | bytes 14155776 | tf_op jit(solution)/shard_map/dot_general | solution.py:46
  225.5 0.1 constant_dynamic-slice_fusion
  225.6 0.7 collective-permute-start.21
  226.3 2.0 convolution_convert_fusion
  228.4 1.3 collective-permute-start.20
  229.7 2.2 select_select_fusion
  231.9 3.1 %fusion.2 = bf16[1,384,1536]{2,1,0:T(8,128)(2,1)} fusion(bf16[1536,1536]{1,0:T(8,128)(2,1)S(1)} %negate_convert_fusion, bf16[384,1536]{1,0:T(8,128)(2,1)S(1)} %collective-permute-done.21, bf16[384,1536]{1,0:T(8,128)(2,1)S(1)} %constant_dynamic-slice_fusion, bf16[1536,1536]{1,0:T(8,128)(2,1)S(1)} %bitcast.22, s32[]{:T(128)S(6)} %select_n.228, ...), kind=kOutput, calls=%fused_computation.12 | convolution fusion | flops 1816068096 | bytes 9443334 | tf_op jit(solution)/shard_map/dot_general | solution.py:46
  235.0 21.2 %collective-permute-done.20 = bf16[384,1536]{1,0:T(8,128)(2,1)S(1)} collective-permute-done((bf16[384,1536]{1,0:T(8,128)(2,1)S(1)}, bf16[384,1536]{1,0:T(8,128)(2,1)S(1)}, u32[]{:S(2)}, u32[]{:S(2)}) %collective-permute-start.20) | collective-permute-done | bytes 1179680 | tf_op jit(solution)/shard_map/ppermute | solution.py:280
  256.2 2.2 subtract_bitcast_fusion
  (62 shorter events, 0.3 us)
Async XLA Ops:
  0.6 5.9 %copy-start.16 = (f32[1,1536]{1,0:T(1,128)S(1)}, f32[1,1536]{1,0:T(1,128)}, u32[]{:S(2)}) copy-start(f32[1,1536]{1,0:T(1,128)} %param.7) | copy-start | bytes 18436
  1.9 7.6 %copy-start.9 = (bf16[1,384,1536]{2,1,0:T(8,128)(2,1)}, bf16[1,384,1536]{2,1,0:T(8,128)(2,1)S(1)}, u32[]{:S(2)}) copy-start(bf16[1,384,1536]{2,1,0:T(8,128)(2,1)S(1)} %copy.15) | copy-start | bytes 3538948
  1.9 38.4 %collective-permute-start.7 = (bf16[384,1536]{1,0:T(8,128)(2,1)}, bf16[384,1536]{1,0:T(8,128)(2,1)S(1)}, u32[]{:S(2)}, u32[]{:S(2)}) collective-permute-start(bf16[384,1536]{1,0:T(8,128)(2,1)} %bitcast.5.refs_0_), channel_id=1, source_target_pairs={{0,1},{1,2},{2,3},{4,5},{5,6},{6,7},{8,9},{9,10},{10,11},{12,13},{... | collective-permute-start | bytes 3538952 | tf_op jit(solution)/shard_map/ppermute | solution.py:289
  5.2 38.9 %collective-permute-start.10 = (bf16[384,1536]{1,0:T(8,128)(2,1)}, bf16[384,1536]{1,0:T(8,128)(2,1)S(1)}, u32[]{:S(2)}, u32[]{:S(2)}) collective-permute-start(bf16[384,1536]{1,0:T(8,128)(2,1)} %bitcast.5.refs_0_), channel_id=1, source_target_pairs={{1,0},{2,1},{3,2},{5,4},{6,5},{7,6},{9,8},{10,9},{11,10},{13,12},{... | collective-permute-start | bytes 3538952 | tf_op jit(solution)/shard_map/ppermute | solution.py:289
  9.5 5.9 %collective-permute-start = (f32[384]{0:T(512)S(1)}, f32[384]{0:T(512)}, u32[]{:S(2)}, u32[]{:S(2)}) collective-permute-start(f32[384]{0:T(512)S(1)} %get-tuple-element.27), channel_id=1, source_target_pairs={{4,0},{8,4},{12,8},{16,12},{20,16},{24,20},{28,24},{5,1},{9,5},{13... | collective-permute-start | bytes 4616 | tf_op jit(solution)/shard_map/ppermute | solution.py:280
  16.1 14.9 %collective-permute-start.1 = (bf16[16,1536]{1,0:T(8,128)(2,1)S(1)}, bf16[16,1536]{1,0:T(8,128)(2,1)}, u32[]{:S(2)}, u32[]{:S(2)}) collective-permute-start(bf16[16,1536]{1,0:T(8,128)(2,1)S(1)} %fusion.19), channel_id=1, source_target_pairs={{0,1},{1,2},{2,3},{4,5},{5,6},{6,7},{8,9},{9,10},{10,11},{12,13},{... | collective-permute-start | bytes 147464 | tf_op jit(solution)/shard_map/ppermute | solution.py:289
  20.7 14.1 %collective-permute-start.2 = (bf16[16,1536]{1,0:T(8,128)(2,1)S(1)}, bf16[16,1536]{1,0:T(8,128)(2,1)}, u32[]{:S(2)}, u32[]{:S(2)}) collective-permute-start(bf16[16,1536]{1,0:T(8,128)(2,1)S(1)} %fusion.19), channel_id=1, source_target_pairs={{1,0},{2,1},{3,2},{5,4},{6,5},{7,6},{9,8},{10,9},{11,10},{13,12},{... | collective-permute-start | bytes 147464 | tf_op jit(solution)/shard_map/ppermute | solution.py:289
  34.9 26.7 %collective-permute-start.3 = (bf16[384,1536]{1,0:T(8,128)(2,1)}, bf16[384,1536]{1,0:T(8,128)(2,1)}, u32[]{:S(2)}, u32[]{:S(2)}) collective-permute-start(bf16[384,1536]{1,0:T(8,128)(2,1)} %shard_map.59), channel_id=1, source_target_pairs={{0,1},{1,2},{2,3},{4,5},{5,6},{6,7},{8,9},{9,10},{10,11},{12,13},{... | collective-permute-start | bytes 3538952 | tf_op jit(solution)/shard_map/ppermute | solution.py:289
  39.0 27.4 %collective-permute-start.5 = (bf16[384,1536]{1,0:T(8,128)(2,1)}, bf16[384,1536]{1,0:T(8,128)(2,1)}, u32[]{:S(2)}, u32[]{:S(2)}) collective-permute-start(bf16[384,1536]{1,0:T(8,128)(2,1)} %shard_map.59), channel_id=1, source_target_pairs={{1,0},{2,1},{3,2},{5,4},{6,5},{7,6},{9,8},{10,9},{11,10},{13,12},{... | collective-permute-start | bytes 3538952 | tf_op jit(solution)/shard_map/ppermute | solution.py:289
  42.2 25.6 %collective-permute-start.8 = (bf16[400,1536]{1,0:T(8,128)(2,1)}, bf16[400,1536]{1,0:T(8,128)(2,1)}, u32[]{:S(2)}, u32[]{:S(2)}) collective-permute-start(bf16[400,1536]{1,0:T(8,128)(2,1)} %pad_maximum_fusion.1), channel_id=1, source_target_pairs={{1,2},{2,3},{5,6},{6,7},{9,10},{10,11},{13,14},{14,15},{17,18},{18... | collective-permute-start | bytes 3686408 | tf_op jit(solution)/shard_map/ppermute | solution.py:289
  46.0 46.8 %collective-permute-start.11 = (bf16[400,1536]{1,0:T(8,128)(2,1)}, bf16[400,1536]{1,0:T(8,128)(2,1)}, u32[]{:S(2)}, u32[]{:S(2)}) collective-permute-start(bf16[400,1536]{1,0:T(8,128)(2,1)} %pad_maximum_fusion.2), channel_id=1, source_target_pairs={{1,0},{2,1},{5,4},{6,5},{9,8},{10,9},{13,12},{14,13},{17,16},{18,1... | collective-permute-start | bytes 3686408 | tf_op jit(solution)/shard_map/ppermute | solution.py:289
  61.6 32.5 %collective-permute-start.4 = (bf16[384,1536]{1,0:T(8,128)(2,1)}, bf16[384,1536]{1,0:T(8,128)(2,1)}, u32[]{:S(2)}, u32[]{:S(2)}) collective-permute-start(bf16[384,1536]{1,0:T(8,128)(2,1)} %collective-permute-done.3), channel_id=1, source_target_pairs={{1,2},{2,3},{5,6},{6,7},{9,10},{10,11},{13,14},{14,15},{17,18},{18... | collective-permute-start | bytes 3538952 | tf_op jit(solution)/shard_map/ppermute | solution.py:289
  66.4 51.6 %collective-permute-start.6 = (bf16[384,1536]{1,0:T(8,128)(2,1)}, bf16[384,1536]{1,0:T(8,128)(2,1)}, u32[]{:S(2)}, u32[]{:S(2)}) collective-permute-start(bf16[384,1536]{1,0:T(8,128)(2,1)} %collective-permute-done.5), channel_id=1, source_target_pairs={{1,0},{2,1},{5,4},{6,5},{9,8},{10,9},{13,12},{14,13},{17,16},{18,1... | collective-permute-start | bytes 3538952 | tf_op jit(solution)/shard_map/ppermute | solution.py:289
  67.8 57.6 %collective-permute-start.9 = (bf16[400,1536]{1,0:T(8,128)(2,1)}, bf16[400,1536]{1,0:T(8,128)(2,1)S(1)}, u32[]{:S(2)}, u32[]{:S(2)}) collective-permute-start(bf16[400,1536]{1,0:T(8,128)(2,1)} %collective-permute-done.8.refs_3_), channel_id=1, source_target_pairs={{2,3},{6,7},{10,11},{14,15},{18,19},{22,23},{26,27},{30,31}} | collective-permute-start | bytes 3686408 | tf_op jit(solution)/shard_map/ppermute | solution.py:289
  92.8 51.5 %collective-permute-start.12 = (bf16[400,1536]{1,0:T(8,128)(2,1)}, bf16[400,1536]{1,0:T(8,128)(2,1)S(1)}, u32[]{:S(2)}, u32[]{:S(2)}) collective-permute-start(bf16[400,1536]{1,0:T(8,128)(2,1)} %collective-permute-done.11.refs_4_), channel_id=1, source_target_pairs={{1,0},{5,4},{9,8},{13,12},{17,16},{21,20},{25,24},{29,28}} | collective-permute-start | bytes 3686408 | tf_op jit(solution)/shard_map/ppermute | solution.py:289
  94.1 85.4 %collective-permute-start.14 = (bf16[384,1536]{1,0:T(8,128)(2,1)}, bf16[384,1536]{1,0:T(8,128)(2,1)S(1)}, u32[]{:S(2)}, u32[]{:S(2)}) collective-permute-start(bf16[384,1536]{1,0:T(8,128)(2,1)} %collective-permute-done.4), channel_id=1, source_target_pairs={{2,3},{6,7},{10,11},{14,15},{18,19},{22,23},{26,27},{30,31}} | collective-permute-start | bytes 3538952 | tf_op jit(solution)/shard_map/ppermute | solution.py:289
  118.0 61.4 %collective-permute-start.15 = (bf16[384,1536]{1,0:T(8,128)(2,1)}, bf16[384,1536]{1,0:T(8,128)(2,1)S(1)}, u32[]{:S(2)}, u32[]{:S(2)}) collective-permute-start(bf16[384,1536]{1,0:T(8,128)(2,1)} %collective-permute-done.6), channel_id=1, source_target_pairs={{1,0},{5,4},{9,8},{13,12},{17,16},{21,20},{25,24},{29,28}} | collective-permute-start | bytes 3538952 | tf_op jit(solution)/shard_map/ppermute | solution.py:289
  145.2 0.6 copy-start.10
  145.2 0.6 copy-start.12
  145.2 0.6 copy-start.14
  145.8 8.0 %copy-start = (bf16[384,1536]{1,0:T(8,128)(2,1)S(1)}, bf16[384,1536]{1,0:T(8,128)(2,1)}, u32[]{:S(2)}) copy-start(bf16[384,1536]{1,0:T(8,128)(2,1)} %get-tuple-element.39.own_rows) | copy-start | bytes 3538948
  145.8 8.0 %collective-permute-start.13 = (bf16[1536]{0:T(1024)(128)(2,1)S(1)}, bf16[1536]{0:T(1024)(128)(2,1)S(1)}, u32[]{:S(2)}, u32[]{:S(2)}) collective-permute-start(bf16[1536]{0:T(1024)(128)(2,1)S(1)} %divide_convert_fusion.1), channel_id=1, source_target_pairs={{0,4},{8,12},{16,20},{24,28},{1,5},{9,13},{17,21},{25,29},{2,6},{1... | collective-permute-start | bytes 9224 | tf_op jit(solution)/shard_map/ppermute | solution.py:280
  179.3 13.8 %copy-start.4 = (f32[384,1536]{1,0:T(8,128)}, f32[384,1536]{1,0:T(8,128)S(1)}, u32[]{:S(2)}) copy-start(f32[384,1536]{1,0:T(8,128)S(1)} %get-tuple-element.14) | copy-start | bytes 7077892
  179.3 13.8 %copy-start.6 = (f32[8,1536]{1,0:T(8,128)}, f32[8,1536]{1,0:T(8,128)S(1)}, u32[]{:S(2)}) copy-start(f32[8,1536]{1,0:T(8,128)S(1)} %get-tuple-element.20) | copy-start | bytes 147460
  179.3 13.8 %copy-start.7 = (f32[8,1536]{1,0:T(8,128)}, f32[8,1536]{1,0:T(8,128)S(1)}, u32[]{:S(2)}) copy-start(f32[8,1536]{1,0:T(8,128)S(1)} %get-tuple-element.22) | copy-start | bytes 147460
  179.3 13.8 %copy-start.8 = (bf16[384,1536]{1,0:T(8,128)(2,1)}, bf16[384,1536]{1,0:T(8,128)(2,1)S(1)}, u32[]{:S(2)}) copy-start(bf16[384,1536]{1,0:T(8,128)(2,1)S(1)} %get-tuple-element.24) | copy-start | bytes 3538948
  179.5 3.5 %copy-start.1 = (bf16[1536,1536]{1,0:T(8,128)(2,1)S(1)}, bf16[1536,1536]{1,0:T(8,128)(2,1)}, u32[]{:S(2)}) copy-start(bf16[1536,1536]{1,0:T(8,128)(2,1)} %get-tuple-element.16.link_in) | copy-start | bytes 14155780
  183.0 2.3 copy-start.3
  185.3 24.3 %copy-start.11 = (f32[384]{0:T(512)S(1)}, f32[384]{0:T(512)}, u32[]{:S(2)}) copy-start(f32[384]{0:T(512)} %copy-done.10) | copy-start | bytes 4612
  185.3 24.3 %copy-start.13 = (f32[384]{0:T(512)S(1)}, f32[384]{0:T(512)}, u32[]{:S(2)}) copy-start(f32[384]{0:T(512)} %copy-done.12) | copy-start | bytes 4612
  185.3 24.4 %copy-start.15 = (f32[384]{0:T(512)S(1)}, f32[384]{0:T(512)}, u32[]{:S(2)}) copy-start(f32[384]{0:T(512)} %copy-done.14) | copy-start | bytes 4612
  193.1 2.2 copy-start.2
  195.4 20.7 %collective-permute-start.16 = (bf16[1536,1536]{1,0:T(8,128)(2,1)}, bf16[1536,1536]{1,0:T(8,128)(2,1)}, u32[]{:S(2)}, u32[]{:S(2)}) collective-permute-start(bf16[1536,1536]{1,0:T(8,128)(2,1)} %get-tuple-element.19), channel_id=1, source_target_pairs={{0,4},{8,12},{16,20},{24,28},{1,5},{9,13},{17,21},{25,29},{2,6},{1... | collective-permute-start | bytes 14155784 | tf_op jit(solution)/shard_map/ppermute | solution.py:280
  197.8 11.9 %collective-permute-start.17 = (f32[1536]{0:T(1024)S(1)}, f32[1536]{0:T(1024)S(1)}, u32[]{:S(2)}, u32[]{:S(2)}) collective-permute-start(f32[1536]{0:T(1024)S(1)} %dynamic_update_slice.6), channel_id=1, source_target_pairs={{8,4},{16,12},{24,20},{9,5},{17,13},{25,21},{10,6},{18,14},{26,22}... | collective-permute-start | bytes 18440 | tf_op jit(solution)/shard_map/ppermute | solution.py:280
  199.1 17.0 %slice-start = ((s8[4718592]{0:T(1024)(128)(4,1)}), s8[4194304]{0:T(1024)(128)(4,1)S(1)}, s32[]{:S(2)}) async-start(s8[4718592]{0:T(1024)(128)(4,1)} %bitcast.21), calls=%async_computation | async-start | bytes 8388608
  199.9 35.1 %collective-permute-start.19 = (bf16[384,1536]{1,0:T(8,128)(2,1)}, bf16[384,1536]{1,0:T(8,128)(2,1)S(1)}, u32[]{:S(2)}, u32[]{:S(2)}) collective-permute-start(bf16[384,1536]{1,0:T(8,128)(2,1)} %constant_dynamic-update-slice_fusion), channel_id=1, source_target_pairs={{4,0},{8,4},{12,8},{16,12},{20,16},{24,20},{28,24},{5,1},{9,5},{13... | collective-permute-start | bytes 3538952 | tf_op jit(solution)/shard_map/ppermute | solution.py:280
  209.7 6.4 %collective-permute-start.18 = (bf16[1536]{0:T(1024)(128)(2,1)S(1)}, bf16[1536]{0:T(1024)(128)(2,1)S(1)}, u32[]{:S(2)}, u32[]{:S(2)}) collective-permute-start(bf16[1536]{0:T(1024)(128)(2,1)S(1)} %get-tuple-element.29), channel_id=1, source_target_pairs={{4,12},{20,28},{5,13},{21,29},{6,14},{22,30},{7,15},{23,31}} | collective-permute-start | bytes 9224 | tf_op jit(solution)/shard_map/ppermute | solution.py:280
  211.2 4.9 %slice-start.1 = ((s8[4718592]{0:T(1024)(128)(4,1)}), s8[524288]{0:T(1024)(128)(4,1)S(1)}, s32[]{:S(2)}) async-start(s8[4718592]{0:T(1024)(128)(4,1)} %bitcast.21), calls=%async_computation.1 | async-start | bytes 1048576
  225.6 6.3 %collective-permute-start.21 = (bf16[384,1536]{1,0:T(8,128)(2,1)S(1)}, bf16[384,1536]{1,0:T(8,128)(2,1)S(1)}, u32[]{:S(2)}, u32[]{:S(2)}) collective-permute-start(bf16[384,1536]{1,0:T(8,128)(2,1)S(1)} %constant_dynamic-slice_fusion), channel_id=1, source_target_pairs={{20,28},{21,29},{22,30},{23,31}} | collective-permute-start | bytes 3538952 | tf_op jit(solution)/shard_map/ppermute | solution.py:280
  228.4 27.9 %collective-permute-start.20 = (bf16[384,1536]{1,0:T(8,128)(2,1)S(1)}, bf16[384,1536]{1,0:T(8,128)(2,1)S(1)}, u32[]{:S(2)}, u32[]{:S(2)}) collective-permute-start(bf16[384,1536]{1,0:T(8,128)(2,1)S(1)} %convolution_convert_fusion), channel_id=1, source_target_pairs={{20,12},{21,13},{22,14},{23,15}} | collective-permute-start | bytes 3538952 | tf_op jit(solution)/shard_map/ppermute | solution.py:280
  231.9 24.3 %copy-start.5 = (f32[384,1536]{1,0:T(8,128)S(1)}, f32[384,1536]{1,0:T(8,128)}, u32[]{:S(2)}) copy-start(f32[384,1536]{1,0:T(8,128)} %copy-done.4) | copy-start | bytes 7077892

commit v5 on v4

v5 whole, which is shorter than its diff:
```python
import functools

import jax
import jax.numpy as jnp
from jax import lax
from jax.experimental import pallas as pl
from jax.experimental.pallas import tpu as pltpu
from jax.sharding import PartitionSpec as P

BF16 = jnp.bfloat16
F32 = jnp.float32
EXTRA = 16
WIDTH = 256

ANY = pl.BlockSpec(memory_space=pl.ANY)
SHAPE = jax.ShapeDtypeStruct
FREE = pl.CostEstimate(flops=0, bytes_accessed=0, transcendentals=0)


def after(block, *others):
    def body(*refs):
        del refs

    return pl.pallas_call(
        body,
        out_shape=SHAPE(block.shape, block.dtype),
        in_specs=[ANY] * (1 + len(others)),
        out_specs=ANY,
        input_output_aliases={0: 0},
    )(block, *others)


def scaled_by(matrix, factors):
    return (matrix.astype(F32) * factors.astype(F32)[None, :]).astype(BF16)


def row_scaled_by(matrix, factors):
    return (matrix.astype(F32) * factors.astype(F32)[:, None]).astype(BF16)


def dot_nt(left, right):
    return lax.dot_general(left, right, (((1,), (1,)), ((), ())), preferred_element_type=F32)


def dot_nn(left, right):
    return lax.dot_general(left, right, (((1,), (0,)), ((), ())), preferred_element_type=F32)


def dot_tn(left, right):
    return lax.dot_general(left, right, (((0,), (0,)), ((), ())), preferred_element_type=F32)


def rows_of(scale):
    return jnp.broadcast_to(scale[None, :], (8, scale.shape[0]))


def whole_spec(shape):
    return pl.BlockSpec(shape, lambda j, f: (0,) * len(shape))


def along_spec(count):
    return pl.BlockSpec((count, WIDTH), lambda j, f: (0, j))


def down_spec(count):
    return pl.BlockSpec((WIDTH, count), lambda j, f: (j, 0))


def opening_kernel(flags, own, prev, separator, reciprocal, long):
    rows, order = own.shape
    row_ids = lax.broadcasted_iota(jnp.int32, (rows, order), 0) + flags[1] * rows
    col_ids = lax.broadcasted_iota(jnp.int32, (rows, order), 1)
    on_diagonal = jnp.where(row_ids == col_ids, separator[...], 0.0)
    ones = jnp.ones((8, order), BF16)

    def split(value):
        high = value.astype(BF16)
        return high, (value - high.astype(F32)).astype(BF16)

    def form_diagonal(block):
        wide = block.astype(F32)
        high, low = split((wide * reciprocal[0:1]).astype(BF16).astype(F32) * wide)
        return (dot_nt(ones, high) + dot_nt(ones, low))[0:1]

    def placed(words, count):
        ids = lax.broadcasted_iota(jnp.int32, (EXTRA, count), 0)
        total = jnp.zeros((EXTRA, count), F32)
        for at, word in words.items():
            total = jnp.where(ids == at, word.astype(F32), total)
        return total.astype(BF16)

    long[0:rows, :] = prev[...]
    high, low = split(jnp.sum(on_diagonal, axis=0, keepdims=True))
    long[rows:, :] = placed({0: high, 1: low}, order)
    own_high, own_low = split(form_diagonal(own[...]))
    prev_high, prev_low = split(form_diagonal(prev[...]))
    local = placed({2: own_high, 3: own_low, 4: prev_high, 5: prev_low}, rows)
    long[rows:, 0:rows] = long[rows:, 0:rows] + local


def opening(flags, own, prev, separator, reciprocal):
    rows, order = own.shape
    return pl.pallas_call(
        opening_kernel,
        out_shape=SHAPE((rows + EXTRA, order), BF16),
        in_specs=[pl.BlockSpec(memory_space=pltpu.SMEM)] + [pl.BlockSpec(memory_space=pltpu.VMEM)] * 4,
        out_specs=pl.BlockSpec(memory_space=pltpu.VMEM),
        compiler_params=pltpu.CompilerParams(vmem_limit_bytes=32 * 1024 * 1024),
        cost_estimate=FREE,
    )(flags, own, prev, separator, reciprocal)


def early_kernel(size, flags, prev_whole, prev_rows, own_rows, separator, *refs):
    sources = refs[: 2 * size - 1]
    link, partial, form, own_out, own, sems = refs[2 * size - 1 :]
    rows = separator.shape[0]
    step = pl.program_id(0)
    here = pl.ds(pl.multiple_of(step * WIDTH, WIDTH), WIDTH)

    def copies():
        for spot in range(size):
            for by, source in enumerate(sources):
                distance = (by + 1) // 2 if by % 2 else -(by // 2)
                target = own.at[pl.ds(spot * rows, rows)]
                copy = pltpu.make_async_copy(source, target, sems.at[spot])
                yield flags[1] - spot == distance, copy

    @pl.when(step == 0)
    def _():
        for chosen, copy in copies():
            pl.when(chosen)(copy.start)
        for chosen, copy in copies():
            pl.when(chosen)(copy.wait)
        pltpu.make_async_copy(own, own_out, sems.at[size]).start()

    block = own[here, :]
    link[...] = jnp.where(flags[0] == 1, 0.0, -dot_nt(prev_whole[...], block)).astype(BF16)
    partial[...] = separator[...] - dot_nt(own_rows[...], block)
    form[...] = dot_nt(prev_rows[...], prev_whole[here, :])

    @pl.when(step == pl.num_programs(0) - 1)
    def _():
        pltpu.make_async_copy(own, own_out, sems.at[size]).wait()


def early_forms(flags, prev_whole, prev_rows, own_rows, separator, sources):
    rows, order = own_rows.shape
    size = order // rows
    return pl.pallas_call(
        functools.partial(early_kernel, size),
        out_shape=[
            SHAPE((order, order), BF16),
            SHAPE((rows, order), F32),
            SHAPE((rows, order), F32),
            SHAPE((order, order), BF16),
        ],
        grid_spec=pltpu.PrefetchScalarGridSpec(
            num_scalar_prefetch=1,
            grid=(order // WIDTH,),
            in_specs=[
                whole_spec((order, order)),
                whole_spec((rows, order)),
                whole_spec((rows, order)),
                along_spec(rows),
            ]
            + [ANY] * len(sources),
            out_specs=[along_spec(order), along_spec(rows), along_spec(rows), ANY],
            scratch_shapes=[pltpu.VMEM((order, order), BF16), pltpu.SemaphoreType.DMA((size + 1,))],
        ),
        compiler_params=pltpu.CompilerParams(vmem_limit_bytes=32 * 1024 * 1024),
        cost_estimate=FREE,
    )(flags, prev_whole, prev_rows, own_rows, separator, *sources)


def late_kernel(
    size, flags, reciprocal, prev_rows, own, from_below, from_above, far, link, corner, raw, scaled, sem
):
    place = flags[1]
    rows = raw.shape[0]
    step = pl.program_id(0)
    width = own.shape[0]
    here = pl.ds(pl.multiple_of(step * width, width), width)

    @pl.when(step == 0)
    def _():
        for chosen, source in (
            (place == 0, from_above.at[pl.ds(0, rows)]),
            (place == size - 1, from_below.at[pl.ds(0, rows)]),
            (jnp.logical_and(place != 0, place != size - 1), far),
        ):
            copy = pltpu.make_async_copy(source, raw, sem)
            pl.when(chosen)(copy.start)
            pl.when(chosen)(copy.wait)
        scaled[...] = (raw[...].astype(F32) * reciprocal[0:1]).astype(BF16)
        corner[...] = dot_nt(prev_rows[...], scaled[...])

    link[:, here] = jnp.where(flags[0] == 1, 0.0, -dot_nt(scaled[...], own[...])).astype(BF16)


def late_forms(flags, reciprocal, prev_rows, own, from_below, from_above, far):
    rows, order = prev_rows.shape
    size = order // rows
    width = 512
    return pl.pallas_call(
        functools.partial(late_kernel, size),
        out_shape=[SHAPE((rows, order), BF16), SHAPE((rows, rows), F32)],
        grid_spec=pltpu.PrefetchScalarGridSpec(
            num_scalar_prefetch=1,
            grid=(order // width,),
            in_specs=[
                whole_spec((8, order)),
                whole_spec((rows, order)),
                pl.BlockSpec((width, order), lambda j, f: (j, 0)),
                ANY,
                ANY,
                ANY,
            ],
            out_specs=[whole_spec((rows, order)), whole_spec((rows, rows))],
            scratch_shapes=[
                pltpu.VMEM((rows, order), BF16),
                pltpu.VMEM((rows, order), BF16),
                pltpu.SemaphoreType.DMA,
            ],
        ),
        compiler_params=pltpu.CompilerParams(vmem_limit_bytes=20 * 1024 * 1024),
    )(flags, reciprocal, prev_rows, own, from_below, from_above, far)


def on_device(sep_block, own_couple, prev_couple, inner_diag):
    separator = sep_block[0]
    own_rows = own_couple[0]
    prev_rows = prev_couple[0]
    reciprocal = 1.0 / inner_diag[0]
    rows, order = own_rows.shape
    place = lax.axis_index("space")
    size = lax.axis_size("space")
    row_start = place * rows
    partition = lax.axis_index("tm")
    parts = lax.axis_size("tm")

    def between(block, route):
        return lax.ppermute(block, "tm", [(a, b) for a, b in route if 0 <= b < parts])

    even = range(0, parts, 2)
    pivots = range(1, parts, 4)
    everyone = range(parts)

    def one_step(ahead, back, step):
        up = [(j, j + 1) for j in range(step - 1, size - 1)]
        down = [(j, j - 1) for j in range(1, size - step + 1)]
        return lax.ppermute(ahead, "space", up), lax.ppermute(back, "space", down)

    def block_at(arrived, spot):
        block = arrived[0][0]
        for step in range(1, len(arrived)):
            if spot + step < size:
                block = jnp.where(place == spot + step, arrived[step][0], block)
            if spot - step >= 0:
                block = jnp.where(place == spot - step, arrived[step][1], block)
        return block

    own_arrived = [(own_rows, own_rows)]
    own_arrived.append(one_step(own_rows, own_rows, 1))

    is_first = partition == 0
    flags = jnp.stack([is_first.astype(jnp.int32), place])
    prev_long = opening(flags, own_rows, prev_rows, separator, rows_of(reciprocal))
    long_arrived = [(prev_long, prev_long)]
    long_arrived.append(one_step(prev_long, prev_long, 1))
    for step in range(2, size):
        own_arrived.append(one_step(*own_arrived[-1], step))
        long_arrived.append(one_step(*long_arrived[-1], step))

    left_side = place < size // 2
    late_start = jnp.where(left_side, size - 1, 0) * rows
    is_end = jnp.logical_or(place == 0, place == size - 1)
    prev_arrived = [tuple(block[:rows] for block in pair) for pair in long_arrived[:-1]]
    words_arrived = [tuple(block[rows:] for block in pair) for pair in long_arrived[:-1]]
    prev_blocks = [block_at(prev_arrived, spot) for spot in range(size)]
    zero = jnp.zeros_like(prev_rows)
    prev_blocks[0] = jnp.where(place == size - 1, zero, prev_blocks[0])
    prev_blocks[-1] = jnp.where(place == 0, zero, prev_blocks[-1])
    prev_first = jnp.concatenate(prev_blocks)
    prev_far = jnp.where(left_side, prev_blocks[-1], prev_blocks[0])
    words = [block_at(words_arrived, spot) for spot in range(size)]
    none = jnp.zeros_like(words[0])
    words[0] = jnp.where(place == size - 1, none, words[0])
    words[-1] = jnp.where(place == 0, none, words[-1])

    def pair_sum(block, at):
        return block[at].astype(F32) + block[at + 1].astype(F32)

    sep_diag = sum(pair_sum(block, 0) for block in words)
    own_diag = jnp.concatenate([pair_sum(block, 2)[:rows] for block in words])
    prev_diag = jnp.concatenate([pair_sum(block, 4)[:rows] for block in words])
    prev_first, prev_far, sep_diag, own_diag, prev_diag = lax.optimization_barrier(
        (prev_first, prev_far, sep_diag, own_diag, prev_diag)
    )

    is_pivot = partition % 2 == 0
    is_receiver = partition % 2 == 1
    own_scaled = scaled_by(own_rows, reciprocal)
    sources = [own_rows]
    for up, down in own_arrived[1:]:
        sources += [up, down]
    link, partial, prev_form, own_full = early_forms(
        flags, scaled_by(prev_first, reciprocal), prev_rows, own_scaled, separator, sources
    )

    from_below, from_above = long_arrived[-1]
    late, corner = late_forms(
        flags, rows_of(reciprocal), prev_rows, own_full, from_below, from_above, prev_far
    )
    link = lax.dynamic_update_slice_in_dim(link, late, late_start, 0)
    pivot_link = between(link, [(p, p + 1) for p in even])
    end_words = jnp.where(left_side, from_above[rows:], from_below[rows:])
    end_words = jnp.where(is_end, end_words, jnp.zeros_like(end_words))
    sep_diag = sep_diag + pair_sum(end_words, 0)
    own_diag = own_diag + lax.dynamic_update_slice_in_dim(
        jnp.zeros_like(own_diag), pair_sum(end_words, 2)[:rows], late_start, 0
    )
    prev_diag = prev_diag + lax.dynamic_update_slice_in_dim(
        jnp.zeros_like(prev_diag), pair_sum(end_words, 4)[:rows], late_start, 0
    )
    diag = sep_diag - own_diag - between(prev_diag, [(p, p - 1) for p in everyone])
    scale = (1.0 / jnp.maximum(diag, 1.0)).astype(BF16)
    pivot_scale = between(scale, [(p, p + 1) for p in even])

    link_rows = lax.dynamic_slice_in_dim(link, row_start, rows, 0)
    left_form = dot_nt(scaled_by(link_rows, scale), link)
    prev_form = lax.dynamic_update_slice_in_dim(prev_form, corner, late_start, 1)
    to_earlier = jnp.where(is_pivot, prev_form + left_form, prev_form).astype(BF16)
    from_even = between(to_earlier, [(p, p - 1) for p in even])
    from_odd = between(to_earlier, [(p, p - 1) for p in range(1, parts, 2)])
    left_diag = between(dot_nt(rows_of(scale), link * link)[0], [(p, p - 1) for p in even])
    right_diag = dot_nn(rows_of(pivot_scale), link * link)[0]

    pivot_rows = lax.dynamic_slice_in_dim(pivot_link, row_start, rows, 0)
    next_rows = (-dot_nn(scaled_by(pivot_rows, pivot_scale), link)).astype(BF16)
    pivot_rows = between(next_rows, [(p, p + 2) for p in pivots if p != 1])
    next_link = (-dot_nn(scaled_by(pivot_link, after(pivot_scale, next_rows)), link)).astype(BF16)

    next_diag = diag - left_diag - right_diag
    next_scale = (1.0 / jnp.maximum(next_diag, 1.0)).astype(BF16)
    next_pivot_scale = between(next_scale, [(p, p + 2) for p in pivots])
    left_next = dot_nt(scaled_by(next_rows, next_scale), next_link).astype(BF16)
    from_pivot = between(left_next, [(p, p - 2) for p in pivots])

    link_cols = lax.dynamic_slice_in_dim(link, row_start, rows, 1)
    right_form = dot_tn(row_scaled_by(link_cols, pivot_scale), link)

    is_last = partition % 4 == 3
    next_cols = lax.dynamic_slice_in_dim(next_link, row_start, rows, 1)
    right_next = dot_tn(row_scaled_by(next_cols, next_pivot_scale), next_link)
    last_rows = (-dot_nn(scaled_by(pivot_rows, next_pivot_scale), next_link)).astype(BF16)
    out_link = jnp.where(is_last, last_rows, jnp.where(is_receiver, next_rows, link_rows))
    updates = jnp.where(is_last, right_form + right_next, jnp.where(is_receiver, right_form, 0.0))
    updates = lax.optimization_barrier(updates)
    schur = partial - updates - (from_even + from_odd).astype(F32) - from_pivot.astype(F32)
    return (schur[None], out_link[None])


def solution(mesh):
    placed = (P("tm", "space", None), P("tm", "space", None), P("tm", "space", None), P("tm", None))
    return jax.shard_map(
        on_device,
        mesh=mesh,
        in_specs=placed,
        out_specs=(P("tm", "space", None), P("tm", "space", None)),
        check_vma=False,
    )
```

time: 260 us -> 270 us (1.038)
  matrix products: 21.5 us -> 43.9 us
  other arithmetic: 23.1 us -> 15.6 us
  Pallas kernels: 33.2 us -> 25.9 us
  waiting for transfers between devices: 122 us -> 128 us
    ppermute x14 -> x12, waiting for transfers between devices: 95.7 us -> 113 us  [one_step(): return (lax.ppermute(ahead, 'space', up), lax.ppermute(back, 'space', down))]
    ppermute x8 -> x9, waiting for transfers between devices: 26.4 us -> 14.9 us  [between(): lax.ppermute(block, 'tm', [(a, b) for a, b in route if 0 <= b < parts])]
    dot_general x2 -> x4, matrix products: 12.4 us -> 23.3 us  [dot_nn(): lax.dot_general(left, right, (((1,), (0,)), ((), ())), preferred_element_...]
    dot_general x1 -> x3, matrix products: 2.02 us -> 12.2 us  [dot_nt(): lax.dot_general(left, right, (((1,), (1,)), ((), ())), preferred_element_...]
    pallas_call x1, Pallas kernels: 25.5 us -> 19.2 us  [early_forms(): pl.pallas_call(functools.partial(early_kernel, size), out_shape=[SHAPE((o...]
    reduce_sum x2 -> x0, other arithmetic: 5.02 us -> none  [the longest x1 2.97 us: on_device(): own_sum = jnp.sum(own_scaled.astype(F32) * own_rows.astype(F32), axis=1)]
    ppermute x14 -> x12, starting transfers between devices: 25.9 us -> 22.1 us  [one_step(): return (lax.ppermute(ahead, 'space', up), lax.ppermute(back, 'space', down))]
    concatenate x2, other arithmetic: 3.83 us -> 0.61 us  [the longest x1 0.6 us: on_device(): prev_diag = jnp.concatenate([pair_sum(block, 4)[:rows] for block in words])]
  transfers between devices with their start and end apart: 22 -> 21, of which waited for: 10 -> 10; matrix products, arithmetic and copies ran while one was open for 17% -> 21% of each run, Pallas kernels for 10% -> 7%
where the time goes in v5:
time: 270 us; the launch traced here: 269 us
  waiting for transfers between devices  128 us (47%)
  matrix products  43.9 us (16%)
  starting transfers between devices  43.8 us (16%)
  Pallas kernels  25.9 us (10%)
  other arithmetic  15.6 us (6%)
  local copies, waits for them, and re-layouts  10.6 us (4%)
    ppermute x12, waiting for transfers between devices, one_step(): return (lax.ppermute(ahead, 'space', up), lax.ppermute(back, 'space', down))  113 us
    dot_general x4, matrix products, dot_nn(): lax.dot_general(left, right, (((1,), (0,)), ((), ())), preferred_element_...  23.3 us
    ppermute x12, starting transfers between devices, one_step(): return (lax.ppermute(ahead, 'space', up), lax.ppermute(back, 'space', down))  22.1 us
    ppermute x9, starting transfers between devices, between(): lax.ppermute(block, 'tm', [(a, b) for a, b in route if 0 <= b < parts])  21.7 us
    pallas_call x1, Pallas kernels, early_forms(): pl.pallas_call(functools.partial(early_kernel, size), out_shape=[SHAPE((o...  19.2 us
    ppermute x9, waiting for transfers between devices, between(): lax.ppermute(block, 'tm', [(a, b) for a, b in route if 0 <= b < parts])  14.9 us
    dot_general x3, matrix products, dot_nt(): lax.dot_general(left, right, (((1,), (1,)), ((), ())), preferred_element_...  12.2 us
    unnamed x36, local copies, waits for them, and re-layouts  8.44 us
  transfers between devices with their start and end apart: 21, of which 10 were waited for; matrix products, arithmetic and copies ran while one was open for 21% of the time, Pallas kernels for 7%

profile of v5, /device:TPU:3, one launch (start us, length us, event | category | flops | bytes accessed | tf_op | source)
XLA Modules:
  0.0 268.5 jit_solution(2400155813534161577)
XLA Ops:
  0.6 0.7 divide_reduce_fusion
  1.4 0.1 pad_add_fusion.flags
  1.4 1.3 copy-done
  2.7 1.3 copy-done.2
  4.0 1.7 copy-done.4
  5.7 2.6 shard_map.59
  8.2 4.2 %collective-permute-start = (bf16[400,1536]{1,0:T(8,128)(2,1)S(1)}, bf16[400,1536]{1,0:T(8,128)(2,1)}, u32[]{:S(2)}, u32[]{:S(2)}) collective-permute-start(bf16[400,1536]{1,0:T(8,128)(2,1)S(1)} %shard_map.59), channel_id=1, source_target_pairs={{0,1},{1,2},{2,3},{4,5},{5,6},{6,7},{8,9},{9,10},{10,11},{12,13},{... | collective-permute-start | bytes 3686408 | tf_op jit(solution)/shard_map/ppermute | solution.py:251
  12.5 1.3 collective-permute-start.2
  13.8 5.0 %collective-permute-start.4 = (bf16[384,1536]{1,0:T(8,128)(2,1)S(1)}, bf16[384,1536]{1,0:T(8,128)(2,1)}, u32[]{:S(2)}, u32[]{:S(2)}) collective-permute-start(bf16[384,1536]{1,0:T(8,128)(2,1)S(1)} %bitcast.23), channel_id=1, source_target_pairs={{0,1},{1,2},{2,3},{4,5},{5,6},{6,7},{8,9},{9,10},{10,11},{12,13},{... | collective-permute-start | bytes 3538952 | tf_op jit(solution)/shard_map/ppermute | solution.py:251
  18.8 1.3 collective-permute-start.5
  20.1 17.0 %collective-permute-done = bf16[400,1536]{1,0:T(8,128)(2,1)} collective-permute-done((bf16[400,1536]{1,0:T(8,128)(2,1)S(1)}, bf16[400,1536]{1,0:T(8,128)(2,1)}, u32[]{:S(2)}, u32[]{:S(2)}) %collective-permute-start) | collective-permute-done | bytes 1228832 | tf_op jit(solution)/shard_map/ppermute | solution.py:251
  37.1 1.7 collective-permute-start.1
  38.9 3.2 %collective-permute-done.2 = bf16[400,1536]{1,0:T(8,128)(2,1)} collective-permute-done((bf16[400,1536]{1,0:T(8,128)(2,1)S(1)}, bf16[400,1536]{1,0:T(8,128)(2,1)}, u32[]{:S(2)}, u32[]{:S(2)}) %collective-permute-start.2) | collective-permute-done | bytes 1228832 | tf_op jit(solution)/shard_map/ppermute | solution.py:251
  42.1 1.3 collective-permute-start.3
  43.3 19.1 %collective-permute-done.4.refs_1_ = bf16[384,1536]{1,0:T(8,128)(2,1)} collective-permute-done((bf16[384,1536]{1,0:T(8,128)(2,1)S(1)}, bf16[384,1536]{1,0:T(8,128)(2,1)}, u32[]{:S(2)}, u32[]{:S(2)}) %collective-permute-start.4) | collective-permute-done | bytes 1179680 | tf_op jit(solution)/shard_map/ppermute | solution.py:251
  62.4 1.7 collective-permute-start.6
  64.1 3.3 %collective-permute-done.5.refs_2_ = bf16[384,1536]{1,0:T(8,128)(2,1)} collective-permute-done((bf16[384,1536]{1,0:T(8,128)(2,1)S(1)}, bf16[384,1536]{1,0:T(8,128)(2,1)}, u32[]{:S(2)}, u32[]{:S(2)}) %collective-permute-start.5) | collective-permute-done | bytes 1179680 | tf_op jit(solution)/shard_map/ppermute | solution.py:251
  67.3 1.3 collective-permute-start.7
  68.7 0.2 multiply_convert_fusion.9.own_rows
  68.9 0.7 collective-permute-start.8
  69.6 49.3 %collective-permute-done.7.refs_4_ = bf16[384,1536]{1,0:T(8,128)(2,1)} collective-permute-done((bf16[384,1536]{1,0:T(8,128)(2,1)}, bf16[384,1536]{1,0:T(8,128)(2,1)}, u32[]{:S(2)}, u32[]{:S(2)}) %collective-permute-start.7) | collective-permute-done | bytes 1179680 | tf_op jit(solution)/shard_map/ppermute | solution.py:251
  119.0 1.3 collective-permute-start.9
  120.3 0.9 select_select_fusion.8
  121.2 0.6 fusion.37
  122.1 2.6 broadcast_select_fusion
  124.7 0.4 pad_maximum_fusion
  125.1 0.6 pad_maximum_fusion.2
  125.7 0.9 collective-permute-start.10
  126.6 1.4 collective-permute-start.11
  128.0 3.4 %multiply_convert_fusion.1.prev_whole = bf16[1536,1536]{1,0:T(8,128)(2,1)} fusion(bf16[1536,1536]{1,0:T(8,128)(2,1)S(1)} %pad_maximum_fusion, f32[1536]{0:T(1024)S(1)} %divide_reduce_fusion), kind=kLoop, calls=%fused_computation.2 | loop fusion | flops 7077888 | bytes 9443328 | tf_op jit(solution)/shard_map/convert_element_type | solution.py:34
  131.4 15.2 %collective-permute-done.9.refs_6_ = bf16[384,1536]{1,0:T(8,128)(2,1)S(1)} collective-permute-done((bf16[384,1536]{1,0:T(8,128)(2,1)}, bf16[384,1536]{1,0:T(8,128)(2,1)S(1)}, u32[]{:S(2)}, u32[]{:S(2)}) %collective-permute-start.9) | collective-permute-done | bytes 1179680 | tf_op jit(solution)/shard_map/ppermute | solution.py:251
  146.6 19.2 %shard_map.60 = (bf16[1536,1536]{1,0:T(8,128)(2,1)}, f32[384,1536]{1,0:T(8,128)S(1)}, f32[384,1536]{1,0:T(8,128)S(1)}, bf16[1536,1536]{1,0:T(8,128)(2,1)}) custom-call(s32[2]{0:T(128)S(1)} %pad_add_fusion.flags, bf16[1536,1536]{1,0:T(8,128)(2,1)} %multiply_convert_fusion.1.prev_whole, bf16[384,1536]{1,0:T(8,128)(2,1)S(1)} %bitcast.20, ...), custom_call_target="tpu_custom_call" | custom-call | tf_op jit(solution)/shard_map/pallas_call | solution.py:149
  165.9 1.4 copy-done.11
  167.3 5.7 %collective-permute-done.11.from_above = bf16[400,1536]{1,0:T(8,128)(2,1)S(1)} collective-permute-done((bf16[400,1536]{1,0:T(8,128)(2,1)}, bf16[400,1536]{1,0:T(8,128)(2,1)S(1)}, u32[]{:S(2)}, u32[]{:S(2)}) %collective-permute-start.11) | collective-permute-done | bytes 1228832 | tf_op jit(solution)/shard_map/ppermute | solution.py:251
  173.0 2.8 %copy-done.6 = bf16[1536,1536]{1,0:T(8,128)(2,1)S(1)} copy-done((bf16[1536,1536]{1,0:T(8,128)(2,1)S(1)}, bf16[1536,1536]{1,0:T(8,128)(2,1)}, u32[]{:S(2)}) %copy-start.6) | copy-done | bytes 4718616
  175.8 4.1 %shard_map.61 = (bf16[384,1536]{1,0:T(8,128)(2,1)S(1)}, f32[384,384]{1,0:T(8,128)S(1)}) custom-call(s32[2]{0:T(128)S(1)} %pad_add_fusion.flags, f32[8,1536]{1,0:T(8,128)S(1)} %copy-done.10, bf16[384,1536]{1,0:T(8,128)(2,1)S(1)} %bitcast.21, bf16[1536,1536]{1,0:T(8,128)(2,1)S(1)} %copy-done.6, bf16[400,1536]{1,0:T(8,128)(2,1)S(1)} %collective-permute-done.10.from_below, ...), custom_call_target="tpu_custom_call" | custom-call | tf_op jit(solution)/shard_map/pallas_call | solution.py:204
  179.9 1.2 constant_dynamic-update-slice_fusion.1
  181.1 1.3 collective-permute-start.14
  182.4 0.8 fusion.27
  183.3 0.2 add_dynamic-update-slice_fusion
  183.5 6.8 %collective-permute-start.12 = (f32[1536]{0:T(1024)S(1)}, f32[1536]{0:T(1024)S(1)}, u32[]{:S(2)}, u32[]{:S(2)}) collective-permute-start(f32[1536]{0:T(1024)S(1)} %add_dynamic-update-slice_fusion), channel_id=1, source_target_pairs={{4,0},{8,4},{12,8},{16,12},{20,16},{24,20},{28,24},{5,1},{9,5},{13... | collective-permute-start | bytes 18440 | tf_op jit(solution)/shard_map/ppermute | solution.py:242
  190.3 0.9 constant_dynamic-update-slice_fusion
  191.1 0.2 add_dynamic-update-slice_fusion.1
  191.3 1.4 collective-permute-done.12
  192.7 1.3 collective-permute-start.13
  194.0 6.5 %fusion.7 = bf16[384,1536]{1,0:T(8,128)(2,1)} fusion(f32[384,1536]{1,0:T(8,128)} %constant_dynamic-update-slice_fusion, bf16[1536,1536]{1,0:T(8,128)(2,1)} %constant_dynamic-update-slice_fusion.1, f32[1536]{0:T(1024)S(1)} %get-tuple-element.24, pred[]{:T(512)S(6)} %eq.26, s32[]{:T(128)S(6)} %select_n.231), kind=kOutput, calls=%fused_computation.16 | convolution fusion | flops 1815478272 | bytes 9443333 | tf_op jit(solution)/shard_map/dot_general | solution.py:42
  200.5 1.3 collective-permute-start.17
  201.8 5.2 %collective-permute-start.18 = (bf16[384,1536]{1,0:T(8,128)(2,1)}, bf16[384,1536]{1,0:T(8,128)(2,1)}, u32[]{:S(2)}, u32[]{:S(2)}) collective-permute-start(bf16[384,1536]{1,0:T(8,128)(2,1)} %fusion.7), channel_id=1, source_target_pairs={{4,0},{12,8},{20,16},{28,24},{5,1},{13,9},{21,17},{29,25},{6,2},{1... | collective-permute-start | bytes 3538952 | tf_op jit(solution)/shard_map/ppermute | solution.py:242
  207.0 3.7 %fusion.20 = f32[1536]{0:T(1024)S(1)} fusion(bf16[1,1536]{1,0:T(2,128)(2,1)S(1)} %reshape.87, bf16[1536,1536]{1,0:T(8,128)(2,1)} %constant_dynamic-update-slice_fusion.1), kind=kOutput, calls=%fused_computation.43 | convolution fusion | flops 7077888 | bytes 4727808 | tf_op jit(solution)/shard_map/dot_general | solution.py:42
  210.7 1.3 collective-permute-start.15
  212.0 3.1 %fusion.23 = f32[1536]{0:T(1024)S(1)} fusion(bf16[1,1536]{1,0:T(2,128)(2,1)S(1)} %reshape.88, bf16[1536,1536]{1,0:T(8,128)(2,1)} %constant_dynamic-update-slice_fusion.1), kind=kOutput, calls=%fused_computation.44 | convolution fusion | flops 7077888 | bytes 4727808 | tf_op jit(solution)/shard_map/dot_general | solution.py:46
  215.1 4.1 %collective-permute-done.15 = f32[1536]{0:T(1024)S(1)} collective-permute-done((f32[1536]{0:T(1024)S(1)}, f32[1536]{0:T(1024)S(1)}, u32[]{:S(2)}, u32[]{:S(2)}) %collective-permute-start.15) | collective-permute-done | bytes 6176 | tf_op jit(solution)/shard_map/ppermute | solution.py:242
  219.2 1.3 collective-permute-start.16
  220.5 6.2 %fusion.8 = f32[384,1536]{1,0:T(8,128)} fusion(bf16[1536,1536]{1,0:T(8,128)(2,1)} %constant_dynamic-update-slice_fusion.1, f32[1536]{0:T(1024)S(1)} %convert_element_type.255, s32[]{:T(128)S(6)} %select_n.231), kind=kOutput, calls=%fused_computation.26 | convolution fusion | flops 1813708800 | bytes 8263684 | tf_op jit(solution)/shard_map/dot_general | solution.py:50
  226.8 4.7 %fusion.5.refs_1_ = bf16[384,1536]{1,0:T(8,128)(2,1)S(1)} fusion(bf16[1536,1536]{1,0:T(8,128)(2,1)} %constant_dynamic-update-slice_fusion.1, f32[1536]{0:T(1024)S(1)} %convert_element_type.255, bf16[1536,1536]{1,0:T(8,128)(2,1)} %collective-permute-done.14, s32[]{:T(128)S(6)} %select_n.231), kind=kOutput, calls=%fused_computation.13 | convolution fusion | flops 1814888448 | bytes 7084036 | tf_op jit(solution)/shard_map/dot_general | solution.py:46
  231.5 1.7 collective-permute-start.20
  233.2 0.7 convert_element_type.261
  233.9 10.8 %negate_convert_fusion = bf16[1536,1536]{1,0:T(8,128)(2,1)S(1)} fusion(bf16[1536,1536]{1,0:T(8,128)(2,1)} %constant_dynamic-update-slice_fusion.1, bf16[1536,1536]{1,0:T(8,128)(2,1)} %collective-permute-done.14, f32[1536]{0:T(1024)S(1)} %convert_element_type.261), kind=kOutput, calls=%fused_computation | convolution fusion | flops 7259553792 | bytes 14161920 | tf_op jit(solution)/shard_map/dot_general | solution.py:46
  244.7 2.0 convolution_convert_fusion
  246.8 1.5 collective-permute-start.19
  248.3 2.2 select_select_fusion
  250.5 4.7 %fusion.10 = bf16[1,384,1536]{2,1,0:T(8,128)(2,1)} fusion(bf16[1536,1536]{1,0:T(8,128)(2,1)S(1)} %negate_convert_fusion, bf16[384,1536]{1,0:T(8,128)(2,1)} %collective-permute-done.20, bf16[384,1536]{1,0:T(8,128)(2,1)S(1)} %copy-done.13, f32[1536]{0:T(1024)S(1)} %convert_element_type.266, pred[]{:T(512)S(6)} %eq.25, pred[]{:T(512)S(6)} %eq.24, ...), kind=kOutput, calls=%fused_computation.28 | convolution fusion | flops 1816068096 | bytes 9443334 | tf_op jit(solution)/shard_map/dot_general | solution.py:46
  255.2 9.4 %collective-permute-done.19 = bf16[384,1536]{1,0:T(8,128)(2,1)S(1)} collective-permute-done((bf16[384,1536]{1,0:T(8,128)(2,1)S(1)}, bf16[384,1536]{1,0:T(8,128)(2,1)S(1)}, u32[]{:S(2)}, u32[]{:S(2)}) %collective-permute-start.19) | collective-permute-done | bytes 1179680 | tf_op jit(solution)/shard_map/ppermute | solution.py:242
  264.6 3.9 %subtract_bitcast_fusion = f32[1,384,1536]{2,1,0:T(8,128)} fusion(bf16[384,1536]{1,0:T(8,128)(2,1)S(1)} %collective-permute-done.19, f32[384,1536]{1,0:T(8,128)S(1)} %get-tuple-element.14, f32[384,1536]{1,0:T(8,128)S(1)} %select_select_fusion, bf16[384,1536]{1,0:T(8,128)(2,1)} %collective-permute-done.17, bf16[384,1536]{1,0:T(8,128)(2,1)} %collective-permute-done.18), kind=kLoop, calls=%fused_computation.18 | loop fusion | flops 3538944 | bytes 10616832 | tf_op jit(solution)/shard_map/broadcast_in_dim | solution.py:360
  (65 shorter events, 0.5 us)
Async XLA Ops:
  1.4 1.3 copy-start
  2.7 1.3 copy-start.2
  4.0 1.7 copy-start.4
  5.7 2.6 copy-start.9
  5.7 63.0 %copy-start.3 = (bf16[1,384,1536]{2,1,0:T(8,128)(2,1)S(1)}, bf16[1,384,1536]{2,1,0:T(8,128)(2,1)}, u32[]{:S(2)}) copy-start(bf16[1,384,1536]{2,1,0:T(8,128)(2,1)} %param.5) | copy-start | bytes 3538948
  8.2 28.9 %collective-permute-start = (bf16[400,1536]{1,0:T(8,128)(2,1)S(1)}, bf16[400,1536]{1,0:T(8,128)(2,1)}, u32[]{:S(2)}, u32[]{:S(2)}) collective-permute-start(bf16[400,1536]{1,0:T(8,128)(2,1)S(1)} %shard_map.59), channel_id=1, source_target_pairs={{0,1},{1,2},{2,3},{4,5},{5,6},{6,7},{8,9},{9,10},{10,11},{12,13},{... | collective-permute-start | bytes 3686408 | tf_op jit(solution)/shard_map/ppermute | solution.py:251
  12.5 29.6 %collective-permute-start.2 = (bf16[400,1536]{1,0:T(8,128)(2,1)S(1)}, bf16[400,1536]{1,0:T(8,128)(2,1)}, u32[]{:S(2)}, u32[]{:S(2)}) collective-permute-start(bf16[400,1536]{1,0:T(8,128)(2,1)S(1)} %shard_map.59), channel_id=1, source_target_pairs={{1,0},{2,1},{3,2},{5,4},{6,5},{7,6},{9,8},{10,9},{11,10},{13,12},{... | collective-permute-start | bytes 3686408 | tf_op jit(solution)/shard_map/ppermute | solution.py:251
  13.8 48.6 %collective-permute-start.4 = (bf16[384,1536]{1,0:T(8,128)(2,1)S(1)}, bf16[384,1536]{1,0:T(8,128)(2,1)}, u32[]{:S(2)}, u32[]{:S(2)}) collective-permute-start(bf16[384,1536]{1,0:T(8,128)(2,1)S(1)} %bitcast.23), channel_id=1, source_target_pairs={{0,1},{1,2},{2,3},{4,5},{5,6},{6,7},{8,9},{9,10},{10,11},{12,13},{... | collective-permute-start | bytes 3538952 | tf_op jit(solution)/shard_map/ppermute | solution.py:251
  18.8 48.5 %collective-permute-start.5 = (bf16[384,1536]{1,0:T(8,128)(2,1)S(1)}, bf16[384,1536]{1,0:T(8,128)(2,1)}, u32[]{:S(2)}, u32[]{:S(2)}) collective-permute-start(bf16[384,1536]{1,0:T(8,128)(2,1)S(1)} %bitcast.24), channel_id=1, source_target_pairs={{1,0},{2,1},{3,2},{5,4},{6,5},{7,6},{9,8},{10,9},{11,10},{13,12},{... | collective-permute-start | bytes 3538952 | tf_op jit(solution)/shard_map/ppermute | solution.py:251
  37.1 83.1 %collective-permute-start.1 = (bf16[400,1536]{1,0:T(8,128)(2,1)}, bf16[400,1536]{1,0:T(8,128)(2,1)}, u32[]{:S(2)}, u32[]{:S(2)}) collective-permute-start(bf16[400,1536]{1,0:T(8,128)(2,1)} %collective-permute-done), channel_id=1, source_target_pairs={{1,2},{2,3},{5,6},{6,7},{9,10},{10,11},{13,14},{14,15},{17,18},{18... | collective-permute-start | bytes 3686408 | tf_op jit(solution)/shard_map/ppermute | solution.py:251
  42.1 78.2 %collective-permute-start.3 = (bf16[400,1536]{1,0:T(8,128)(2,1)}, bf16[400,1536]{1,0:T(8,128)(2,1)}, u32[]{:S(2)}, u32[]{:S(2)}) collective-permute-start(bf16[400,1536]{1,0:T(8,128)(2,1)} %collective-permute-done.2), channel_id=1, source_target_pairs={{1,0},{2,1},{5,4},{6,5},{9,8},{10,9},{13,12},{14,13},{17,16},{18,1... | collective-permute-start | bytes 3686408 | tf_op jit(solution)/shard_map/ppermute | solution.py:251
  62.4 6.5 %collective-permute-start.6 = (bf16[384,1536]{1,0:T(8,128)(2,1)}, bf16[384,1536]{1,0:T(8,128)(2,1)}, u32[]{:S(2)}, u32[]{:S(2)}) collective-permute-start(bf16[384,1536]{1,0:T(8,128)(2,1)} %collective-permute-done.4.refs_1_), channel_id=1, source_target_pairs={{1,2},{2,3},{5,6},{6,7},{9,10},{10,11},{13,14},{14,15},{17,18},{18... | collective-permute-start | bytes 3538952 | tf_op jit(solution)/shard_map/ppermute | solution.py:251
  67.3 51.6 %collective-permute-start.7 = (bf16[384,1536]{1,0:T(8,128)(2,1)}, bf16[384,1536]{1,0:T(8,128)(2,1)}, u32[]{:S(2)}, u32[]{:S(2)}) collective-permute-start(bf16[384,1536]{1,0:T(8,128)(2,1)} %collective-permute-done.5.refs_2_), channel_id=1, source_target_pairs={{1,0},{2,1},{5,4},{6,5},{9,8},{10,9},{13,12},{14,13},{17,16},{18,1... | collective-permute-start | bytes 3538952 | tf_op jit(solution)/shard_map/ppermute | solution.py:251
  68.9 62.5 %collective-permute-start.8 = (bf16[384,1536]{1,0:T(8,128)(2,1)}, bf16[384,1536]{1,0:T(8,128)(2,1)S(1)}, u32[]{:S(2)}, u32[]{:S(2)}) collective-permute-start(bf16[384,1536]{1,0:T(8,128)(2,1)} %collective-permute-done.6.refs_3_), channel_id=1, source_target_pairs={{2,3},{6,7},{10,11},{14,15},{18,19},{22,23},{26,27},{30,31}} | collective-permute-start | bytes 3538952 | tf_op jit(solution)/shard_map/ppermute | solution.py:251
  119.0 27.7 %collective-permute-start.9 = (bf16[384,1536]{1,0:T(8,128)(2,1)}, bf16[384,1536]{1,0:T(8,128)(2,1)S(1)}, u32[]{:S(2)}, u32[]{:S(2)}) collective-permute-start(bf16[384,1536]{1,0:T(8,128)(2,1)} %collective-permute-done.7.refs_4_), channel_id=1, source_target_pairs={{1,0},{5,4},{9,8},{13,12},{17,16},{21,20},{25,24},{29,28}} | collective-permute-start | bytes 3538952 | tf_op jit(solution)/shard_map/ppermute | solution.py:251
  125.7 20.9 %copy-start.1 = (bf16[1,384,1536]{2,1,0:T(8,128)(2,1)S(1)}, bf16[1,384,1536]{2,1,0:T(8,128)(2,1)}, u32[]{:S(2)}) copy-start(bf16[1,384,1536]{2,1,0:T(8,128)(2,1)} %param.6) | copy-start | bytes 3538948
  125.7 20.9 %copy-start.5 = (f32[1,384,1536]{2,1,0:T(8,128)S(1)}, f32[1,384,1536]{2,1,0:T(8,128)}, u32[]{:S(2)}) copy-start(f32[1,384,1536]{2,1,0:T(8,128)} %param.4) | copy-start | bytes 7077892
  125.7 41.6 %collective-permute-start.10 = (bf16[400,1536]{1,0:T(8,128)(2,1)}, bf16[400,1536]{1,0:T(8,128)(2,1)S(1)}, u32[]{:S(2)}, u32[]{:S(2)}) collective-permute-start(bf16[400,1536]{1,0:T(8,128)(2,1)} %collective-permute-done.1), channel_id=1, source_target_pairs={{2,3},{6,7},{10,11},{14,15},{18,19},{22,23},{26,27},{30,31}} | collective-permute-start | bytes 3686408 | tf_op jit(solution)/shard_map/ppermute | solution.py:251
  126.6 46.4 %collective-permute-start.11 = (bf16[400,1536]{1,0:T(8,128)(2,1)}, bf16[400,1536]{1,0:T(8,128)(2,1)S(1)}, u32[]{:S(2)}, u32[]{:S(2)}) collective-permute-start(bf16[400,1536]{1,0:T(8,128)(2,1)} %collective-permute-done.3), channel_id=1, source_target_pairs={{1,0},{5,4},{9,8},{13,12},{17,16},{21,20},{25,24},{29,28}} | collective-permute-start | bytes 3686408 | tf_op jit(solution)/shard_map/ppermute | solution.py:251
  131.4 41.6 %copy-start.10 = (f32[8,1536]{1,0:T(8,128)S(1)}, f32[8,1536]{1,0:T(8,128)}, u32[]{:S(2)}) copy-start(f32[8,1536]{1,0:T(8,128)} %copy-done.9) | copy-start | bytes 147460
  165.9 1.4 copy-start.11
  167.3 12.6 %copy-start.7 = (bf16[400,1536]{1,0:T(8,128)(2,1)}, bf16[400,1536]{1,0:T(8,128)(2,1)S(1)}, u32[]{:S(2)}) copy-start(bf16[400,1536]{1,0:T(8,128)(2,1)S(1)} %collective-permute-done.10.from_below) | copy-start | bytes 3686404
  173.0 6.9 %copy-start.8 = (bf16[400,1536]{1,0:T(8,128)(2,1)}, bf16[400,1536]{1,0:T(8,128)(2,1)S(1)}, u32[]{:S(2)}) copy-start(bf16[400,1536]{1,0:T(8,128)(2,1)S(1)} %collective-permute-done.11.from_above) | copy-start | bytes 3686404
  173.0 2.8 %copy-start.6 = (bf16[1536,1536]{1,0:T(8,128)(2,1)S(1)}, bf16[1536,1536]{1,0:T(8,128)(2,1)}, u32[]{:S(2)}) copy-start(bf16[1536,1536]{1,0:T(8,128)(2,1)} %get-tuple-element.16.own) | copy-start | bytes 14155780
  179.9 3.4 %copy-start.16 = (f32[1536]{0:T(1024)S(1)}, f32[1536]{0:T(1024)}, u32[]{:S(2)}) copy-start(f32[1536]{0:T(1024)} %pad_maximum_fusion.2) | copy-start | bytes 18436
  179.9 12.8 %copy-start.15 = (f32[1536]{0:T(1024)S(1)}, f32[1536]{0:T(1024)}, u32[]{:S(2)}) copy-start(f32[1536]{0:T(1024)} %fusion.37) | copy-start | bytes 18436
  181.1 45.7 %collective-permute-start.14 = (bf16[1536,1536]{1,0:T(8,128)(2,1)}, bf16[1536,1536]{1,0:T(8,128)(2,1)}, u32[]{:S(2)}, u32[]{:S(2)}) collective-permute-start(bf16[1536,1536]{1,0:T(8,128)(2,1)} %constant_dynamic-update-slice_fusion.1), channel_id=1, source_target_pairs={{0,4},{8,12},{16,20},{24,28},{1,5},{9,13},{17,21},{25,29},{2,6},{1... | collective-permute-start | bytes 14155784 | tf_op jit(solution)/shard_map/ppermute | solution.py:242
  183.5 9.2 %collective-permute-start.12 = (f32[1536]{0:T(1024)S(1)}, f32[1536]{0:T(1024)S(1)}, u32[]{:S(2)}, u32[]{:S(2)}) collective-permute-start(f32[1536]{0:T(1024)S(1)} %add_dynamic-update-slice_fusion), channel_id=1, source_target_pairs={{4,0},{8,4},{12,8},{16,12},{20,16},{24,20},{28,24},{5,1},{9,5},{13... | collective-permute-start | bytes 18440 | tf_op jit(solution)/shard_map/ppermute | solution.py:242
  192.7 19.3 %collective-permute-start.13 = (bf16[1536]{0:T(1024)(128)(2,1)S(1)}, bf16[1536]{0:T(1024)(128)(2,1)S(1)}, u32[]{:S(2)}, u32[]{:S(2)}) collective-permute-start(bf16[1536]{0:T(1024)(128)(2,1)S(1)} %get-tuple-element.25), channel_id=1, source_target_pairs={{0,4},{8,12},{16,20},{24,28},{1,5},{9,13},{17,21},{25,29},{2,6},{1... | collective-permute-start | bytes 9224 | tf_op jit(solution)/shard_map/ppermute | solution.py:242
  200.5 54.7 %collective-permute-start.17 = (bf16[384,1536]{1,0:T(8,128)(2,1)}, bf16[384,1536]{1,0:T(8,128)(2,1)}, u32[]{:S(2)}, u32[]{:S(2)}) collective-permute-start(bf16[384,1536]{1,0:T(8,128)(2,1)} %fusion.7), channel_id=1, source_target_pairs={{8,4},{16,12},{24,20},{9,5},{17,13},{25,21},{10,6},{18,14},{26,22}... | collective-permute-start | bytes 3538952 | tf_op jit(solution)/shard_map/ppermute | solution.py:242
  201.8 53.4 %collective-permute-start.18 = (bf16[384,1536]{1,0:T(8,128)(2,1)}, bf16[384,1536]{1,0:T(8,128)(2,1)}, u32[]{:S(2)}, u32[]{:S(2)}) collective-permute-start(bf16[384,1536]{1,0:T(8,128)(2,1)} %fusion.7), channel_id=1, source_target_pairs={{4,0},{12,8},{20,16},{28,24},{5,1},{13,9},{21,17},{29,25},{6,2},{1... | collective-permute-start | bytes 3538952 | tf_op jit(solution)/shard_map/ppermute | solution.py:242
  210.7 8.5 %collective-permute-start.15 = (f32[1536]{0:T(1024)S(1)}, f32[1536]{0:T(1024)S(1)}, u32[]{:S(2)}, u32[]{:S(2)}) collective-permute-start(f32[1536]{0:T(1024)S(1)} %fusion.20), channel_id=1, source_target_pairs={{8,4},{16,12},{24,20},{9,5},{17,13},{25,21},{10,6},{18,14},{26,22}... | collective-permute-start | bytes 18440 | tf_op jit(solution)/shard_map/ppermute | solution.py:242
  212.0 3.1 %copy-start.14 = (bf16[1536]{0:T(1024)(128)(2,1)}, bf16[1536]{0:T(1024)(128)(2,1)S(1)}, u32[]{:S(2)}) copy-start(bf16[1536]{0:T(1024)(128)(2,1)S(1)} %collective-permute-done.13.refs_0_) | copy-start | bytes 9220
  219.2 7.5 %collective-permute-start.16 = (bf16[1536]{0:T(1024)(128)(2,1)S(1)}, bf16[1536]{0:T(1024)(128)(2,1)S(1)}, u32[]{:S(2)}, u32[]{:S(2)}) collective-permute-start(bf16[1536]{0:T(1024)(128)(2,1)S(1)} %get-tuple-element.28), channel_id=1, source_target_pairs={{4,12},{20,28},{5,13},{21,29},{6,14},{22,30},{7,15},{23,31}} | collective-permute-start | bytes 9224 | tf_op jit(solution)/shard_map/ppermute | solution.py:242
  231.5 1.7 copy-start.12
  231.5 19.0 %collective-permute-start.20 = (bf16[384,1536]{1,0:T(8,128)(2,1)S(1)}, bf16[384,1536]{1,0:T(8,128)(2,1)}, u32[]{:S(2)}, u32[]{:S(2)}) collective-permute-start(bf16[384,1536]{1,0:T(8,128)(2,1)S(1)} %fusion.5.refs_1_), channel_id=1, source_target_pairs={{20,28},{21,29},{22,30},{23,31}} | collective-permute-start | bytes 3538952 | tf_op jit(solution)/shard_map/ppermute | solution.py:242
  233.9 10.8 %copy-start.13 = (bf16[384,1536]{1,0:T(8,128)(2,1)S(1)}, bf16[384,1536]{1,0:T(8,128)(2,1)}, u32[]{:S(2)}) copy-start(bf16[384,1536]{1,0:T(8,128)(2,1)} %copy-done.12) | copy-start | bytes 3538948
  244.7 3.6 %copy-start.17 = (f32[384,1536]{1,0:T(8,128)S(1)}, f32[384,1536]{1,0:T(8,128)}, u32[]{:S(2)}) copy-start(f32[384,1536]{1,0:T(8,128)} %fusion.8) | copy-start | bytes 7077892
  246.8 17.8 %collective-permute-start.19 = (bf16[384,1536]{1,0:T(8,128)(2,1)S(1)}, bf16[384,1536]{1,0:T(8,128)(2,1)S(1)}, u32[]{:S(2)}, u32[]{:S(2)}) collective-permute-start(bf16[384,1536]{1,0:T(8,128)(2,1)S(1)} %convolution_convert_fusion), channel_id=1, source_target_pairs={{20,12},{21,13},{22,14},{23,15}} | collective-permute-start | bytes 3538952 | tf_op jit(solution)/shard_map/ppermute | solution.py:242
